TPU v7x, 32 devices: a whole 2x2x4 slice. The times are simulated.
32 devices in a mesh: dp: 4 (over z), tm: 2 (over core), rows: 4 (over y, x).
Axes of the slice: x: 2, y: 2, z: 4, core: 2. Of those that a mesh axis runs over, the one named last changes fastest.
Arguments:
- latent: bfloat16 [4, 4, 8, 176, 256], P('dp', 'tm', 'rows'), may hold values from -12 to 12, as said below
- gamma: float32 [256], replicated, may hold values from 0.1 to 1.9
- beta: float32 [256], replicated, may hold values from -3 to 3
- weight: bfloat16 [3, 3, 3, 256, 256], replicated, may hold values from -0.078125 to 0.078125
- bias: float32 [256], replicated, may hold values from -3 to 3
- cotangent: bfloat16 [4, 4, 8, 176, 256], P('dp', 'tm', 'rows'), may hold values from -0.039794922 to 0.039794922
Outputs:
- output: bfloat16 [4, 4, 8, 176, 256], P('dp', 'tm', 'rows')
- weight_grad: float32 [2304, 256], P(('tm', 'rows'))
Inputs may be any that keep to these rules, and one draw needn't show every extreme that they name: `latent`: feature values, with each clip's group variance at least 0.5.
All inputs are finite; a program needn't handle non-finite values.
Results may differ from a plain program's by a relative error of at most 0.0029.
Values may be sent and summed in bfloat16 or wider, within the bound.
No kernel may reach another device: no remote copies, remote signals or barrier semaphores. Data moves between devices by JAX's collectives and lax.ppermute only.
A program may use at most 64 MiB of HBM per device.

v0:
```python
import jax
import jax.numpy as jnp
from jax import lax
from jax.sharding import PartitionSpec as P

GROUPS = 32


def with_halo(block, sides, width):
    for axis, dim in sides:
        count = lax.axis_size(axis)
        forward = [(i, i + 1) for i in range(count - 1)]
        backward = [(target, source) for source, target in forward]
        low = lax.ppermute(
            lax.slice_in_dim(block, block.shape[dim] - width, None, axis=dim), axis, forward
        )
        high = lax.ppermute(lax.slice_in_dim(block, 0, width, axis=dim), axis, backward)
        block = jnp.concatenate([low, block, high], axis=dim)
    return block


def shifted(value, axis, steps):
    count = lax.axis_size(axis)
    initial, last = (max(0, -steps), min(count, count - steps))
    return lax.ppermute(value, axis, [(source, source + steps) for source in range(initial, last)])


def build_patches(padded, frames, height, width):
    pieces = []
    for offset_t in range(3):
        for offset_h in range(3):
            for offset_w in range(3):
                pieces.append(
                    padded[
                        :,
                        offset_t : offset_t + frames,
                        offset_h : offset_h + height,
                        offset_w : offset_w + width,
                        :,
                    ]
                )
    return jnp.concatenate(pieces, axis=-1)


def body(latent, gamma, beta, weight, bias, cotangent):
    nclip, frames, height, width, chans = latent.shape
    per_group = chans // GROUPS
    latent_f = latent.astype(jnp.float32)
    grouped = latent_f.reshape(nclip, frames * height * width, GROUPS, per_group)
    part_sum = jnp.sum(grouped, axis=(1, 3))
    part_squares = jnp.sum(grouped * grouped, axis=(1, 3))
    total_sum, total_squares = lax.psum((part_sum, part_squares), ("tm", "rows"))
    count = frames * height * width * per_group * lax.axis_size("tm") * lax.axis_size("rows")
    mean = total_sum / count
    var = total_squares / count - mean * mean
    inverse = lax.rsqrt(var + 1e-06)
    normed = ((grouped - mean[:, None, :, None]) * inverse[:, None, :, None]).reshape(latent.shape)
    act = jax.nn.silu(normed * gamma + beta).astype(jnp.bfloat16)
    rimmed = with_halo(act, (("rows", 2),), 1)
    rimmed = jnp.pad(rimmed, ((0, 0), (0, 0), (0, 0), (1, 1), (0, 0)))
    earlier = shifted(rimmed, "tm", 1)
    leading = jnp.broadcast_to(rimmed[:, :1], earlier.shape)
    earlier = jnp.where(lax.axis_index("tm") == 0, leading, earlier)
    padded = jnp.concatenate([earlier, rimmed], axis=1)
    patches = build_patches(padded, frames, height, width).reshape(
        nclip * frames * height * width, 27 * chans
    )
    kernel = weight.reshape(27 * chans, chans)
    conv = jnp.dot(patches, kernel, preferred_element_type=jnp.float32).reshape(latent.shape)
    output = (latent_f + bias + conv).astype(jnp.bfloat16)
    flat_grad = cotangent.reshape(-1, chans)
    earliest = patches[:, : 9 * chans]
    shard = lax.psum_scatter(
        lax.dot_general(
            earliest, flat_grad, (((0,), (0,)), ((), ())), preferred_element_type=jnp.float32
        ),
        ("tm", "rows"),
        scatter_dimension=0,
        tiled=True,
    )
    weight_grad = lax.psum(shard, "dp")
    return (output, weight_grad)


def solution(mesh):
    placed = (
        P("dp", "tm", "rows", None, None),
        P(),
        P(),
        P(),
        P(),
        P("dp", "tm", "rows", None, None),
    )
    return jax.shard_map(
        body,
        mesh=mesh,
        in_specs=placed,
        out_specs=(P("dp", "tm", "rows", None, None), P(("tm", "rows"), None)),
        check_vma=False,
    )
```

profile of v0, /device:TPU:0, one launch (start us, length us, event | category | flops | bytes accessed | tf_op | source)
XLA Modules:
  0.0 151.3 jit_solution(16156035599880228167)
XLA Ops:
  7.2 1.8 %convert_reduce_fusion = (f32[256]{0:T(256)}, f32[256]{0:T(256)}) fusion(bf16[1,2,2,176,256]{4,3,2,1,0:T(8,128)(2,1)} %param.6), kind=kLoop, calls=%fused_computation.27 | loop fusion | flops 720384 | bytes 362496 | tf_op jit(solution)/shard_map/reduce_sum | solution.py:50
  9.1 0.8 reduce_sum.26
  9.8 1.4 reduce_sum.41
  11.8 0.8 reduce_sum.42
  12.7 15.9 %all-reduce.1 = (f32[1,32]{1,0:T(1,128)S(1)}, f32[1,32]{1,0:T(1,128)S(1)}) all-reduce(f32[1,32]{1,0:T(1,128)S(1)} %bitcast.35, f32[1,32]{1,0:T(1,128)} %bitcast.34), channel_id=1, replica_groups=mesh['dp'=4,'tm'=2,'rows'=4] {'tm','rows'}, use_global_device_ids=true, to_apply=%region_5.6 | all-reduce | flops 64 | bytes 512 | tf_op jit(solution)/shard_map/psum | solution.py:52
  29.2 0.7 sub.23
  29.8 0.7 mul.46
  31.2 1.3 fusion.27
  32.5 3.3 %collective-permute-start = (bf16[1,2,1,176,256]{4,3,2,1,0:T(8,128)(2,1)S(1)}, bf16[1,2,1,176,256]{4,3,2,1,0:T(8,128)(2,1)S(1)}, u32[]{:S(2)}, u32[]{:S(2)}) collective-permute-start(bf16[1,2,1,176,256]{4,3,2,1,0:T(8,128)(2,1)S(1)} %get-tuple-element.6), channel_id=1, source_target_pairs={{0,1},{1,2},{2,3},{4,5},{5,6},{6,7},{8,9},{9,10},{10,11},{12,13},{... | collective-permute-start | bytes 540680 | tf_op jit(solution)/shard_map/ppermute | solution.py:14
  35.8 1.3 collective-permute-start.1
  37.1 1.7 %collective-permute-done = bf16[1,2,1,176,256]{4,3,2,1,0:T(8,128)(2,1)S(1)} collective-permute-done((bf16[1,2,1,176,256]{4,3,2,1,0:T(8,128)(2,1)S(1)}, bf16[1,2,1,176,256]{4,3,2,1,0:T(8,128)(2,1)S(1)}, u32[]{:S(2)}, u32[]{:S(2)}) %collective-permute-start) | collective-permute-done | bytes 180256 | tf_op jit(solution)/shard_map/ppermute | solution.py:14
  38.8 5.9 %collective-permute-done.1 = bf16[1,2,1,176,256]{4,3,2,1,0:T(8,128)(2,1)S(1)} collective-permute-done((bf16[1,2,1,176,256]{4,3,2,1,0:T(8,128)(2,1)S(1)}, bf16[1,2,1,176,256]{4,3,2,1,0:T(8,128)(2,1)S(1)}, u32[]{:S(2)}, u32[]{:S(2)}) %collective-permute-start.1) | collective-permute-done | bytes 180256 | tf_op jit(solution)/shard_map/ppermute | solution.py:17
  44.9 0.9 copy-done.1
  45.8 1.1 copy.8
  46.9 2.2 %collective-permute-start.2 = (bf16[1,2,4,178,256]{4,2,3,1,0:T(4,128)(2,1)}, bf16[1,2,4,178,256]{4,2,3,1,0:T(4,128)(2,1)}, u32[]{:S(2)}, u32[]{:S(2)}) collective-permute-start(bf16[1,2,4,178,256]{4,2,3,1,0:T(4,128)(2,1)} %copy.8), channel_id=1, source_target_pairs={{0,4},{1,5},{2,6},{3,7},{8,12},{9,13},{10,14},{11,15},{16,20},{17,... | collective-permute-start | bytes 2187272 | tf_op jit(solution)/shard_map/ppermute | solution.py:25
  49.1 1.1 slice_bitcast_fusion
  50.4 1.2 copy_select_fusion
  52.4 1.0 fusion.32
  54.8 3.7 %copy-done.10 = bf16[1,2,2,176,6912]{4,3,2,1,0:T(8,128)(2,1)} copy-done((bf16[1,2,2,176,6912]{4,3,2,1,0:T(8,128)(2,1)}, bf16[1,2,2,176,6912]{4,3,2,1,0:T(8,128)(2,1)S(1)}, u32[]{:S(2)}) %copy-start.10) | copy-done | bytes 9732120
  58.6 2.6 %fusion.2 = f32[2304,256]{1,0:T(8,128)} fusion(bf16[704,256]{1,0:T(8,128)(2,1)S(1)} %bitcast.36, bf16[704,6912]{1,0:T(8,128)(2,1)S(1)} %bitcast.33), kind=kOutput, calls=%fused_computation.2 | convolution fusion | flops 830472192 | bytes 5963776 | tf_op jit(solution)/shard_map/dot_general | solution.py:74
  61.2 43.2 %reduce-scatter.2.cloned.1.call-done = f32[288,256]{1,0:T(8,128)} async-done(((f32[2304,256]{1,0:T(8,128)}), f32[288,256]{1,0:T(8,128)}) %reduce-scatter.2.cloned.1.call-update) | async-done | bytes 294928 | tf_op jit(solution)/shard_map/reduce_scatter | solution.py:73
  104.5 7.2 %fusion.11 = bf16[1,2,2,176,256]{4,3,2,1,0:T(8,128)(2,1)} fusion(bf16[6912,256,1,1]{1,0,3,2:T(8,128)(2,1)S(1)} %bitcast.32, bf16[1,2,2,176,6912]{4,3,2,1,0:T(8,128)(2,1)} %copy-done.10, bf16[1,2,2,176,256]{4,3,2,1,0:T(8,128)(2,1)} %param.6, f32[256]{0:T(256)S(1)} %copy-done.16), kind=kOutput, calls=%fused_computation.29 | convolution fusion | flops 2492137472 | bytes 13992960 | tf_op jit(solution)/shard_map/dot_general | solution.py:69
  111.7 31.1 %all-reduce.4.cloned.1.call-done = f32[288,256]{1,0:T(8,128)} async-done(((f32[288,256]{1,0:T(8,128)}), f32[288,256]{1,0:T(8,128)}) %all-reduce.4.cloned.1.call-update) | async-done | bytes 294928 | tf_op jit(solution)/shard_map/psum | solution.py:81
  142.8 1.7 %copy.39 = f32[288,256]{1,0:T(8,128)} copy(f32[288,256]{1,0:T(8,128)} %all-reduce.4.cloned.1.call-done) | data formatting | bytes 589824
  (69 shorter events, 4.3 us)
Async XLA Ops:
  7.2 97.3 %copy-start = (bf16[3,3,3,256,256]{4,3,2,1,0:T(8,128)(2,1)S(1)}, bf16[3,3,3,256,256]{4,3,2,1,0:T(8,128)(2,1)}, u32[]{:S(2)}) copy-start(bf16[3,3,3,256,256]{4,3,2,1,0:T(8,128)(2,1)} %param.9) | copy-start | bytes 10616836
  7.2 97.3 %reduce-scatter.2.cloned.1.call-start = ((), (), s32[]{:S(2)}) async-start(), calls=%async_computation.1 | async-start | bytes 2654208 | tf_op jit(solution)/shard_map/reduce_scatter | solution.py:73
  32.5 14.4 %copy-start.3 = (bf16[1,2,2,176,256]{4,3,2,1,0:T(8,128)(2,1)}, bf16[1,2,2,176,256]{4,3,2,1,0:T(8,128)(2,1)S(1)}, u32[]{:S(2)}) copy-start(bf16[1,2,2,176,256]{4,3,2,1,0:T(8,128)(2,1)S(1)} %fusion.27) | copy-start | bytes 1081348
  32.5 6.3 %collective-permute-start = (bf16[1,2,1,176,256]{4,3,2,1,0:T(8,128)(2,1)S(1)}, bf16[1,2,1,176,256]{4,3,2,1,0:T(8,128)(2,1)S(1)}, u32[]{:S(2)}, u32[]{:S(2)}) collective-permute-start(bf16[1,2,1,176,256]{4,3,2,1,0:T(8,128)(2,1)S(1)} %get-tuple-element.6), channel_id=1, source_target_pairs={{0,1},{1,2},{2,3},{4,5},{5,6},{6,7},{8,9},{9,10},{10,11},{12,13},{... | collective-permute-start | bytes 540680 | tf_op jit(solution)/shard_map/ppermute | solution.py:14
  35.8 8.9 %collective-permute-start.1 = (bf16[1,2,1,176,256]{4,3,2,1,0:T(8,128)(2,1)S(1)}, bf16[1,2,1,176,256]{4,3,2,1,0:T(8,128)(2,1)S(1)}, u32[]{:S(2)}, u32[]{:S(2)}) collective-permute-start(bf16[1,2,1,176,256]{4,3,2,1,0:T(8,128)(2,1)S(1)} %get-tuple-element.7), channel_id=1, source_target_pairs={{1,0},{2,1},{3,2},{5,4},{6,5},{7,6},{9,8},{10,9},{11,10},{13,12},{... | collective-permute-start | bytes 540680 | tf_op jit(solution)/shard_map/ppermute | solution.py:17
  38.8 10.3 %copy-start.8 = (bf16[1,2,1,176,256]{4,3,2,1,0:T(8,128)(2,1)}, bf16[1,2,1,176,256]{4,3,2,1,0:T(8,128)(2,1)S(1)}, u32[]{:S(2)}) copy-start(bf16[1,2,1,176,256]{4,3,2,1,0:T(8,128)(2,1)S(1)} %collective-permute-done) | copy-start | bytes 540676
  44.7 4.4 %copy-start.6 = (bf16[1,2,1,176,256]{4,3,2,1,0:T(8,128)(2,1)}, bf16[1,2,1,176,256]{4,3,2,1,0:T(8,128)(2,1)S(1)}, u32[]{:S(2)}) copy-start(bf16[1,2,1,176,256]{4,3,2,1,0:T(8,128)(2,1)S(1)} %collective-permute-done.1) | copy-start | bytes 540676
  44.9 0.9 copy-start.1
  46.9 3.4 %collective-permute-start.2 = (bf16[1,2,4,178,256]{4,2,3,1,0:T(4,128)(2,1)}, bf16[1,2,4,178,256]{4,2,3,1,0:T(4,128)(2,1)}, u32[]{:S(2)}, u32[]{:S(2)}) collective-permute-start(bf16[1,2,4,178,256]{4,2,3,1,0:T(4,128)(2,1)} %copy.8), channel_id=1, source_target_pairs={{0,4},{1,5},{2,6},{3,7},{8,12},{9,13},{10,14},{11,15},{16,20},{17,... | collective-permute-start | bytes 2187272 | tf_op jit(solution)/shard_map/ppermute | solution.py:25
  49.1 4.2 %copy-start.2 = (bf16[1,2,4,178,256]{4,3,2,1,0:T(8,128)(2,1)S(1)}, bf16[1,2,4,178,256]{4,3,2,1,0:T(8,128)(2,1)}, u32[]{:S(2)}) copy-start(bf16[1,2,4,178,256]{4,3,2,1,0:T(8,128)(2,1)} %copy-done.1) | copy-start | bytes 2187268
  52.0 2.0 %copy-start.4 = (bf16[1,2,2,176,256]{4,3,2,1,0:T(8,128)(2,1)S(1)}, bf16[1,2,2,176,256]{4,3,2,1,0:T(8,128)(2,1)}, u32[]{:S(2)}) copy-start(bf16[1,2,2,176,256]{4,3,2,1,0:T(8,128)(2,1)} %copy-done.3) | copy-start | bytes 1081348
  52.1 2.0 %copy-start.9 = (bf16[1,2,1,176,256]{4,3,2,1,0:T(8,128)(2,1)S(1)}, bf16[1,2,1,176,256]{4,3,2,1,0:T(8,128)(2,1)}, u32[]{:S(2)}) copy-start(bf16[1,2,1,176,256]{4,3,2,1,0:T(8,128)(2,1)} %copy-done.8) | copy-start | bytes 540676
  52.3 2.0 %copy-start.5 = (bf16[1,2,2,176,256]{4,3,2,1,0:T(8,128)(2,1)S(1)}, bf16[1,2,2,176,256]{4,3,2,1,0:T(8,128)(2,1)}, u32[]{:S(2)}) copy-start(bf16[1,2,2,176,256]{4,3,2,1,0:T(8,128)(2,1)} %param.6) | copy-start | bytes 1081348
  52.3 2.0 %copy-start.11 = (f32[256]{0:T(256)S(1)}, f32[256]{0:T(256)}, u32[]{:S(2)}) copy-start(f32[256]{0:T(256)} %sub.23) | copy-start | bytes 3076
  52.3 2.0 %copy-start.12 = (f32[256]{0:T(256)S(1)}, f32[256]{0:T(256)}, u32[]{:S(2)}) copy-start(f32[256]{0:T(256)} %mul.47) | copy-start | bytes 3076
  52.3 2.0 %copy-start.13 = (f32[256]{0:T(256)S(1)}, f32[256]{0:T(256)}, u32[]{:S(2)}) copy-start(f32[256]{0:T(256)} %param.8) | copy-start | bytes 3076
  52.3 2.0 %copy-start.14 = (f32[256]{0:T(256)S(1)}, f32[256]{0:T(256)}, u32[]{:S(2)}) copy-start(f32[256]{0:T(256)} %param.7) | copy-start | bytes 3076
  53.4 1.3 copy-start.7
  53.5 5.1 %copy-start.15 = (bf16[1,2,2,176,256]{4,3,2,1,0:T(8,128)(2,1)S(1)}, bf16[1,2,2,176,256]{4,3,2,1,0:T(8,128)(2,1)}, u32[]{:S(2)}) copy-start(bf16[1,2,2,176,256]{4,3,2,1,0:T(8,128)(2,1)} %param.11) | copy-start | bytes 1081348
  54.1 50.4 %copy-start.16 = (f32[256]{0:T(256)S(1)}, f32[256]{0:T(256)}, u32[]{:S(2)}) copy-start(f32[256]{0:T(256)} %param.10) | copy-start | bytes 3076
  54.8 3.8 %copy-start.10 = (bf16[1,2,2,176,6912]{4,3,2,1,0:T(8,128)(2,1)}, bf16[1,2,2,176,6912]{4,3,2,1,0:T(8,128)(2,1)S(1)}, u32[]{:S(2)}) copy-start(bf16[1,2,2,176,6912]{4,3,2,1,0:T(8,128)(2,1)S(1)} %slice_dynamic-update-slice_fusion) | copy-start | bytes 29196292
  61.2 81.6 %all-reduce.4.cloned.1.call-start = ((), (), s32[]{:S(2)}) async-start(), calls=%async_computation.2 | async-start | bytes 589824 | tf_op jit(solution)/shard_map/psum | solution.py:81
Sparse Core Ops, SparseCore 0:
  61.3 43.0 reduce-scatter.1
  106.9 35.8 all-reduce.3
where the time goes:
time: 152 us; the launch traced here: 151 us
  waiting for transfers between devices  82.1 us (54%)
  blocking collectives  15.9 us (10%)
  between operations  14.5 us (10%)
  local copies, waits for them, and re-layouts  13.9 us (9%)
  matrix products  9.78 us (6%)
  other arithmetic  8.36 us (6%)
  starting transfers between devices  6.82 us (4%)
    reduce_scatter x1, waiting for transfers between devices, body(): lax.psum_scatter(lax.dot_general(earliest, flat_grad, (((0,), (0,)), ((),...  43.2 us
    psum x1, waiting for transfers between devices, body(): weight_grad = lax.psum(shard, 'dp')  31.1 us
    psum x1, blocking collectives, body(): lax.psum((part_sum, part_squares), ('tm', 'rows'))  15.9 us
    unnamed x49, local copies, waits for them, and re-layouts  7.24 us
    dot_general x1, matrix products, body(): jnp.dot(patches, kernel, preferred_element_type=jnp.float32)  7.21 us
    ppermute x1, waiting for transfers between devices, with_halo(): lax.ppermute(lax.slice_in_dim(block, 0, width, axis=dim), axis, backward)  5.92 us
    ppermute x1, starting transfers between devices, with_halo(): lax.ppermute(lax.slice_in_dim(block, block.shape[dim] - width, None, axis...  3.27 us
  transfers between devices with their start and end apart: 5, of which 5 were waited for; matrix products, arithmetic and copies ran while one was open for 5% of the time, Pallas kernels for 0%

commit v1 on v0

v1 whole, which is shorter than its diff:
```python
import functools

import jax
import jax.numpy as jnp
from jax import lax
from jax.experimental import pallas as pl
from jax.experimental.pallas import tpu as pltpu
from jax.sharding import PartitionSpec as P

GROUPS = 32
BF16 = jnp.bfloat16
F32 = jnp.float32
VMEM_LIMIT = 40 * 1024 * 1024


def call(kernel, outs, ins, scratch=(), flops=0, nbytes=0, trans=0, name=None):
    specs = [
        pl.BlockSpec(memory_space=pltpu.SMEM)
        if a.dtype == jnp.int32
        else pl.BlockSpec(memory_space=pltpu.VMEM)
        for a in ins
    ]
    return pl.pallas_call(
        kernel,
        out_shape=outs,
        in_specs=specs,
        out_specs=jax.tree.map(lambda _: pl.BlockSpec(memory_space=pltpu.VMEM), outs),
        scratch_shapes=list(scratch),
        compiler_params=pltpu.CompilerParams(vmem_limit_bytes=VMEM_LIMIT),
        cost_estimate=pl.CostEstimate(flops=flops, bytes_accessed=nbytes, transcendentals=trans),
        name=name,
    )(*ins)


def stats_kernel(own_ref, other_ref, out_ref):
    rows, chans = own_ref.shape
    step = 88
    total = jnp.zeros((8, chans), F32)
    squares = jnp.zeros((8, chans), F32)
    for ref in (own_ref, other_ref):
        for at in range(0, rows, step):
            x = ref[at : at + step, :].astype(F32).reshape(step // 8, 8, chans)
            total = total + jnp.sum(x, axis=0)
            squares = squares + jnp.sum(x * x, axis=0)
    out_ref[0:8, :] = total
    out_ref[8:16, :] = squares


def shift_rows(x, by):
    zero = jnp.zeros((1, x.shape[1]), x.dtype)
    if by == 1:
        return jnp.concatenate([x[1:], zero], axis=0)
    if by == -1:
        return jnp.concatenate([zero, x[:-1]], axis=0)
    return x


def cot_kernel(where_ref, own_ref, other_ref, out_ref):
    _, height, width, chans = own_ref.shape
    is_late = where_ref[0] == 1
    for h in range(height):
        a0 = own_ref[0, h].astype(F32)
        a1 = own_ref[1, h].astype(F32)
        b0 = other_ref[0, h].astype(F32)
        b1 = other_ref[1, h].astype(F32)
        first = a0 + b0 + jnp.where(is_late, b1, a1)
        last = jnp.where(is_late, a1, b1)
        high = first.astype(BF16).astype(F32)
        low = first - high
        for term, value in enumerate((high, low, last)):
            for kw in range(3):
                out_ref[kw, term, h] = shift_rows(value, 1 - kw).astype(BF16)


def group_sum(x, per_group):
    chans = x.shape[1]
    lane = lax.broadcasted_iota(jnp.int32, x.shape, 1)
    step = 1
    while step < per_group:
        up = pltpu.roll(x, step, 1)
        down = pltpu.roll(x, chans - step, 1)
        x = x + jnp.where((lane & step) != 0, up, down)
        step *= 2
    return x


def activate(x, scale, shift):
    v = x.astype(F32) * scale + shift
    return v * (0.5 + 0.5 * jnp.tanh(0.5 * v))


def grad_kernel(count, n_stats, n_pieces, rows_out, *refs):
    where_ref = refs[0]
    stats = refs[1 : 1 + n_stats]
    (gamma_ref, beta_ref, own_ref, other_ref, own_low, own_high, other_low, other_high, cots_ref) = refs[
        1 + n_stats : 10 + n_stats
    ]
    act_ref, norm_ref = refs[10 + n_stats : 12 + n_stats]
    pieces = refs[12 + n_stats : 12 + n_stats + n_pieces]
    wg_ref = refs[12 + n_stats + n_pieces]
    late = where_ref[0]
    is_late = late == 1
    frames, height, width, chans = own_ref.shape
    sums = stats[0][...]
    for ref in stats[1:]:
        sums = sums + ref[...]
    total = jnp.sum(sums[0:8], axis=0, keepdims=True)
    squares = jnp.sum(sums[8:16], axis=0, keepdims=True)
    both = group_sum(jnp.concatenate([total, squares] + [total] * 6, axis=0), chans // GROUPS) / count
    mean = both[0:1]
    var = both[1:2] - mean * mean
    scale = lax.rsqrt(var + 1e-06) * gamma_ref[...]
    shift = beta_ref[...] - mean * scale
    norm_ref[0:1, :] = scale
    norm_ref[1:2, :] = shift
    norm_ref[2:8, :] = jnp.zeros((6, chans), F32)
    keep_low = (where_ref[1] != 0).astype(F32)
    keep_high = (where_ref[2] != 0).astype(F32)
    for f in range(frames):
        low = jnp.where(is_late, other_low[f], own_low[f])
        act_ref[f, 0] = (activate(low, scale, shift) * keep_low).astype(BF16)
        for h in range(height):
            x = jnp.where(is_late, other_ref[f, h], own_ref[f, h])
            act_ref[f, h + 1] = activate(x, scale, shift).astype(BF16)
        high = jnp.where(is_late, other_high[f], own_high[f])
        act_ref[f, height + 1] = (activate(high, scale, shift) * keep_high).astype(BF16)

    contract = (((0,), (0,)), ((), ()))
    terms = 3 * height * width

    def stack(kh):
        a0 = act_ref[0, pl.ds(kh, height)].reshape(height * width, chans)
        a1 = act_ref[1, pl.ds(kh, height)].reshape(height * width, chans)
        return jnp.concatenate([a0, a0, a1], axis=0)

    def cots(kw):
        return cots_ref[kw].reshape(terms, chans)

    half = chans // 2
    outer = stack(2 * late)
    base = pl.multiple_of(late * (chans + half), half)
    for kw in range(3):
        wg_ref[pl.ds(base + kw * chans, chans), :] = lax.dot_general(
            outer, cots(kw), contract, preferred_element_type=F32
        )
    middle = stack(1)
    base = pl.multiple_of(3 * chans - late * (5 * half), half)
    wg_ref[pl.ds(base, chans), :] = lax.dot_general(middle, cots(2 * late), contract, preferred_element_type=F32)
    lanes = jnp.where(is_late, middle[:, half:], middle[:, :half])
    base = pl.multiple_of((1 - late) * (4 * chans), half)
    wg_ref[pl.ds(base, half), :] = lax.dot_general(lanes, cots(1), contract, preferred_element_type=F32)
    for k, ref in enumerate(pieces):
        start = pl.multiple_of(where_ref[3 + k], 16)
        ref[...] = wg_ref[pl.ds(start, rows_out), :].astype(ref.dtype)


def conv_kernel(
    where_ref, norm_ref, act_ref, own_ref, own_low, own_high, weight_ref, bias_ref, out_ref, planes, acc
):
    late = where_ref[0]
    frames, height, width, chans = own_ref.shape
    scale = norm_ref[0:1, :]
    shift = norm_ref[1:2, :]
    keep_low = (where_ref[1] != 0).astype(F32)
    keep_high = (where_ref[2] != 0).astype(F32)
    planes[0] = act_ref[0]
    planes[1] = act_ref[late]
    for f in range(frames):
        planes[frames + f, 0] = (activate(own_low[f], scale, shift) * keep_low).astype(BF16)
        for h in range(height):
            planes[frames + f, h + 1] = activate(own_ref[f, h], scale, shift).astype(BF16)
        planes[frames + f, height + 1] = (activate(own_high[f], scale, shift) * keep_high).astype(BF16)
    for f in range(frames):
        for kw in range(3):
            total = None
            for kt in range(3):
                for kh in range(3):
                    lhs = planes[f + kt, kh : kh + height].reshape(height * width, chans)
                    part = jnp.dot(lhs, weight_ref[kt, kh, kw], preferred_element_type=F32)
                    total = part if total is None else total + part
            acc[kw] = total.reshape(height, width, chans)
        for h in range(height):
            value = own_ref[f, h].astype(F32) + bias_ref[...]
            value = value + acc[1, h] + shift_rows(acc[0, h], -1) + shift_rows(acc[2, h], 1)
            out_ref[f, h] = value.astype(BF16)


def body(dp, rows, latent, gamma, beta, weight, bias, cotangent):
    nclip, frames, height, width, chans = latent.shape
    lat = latent[0]
    cot = cotangent[0]
    swap = [(0, 1), (1, 0)]
    clip = lax.axis_index("dp")
    late = lax.axis_index("tm")
    band = lax.axis_index("rows")
    count = frames * height * width * (chans // GROUPS) * 2 * rows
    size = frames * height * width * chans

    other = lax.ppermute(lat, "tm", swap)
    other_cot = lax.ppermute(cot, "tm", swap)
    own_low = lax.ppermute(lat[:, height - 1], "rows", [(i, i + 1) for i in range(rows - 1)])
    own_high = lax.ppermute(lat[:, 0], "rows", [(i + 1, i) for i in range(rows - 1)])
    other_low = lax.ppermute(own_low, "tm", [(0, 1)])
    other_high = lax.ppermute(own_high, "tm", [(0, 1)])

    sums = call(
        stats_kernel,
        jax.ShapeDtypeStruct((16, chans), F32),
        (lat.reshape(-1, chans), other.reshape(-1, chans)),
        flops=6 * size,
        nbytes=4 * size,
        name="stats",
    )
    small = rows == 4 and dp == 4
    if small:
        stats = [sums] + [lax.ppermute(sums, "rows", [(i, i ^ k) for i in range(4)]) for k in (1, 2, 3)]
    else:
        stats = [lax.psum(sums, "rows")]

    half = 9 * chans // 2
    if small:
        piece = half // 8
        order = [(dz, dr) for dz in (0, 1) for dr in range(4)]
        starts = [(band ^ dr) * (2 * piece) + ((clip ^ dz) & 1) * piece for dz, dr in order]
        kinds = [F32] + [BF16] * 7
    else:
        piece = half
        starts = [jnp.int32(0)]
        kinds = [F32]
    where = jnp.stack([late, (band != 0).astype(jnp.int32), (band != rows - 1).astype(jnp.int32)] + starts).astype(
        jnp.int32
    )
    cots = call(
        cot_kernel,
        jax.ShapeDtypeStruct((3, 3, height, width, chans), BF16),
        (where, cot, other_cot),
        flops=10 * size,
        nbytes=14 * size,
        name="cots",
    )
    act, norm, *parts = call(
        functools.partial(grad_kernel, count, len(stats), len(kinds), piece),
        [
            jax.ShapeDtypeStruct((frames, height + 2, width, chans), BF16),
            jax.ShapeDtypeStruct((8, chans), F32),
        ]
        + [jax.ShapeDtypeStruct((piece, chans), k) for k in kinds],
        (where, *stats, gamma.reshape(1, -1), beta.reshape(1, -1), lat, other, own_low, own_high, other_low, other_high, cots),
        scratch=[pltpu.VMEM((half, chans), F32)],
        flops=2 * half * 3 * height * width * chans,
        nbytes=20 * size,
        trans=2 * size,
        name="grad",
    )
    output = call(
        conv_kernel,
        jax.ShapeDtypeStruct((frames, height, width, chans), BF16),
        (where, norm, act, lat, own_low, own_high, weight, bias.reshape(1, -1)),
        scratch=[
            pltpu.VMEM((4, height + 2, width, chans), BF16),
            pltpu.VMEM((3, height, width, chans), F32),
        ],
        flops=2 * 27 * size * chans,
        nbytes=4 * size + 2 * weight.size,
        trans=2 * size,
        name="conv",
    )
    if small:
        got = [
            lax.ppermute(
                p,
                ("dp", "rows"),
                [(z * 4 + r, (z ^ dz) * 4 + (r ^ dr)) for z in range(4) for r in range(4)],
            )
            for p, (dz, dr) in zip(parts[1:], order[1:])
        ]
        total = parts[0]
        for g in got:
            total = total + g.astype(F32)
        total = total.astype(BF16)
        by = [total] + [lax.ppermute(total, "dp", [(z, z ^ k) for z in range(4)]) for k in (1, 2, 3)]
        by = [b.astype(F32) for b in by]
        mine = by[0] + by[2]
        theirs = by[1] + by[3]
        even = clip % 2 == 0
        grad = jnp.concatenate([jnp.where(even, mine, theirs), jnp.where(even, theirs, mine)], axis=0)
    else:
        grad = lax.psum(lax.psum_scatter(parts[0], "rows", scatter_dimension=0, tiled=True), "dp")
    return output[None], grad


def solution(mesh):
    placed = (
        P("dp", "tm", "rows", None, None),
        P(),
        P(),
        P(),
        P(),
        P("dp", "tm", "rows", None, None),
    )
    return jax.shard_map(
        functools.partial(body, mesh.shape["dp"], mesh.shape["rows"]),
        mesh=mesh,
        in_specs=placed,
        out_specs=(P("dp", "tm", "rows", None, None), P(("tm", "rows"), None)),
        check_vma=False,
    )
```

time: 152 us -> 53.6 us (0.35)
  waiting for transfers between devices: 82.1 us -> 9.22 us
  starting transfers between devices: 6.82 us -> 29.9 us
  blocking collectives: 15.9 us -> 0 us
  between operations: 14.5 us -> 0.8 us
  matrix products: 9.78 us -> 0 us
  local copies, waits for them, and re-layouts: 13.9 us -> 5.17 us
  other arithmetic: 8.36 us -> 0.87 us
  Pallas kernels: 0 us -> 7.35 us
    reduce_scatter x1 -> x0, waiting for transfers between devices: 43.2 us -> none  [body(): lax.psum_scatter(lax.dot_general(earliest, flat_grad, (((0,), (0,)), ((),...]
    psum x1 -> x0, waiting for transfers between devices: 31.1 us -> none  [body(): weight_grad = lax.psum(shard, 'dp')]
    ppermute x3 -> x19, starting transfers between devices: 6.74 us -> 29.9 us  [the longest x7 9.58 us: body(): lax.ppermute(p, ('dp', 'rows'), [(z * 4 + r, (z ^ dz) * 4 + (r ^ dr)) for...]
    psum x1 -> x0, blocking collectives: 15.9 us -> none  [body(): lax.psum((part_sum, part_squares), ('tm', 'rows'))]
    dot_general x2 -> x0, matrix products: 9.78 us -> none  [the longest x1 7.21 us: body(): jnp.dot(patches, kernel, preferred_element_type=jnp.float32)]
    pallas_call x0 -> x4, Pallas kernels: none -> 7.35 us  [call(): pl.pallas_call(kernel, out_shape=outs, in_specs=specs, out_specs=jax.tree...]
    reduce_sum x3 -> x0, other arithmetic: 3.29 us -> none  [the longest x2 2.46 us: body(): part_sum = jnp.sum(grouped, axis=(1, 3))]
    unnamed x49 -> x15, local copies, waits for them, and re-layouts: 7.24 us -> 5.04 us
  transfers between devices with their start and end apart: 5 -> 19, of which waited for: 5 -> 5; matrix products, arithmetic and copies ran while one was open for 5% -> 0% of each run, Pallas kernels for 0% -> 9%
where the time goes in v1:
time: 53.6 us; the launch traced here: 53.3 us
  starting transfers between devices  29.9 us (56%)
  waiting for transfers between devices  9.22 us (17%)
  Pallas kernels  7.35 us (14%)
  local copies, waits for them, and re-layouts  5.17 us (10%)
  other arithmetic  0.87 us (2%)
  between operations  0.8 us (1%)
    ppermute x7, starting transfers between devices, body(): lax.ppermute(p, ('dp', 'rows'), [(z * 4 + r, (z ^ dz) * 4 + (r ^ dr)) for...  9.58 us
    pallas_call x4, Pallas kernels, call(): pl.pallas_call(kernel, out_shape=outs, in_specs=specs, out_specs=jax.tree...  7.35 us
    ppermute x3, starting transfers between devices, body(): lax.ppermute(sums, 'rows', [(i, i ^ k) for i in range(4)])  5.77 us
    ppermute x1, starting transfers between devices, body(): lax.ppermute(lat[:, height - 1], 'rows', [(i, i + 1) for i in range(rows...  5.46 us
    ppermute x7, waiting for transfers between devices, body(): lax.ppermute(p, ('dp', 'rows'), [(z * 4 + r, (z ^ dz) * 4 + (r ^ dr)) for...  5.32 us
    unnamed x15, local copies, waits for them, and re-layouts  5.04 us
    ppermute x3, starting transfers between devices, body(): lax.ppermute(total, 'dp', [(z, z ^ k) for z in range(4)])  4.45 us
    ppermute x1, waiting for transfers between devices, body(): lax.ppermute(lat[:, 0], 'rows', [(i + 1, i) for i in range(rows - 1)])  2.84 us
  transfers between devices with their start and end apart: 19, of which 5 were waited for; matrix products, arithmetic and copies ran while one was open for 0% of the time, Pallas kernels for 9%

profile of v1, /device:TPU:0, one launch (start us, length us, event | category | flops | bytes accessed | tf_op | source)
XLA Modules:
  0.0 53.3 jit_solution(13116475845016512696)
XLA Ops:
  0.7 1.1 %copy.19 = bf16[1,2,2,176,256]{4,3,1,2,0:T(8,128)(2,1)S(1)} copy(bf16[1,2,2,176,256]{4,3,2,1,0:T(8,128)(2,1)} %param.6) | data formatting | bytes 720896 | tf_op args[0]
  2.3 1.3 %collective-permute-start.5 = (bf16[2,176,256]{2,1,0:T(8,128)(2,1)S(1)}, bf16[2,176,256]{2,1,0:T(8,128)(2,1)S(1)}, u32[]{:S(2)}, u32[]{:S(2)}) collective-permute-start(bf16[2,176,256]{2,1,0:T(8,128)(2,1)S(1)} %get-tuple-element.22), channel_id=1, source_target_pairs={{1,0},{2,1},{3,2},{5,4},{6,5},{7,6},{9,8},{10,9},{11,10},{13,12},{... | collective-permute-start | bytes 540680 | tf_op jit(solution)/shard_map/ppermute | solution.py:202
  3.6 5.5 %collective-permute-start.4 = (bf16[2,176,256]{2,1,0:T(8,128)(2,1)S(1)}, bf16[2,176,256]{2,1,0:T(8,128)(2,1)S(1)}, u32[]{:S(2)}, u32[]{:S(2)}) collective-permute-start(bf16[2,176,256]{2,1,0:T(8,128)(2,1)S(1)} %get-tuple-element.23), channel_id=1, source_target_pairs={{0,1},{1,2},{2,3},{4,5},{5,6},{6,7},{8,9},{9,10},{10,11},{12,13},{... | collective-permute-start | bytes 540680 | tf_op jit(solution)/shard_map/ppermute | solution.py:201
  9.1 2.8 %collective-permute-done.5.refs_10_.own_high = bf16[2,176,256]{2,1,0:T(8,128)(2,1)S(1)} collective-permute-done((bf16[2,176,256]{2,1,0:T(8,128)(2,1)S(1)}, bf16[2,176,256]{2,1,0:T(8,128)(2,1)S(1)}, u32[]{:S(2)}, u32[]{:S(2)}) %collective-permute-start.5) | collective-permute-done | bytes 180256 | tf_op jit(solution)/shard_map/ppermute | solution.py:202
  12.0 1.5 %collective-permute-start.7 = (bf16[2,176,256]{2,1,0:T(8,128)(2,1)S(1)}, bf16[2,176,256]{2,1,0:T(8,128)(2,1)S(1)}, u32[]{:S(2)}, u32[]{:S(2)}) collective-permute-start(bf16[2,176,256]{2,1,0:T(8,128)(2,1)S(1)} %collective-permute-done.5.refs_10_.own_high), channel_id=1, source_target_pairs={{0,4},{1,5},{2,6},{3,7},{8,12},{9,13},{10,14},{11,15},{16,20},{17,... | collective-permute-start | bytes 540680 | tf_op jit(solution)/shard_map/ppermute | solution.py:204
  13.4 1.3 %collective-permute-start.6 = (bf16[2,176,256]{2,1,0:T(8,128)(2,1)S(1)}, bf16[2,176,256]{2,1,0:T(8,128)(2,1)S(1)}, u32[]{:S(2)}, u32[]{:S(2)}) collective-permute-start(bf16[2,176,256]{2,1,0:T(8,128)(2,1)S(1)} %collective-permute-done.4.refs_9_.own_low), channel_id=1, source_target_pairs={{0,4},{1,5},{2,6},{3,7},{8,12},{9,13},{10,14},{11,15},{16,20},{17,... | collective-permute-start | bytes 540680 | tf_op jit(solution)/shard_map/ppermute | solution.py:203
  14.8 1.0 %copy-done = bf16[1,2,2,176,256]{4,3,2,1,0:T(8,128)(2,1)S(1)} copy-done((bf16[1,2,2,176,256]{4,3,2,1,0:T(8,128)(2,1)S(1)}, bf16[1,2,2,176,256]{4,3,2,1,0:T(8,128)(2,1)}, u32[]{:S(2)}) %copy-start) | copy-done | bytes 360472
  15.9 5.1 %collective-permute-start.3 = (f32[16,256]{1,0:T(8,128)S(1)}, f32[16,256]{1,0:T(8,128)S(1)}, u32[]{:S(2)}, u32[]{:S(2)}) collective-permute-start(f32[16,256]{1,0:T(8,128)S(1)} %stats.1.refs_1_), channel_id=1, source_target_pairs={{0,3},{1,2},{2,1},{3,0},{4,7},{5,6},{6,5},{7,4},{8,11},{9,10},{10,... | collective-permute-start | bytes 49160 | tf_op jit(solution)/shard_map/ppermute | solution.py:216
  21.8 1.0 %copy-done.2 = bf16[1,2,2,176,256]{4,3,2,1,0:T(8,128)(2,1)S(1)} copy-done((bf16[1,2,2,176,256]{4,3,2,1,0:T(8,128)(2,1)S(1)}, bf16[1,2,2,176,256]{4,3,2,1,0:T(8,128)(2,1)}, u32[]{:S(2)}) %copy-start.2) | copy-done | bytes 360472
  22.8 0.9 %cots.1.refs_13_ = bf16[3,3,2,176,256]{4,3,2,1,0:T(8,128)(2,1)S(1)} custom-call(s32[11]{0:T(128)S(1)} %stack.55.where_ref.refs_0_, bf16[2,2,176,256]{3,2,1,0:T(8,128)(2,1)S(1)} %bitcast.31, bf16[2,2,176,256]{3,2,1,0:T(8,128)(2,1)S(1)} %collective-permute-done.8.other_ref), custom_call_target="tpu_custom_call" | custom-call | flops 1802240 | bytes 2523136 | tf_op jit(solution)/shard_map/cots/pallas_call | solution.py:23
  23.7 1.0 %collective-permute-done.2.refs_3_ = f32[16,256]{1,0:T(8,128)S(1)} collective-permute-done((f32[16,256]{1,0:T(8,128)S(1)}, f32[16,256]{1,0:T(8,128)S(1)}, u32[]{:S(2)}, u32[]{:S(2)}) %collective-permute-start.2) | collective-permute-done | bytes 16416 | tf_op jit(solution)/shard_map/ppermute | solution.py:216
  24.7 2.3 %grad.1 = (bf16[2,4,176,256]{3,2,1,0:T(8,128)(2,1)S(1)}, f32[8,256]{1,0:T(8,128)S(1)}, f32[144,256]{1,0:T(8,128)S(1)}, bf16[144,256]{1,0:T(8,128)(2,1)S(1)}, bf1...) custom-call(s32[11]{0:T(128)S(1)} %stack.55.where_ref.refs_0_, ...), custom_call_target="tpu_custom_call" | custom-call | flops 622854144 | bytes 3604480 | tf_op jit(solution)/shard_map/grad/pallas_call | solution.py:23
  27.8 2.0 %collective-permute-start.10 = (bf16[144,256]{1,0:T(8,128)(2,1)S(1)}, bf16[144,256]{1,0:T(8,128)(2,1)S(1)}, u32[]{:S(2)}, u32[]{:S(2)}) collective-permute-start(bf16[144,256]{1,0:T(8,128)(2,1)S(1)} %get-tuple-element.16), channel_id=1, source_target_pairs={{0,2},{1,3},{2,0},{3,1},{8,10},{9,11},{10,8},{11,9},{16,18},{17,19... | collective-permute-start | bytes 221192 | tf_op jit(solution)/shard_map/ppermute | solution.py:270
  29.9 0.8 %collective-permute-start.11 = (bf16[144,256]{1,0:T(8,128)(2,1)S(1)}, bf16[144,256]{1,0:T(8,128)(2,1)S(1)}, u32[]{:S(2)}, u32[]{:S(2)}) collective-permute-start(bf16[144,256]{1,0:T(8,128)(2,1)S(1)} %get-tuple-element.17), channel_id=1, source_target_pairs={{0,3},{1,2},{2,1},{3,0},{8,11},{9,10},{10,9},{11,8},{16,19},{17,18... | collective-permute-start | bytes 221192 | tf_op jit(solution)/shard_map/ppermute | solution.py:270
  30.6 1.6 %collective-permute-start.12 = (bf16[144,256]{1,0:T(8,128)(2,1)S(1)}, bf16[144,256]{1,0:T(8,128)(2,1)S(1)}, u32[]{:S(2)}, u32[]{:S(2)}) collective-permute-start(bf16[144,256]{1,0:T(8,128)(2,1)S(1)} %get-tuple-element.18), channel_id=1, source_target_pairs={{0,8},{1,9},{2,10},{3,11},{8,0},{9,1},{10,2},{11,3},{16,24},{17,25... | collective-permute-start | bytes 221192 | tf_op jit(solution)/shard_map/ppermute | solution.py:270
  32.8 3.0 %collective-permute-start.14 = (bf16[144,256]{1,0:T(8,128)(2,1)S(1)}, bf16[144,256]{1,0:T(8,128)(2,1)S(1)}, u32[]{:S(2)}, u32[]{:S(2)}) collective-permute-start(bf16[144,256]{1,0:T(8,128)(2,1)S(1)} %get-tuple-element.20), channel_id=1, source_target_pairs={{0,10},{1,11},{2,8},{3,9},{8,2},{9,3},{10,0},{11,1},{16,26},{17,27... | collective-permute-start | bytes 221192 | tf_op jit(solution)/shard_map/ppermute | solution.py:270
  35.8 0.8 %collective-permute-start.15 = (bf16[144,256]{1,0:T(8,128)(2,1)S(1)}, bf16[144,256]{1,0:T(8,128)(2,1)S(1)}, u32[]{:S(2)}, u32[]{:S(2)}) collective-permute-start(bf16[144,256]{1,0:T(8,128)(2,1)S(1)} %get-tuple-element.21), channel_id=1, source_target_pairs={{0,11},{1,10},{2,9},{3,8},{8,3},{9,2},{10,1},{11,0},{16,27},{17,26... | collective-permute-start | bytes 221192 | tf_op jit(solution)/shard_map/ppermute | solution.py:270
  36.7 0.8 %collective-permute-done.13 = bf16[144,256]{1,0:T(8,128)(2,1)S(1)} collective-permute-done((bf16[144,256]{1,0:T(8,128)(2,1)S(1)}, bf16[144,256]{1,0:T(8,128)(2,1)S(1)}, u32[]{:S(2)}, u32[]{:S(2)}) %collective-permute-start.13) | collective-permute-done | bytes 73760 | tf_op jit(solution)/shard_map/ppermute | solution.py:270
  37.5 1.5 %collective-permute-done.14 = bf16[144,256]{1,0:T(8,128)(2,1)S(1)} collective-permute-done((bf16[144,256]{1,0:T(8,128)(2,1)S(1)}, bf16[144,256]{1,0:T(8,128)(2,1)S(1)}, u32[]{:S(2)}, u32[]{:S(2)}) %collective-permute-start.14) | collective-permute-done | bytes 73760 | tf_op jit(solution)/shard_map/ppermute | solution.py:270
  39.0 3.0 %collective-permute-done.15 = bf16[144,256]{1,0:T(8,128)(2,1)S(1)} collective-permute-done((bf16[144,256]{1,0:T(8,128)(2,1)S(1)}, bf16[144,256]{1,0:T(8,128)(2,1)S(1)}, u32[]{:S(2)}, u32[]{:S(2)}) %collective-permute-start.15) | collective-permute-done | bytes 73760 | tf_op jit(solution)/shard_map/ppermute | solution.py:270
  42.1 3.0 %collective-permute-start.18 = (bf16[144,256]{1,0:T(8,128)(2,1)S(1)}, bf16[144,256]{1,0:T(8,128)(2,1)S(1)}, u32[]{:S(2)}, u32[]{:S(2)}) collective-permute-start(bf16[144,256]{1,0:T(8,128)(2,1)S(1)} %add_convert_fusion), channel_id=1, source_target_pairs={{0,24},{8,16},{16,8},{24,0},{1,25},{9,17},{17,9},{25,1},{2,26},{10... | collective-permute-start | bytes 221192 | tf_op jit(solution)/shard_map/ppermute | solution.py:281
  45.1 0.8 %collective-permute-start.17 = (bf16[144,256]{1,0:T(8,128)(2,1)S(1)}, bf16[144,256]{1,0:T(8,128)(2,1)S(1)}, u32[]{:S(2)}, u32[]{:S(2)}) collective-permute-start(bf16[144,256]{1,0:T(8,128)(2,1)S(1)} %add_convert_fusion), channel_id=1, source_target_pairs={{0,8},{8,0},{16,24},{24,16},{1,9},{9,1},{17,25},{25,17},{2,10},{10... | collective-permute-start | bytes 221192 | tf_op jit(solution)/shard_map/ppermute | solution.py:281
  46.5 2.0 %copy-done.5 = bf16[3,3,3,256,256]{4,3,2,1,0:T(8,128)(2,1)S(1)} copy-done((bf16[3,3,3,256,256]{4,3,2,1,0:T(8,128)(2,1)S(1)}, bf16[3,3,3,256,256]{4,3,2,1,0:T(8,128)(2,1)}, u32[]{:S(2)}) %copy-start.5) | copy-done | bytes 3538968
  48.5 4.0 %conv.1 = bf16[2,2,176,256]{3,2,1,0:T(8,128)(2,1)} custom-call(s32[11]{0:T(128)S(1)} %stack.55.where_ref.refs_0_, f32[8,256]{1,0:T(8,128)S(1)} %get-tuple-element.12.norm_ref, bf16[2,4,176,256]{3,2,1,0:T(8,128)(2,1)S(1)} %get-tuple-element.13.act_ref, bf16[2,2,176,256]{3,2,1,0:T(8,128)(2,1)S(1)} %bitcast.28, ...), custom_call_target="tpu_custom_call" | custom-call | flops 2491416576 | bytes 4259840 | tf_op jit(solution)/shard_map/conv/pallas_call | solution.py:23
  (39 shorter events, 4.5 us)
Async XLA Ops:
  0.6 24.1 %copy-start.1 = (bf16[1,2,2,176,256]{4,3,2,1,0:T(8,128)(2,1)S(1)}, bf16[1,2,2,176,256]{4,3,2,1,0:T(8,128)(2,1)}, u32[]{:S(2)}) copy-start(bf16[1,2,2,176,256]{4,3,2,1,0:T(8,128)(2,1)} %param.6) | copy-start | bytes 1081348
  0.6 24.1 %copy-start.4 = (f32[256]{0:T(256)S(1)}, f32[256]{0:T(256)}, u32[]{:S(2)}) copy-start(f32[256]{0:T(256)} %param.8) | copy-start | bytes 3076
  0.7 24.1 %copy-start.3 = (f32[256]{0:T(256)S(1)}, f32[256]{0:T(256)}, u32[]{:S(2)}) copy-start(f32[256]{0:T(256)} %param.7) | copy-start | bytes 3076
  1.7 13.0 %collective-permute-start = (bf16[2,2,176,256]{3,2,0,1:T(8,128)(2,1)S(1)}, bf16[2,2,176,256]{3,2,0,1:T(8,128)(2,1)S(1)}, u32[]{:S(2)}, u32[]{:S(2)}) collective-permute-start(bf16[2,2,176,256]{3,2,0,1:T(8,128)(2,1)S(1)} %bitcast.35), channel_id=1, source_target_pairs={{0,4},{4,0},{1,5},{5,1},{2,6},{6,2},{3,7},{7,3},{8,12},{12,8},{9,1... | collective-permute-start | bytes 1081352 | tf_op jit(solution)/shard_map/ppermute | solution.py:199
  2.2 18.8 %collective-permute-start.8 = (bf16[2,2,176,256]{3,2,1,0:T(8,128)(2,1)}, bf16[2,2,176,256]{3,2,1,0:T(8,128)(2,1)S(1)}, u32[]{:S(2)}, u32[]{:S(2)}) collective-permute-start(bf16[2,2,176,256]{3,2,1,0:T(8,128)(2,1)} %bitcast.30), channel_id=1, source_target_pairs={{0,4},{4,0},{1,5},{5,1},{2,6},{6,2},{3,7},{7,3},{8,12},{12,8},{9,1... | collective-permute-start | bytes 1081352 | tf_op jit(solution)/shard_map/ppermute | solution.py:200
  2.3 9.6 %collective-permute-start.5 = (bf16[2,176,256]{2,1,0:T(8,128)(2,1)S(1)}, bf16[2,176,256]{2,1,0:T(8,128)(2,1)S(1)}, u32[]{:S(2)}, u32[]{:S(2)}) collective-permute-start(bf16[2,176,256]{2,1,0:T(8,128)(2,1)S(1)} %get-tuple-element.22), channel_id=1, source_target_pairs={{1,0},{2,1},{3,2},{5,4},{6,5},{7,6},{9,8},{10,9},{11,10},{13,12},{... | collective-permute-start | bytes 540680 | tf_op jit(solution)/shard_map/ppermute | solution.py:202
  3.6 9.8 %collective-permute-start.4 = (bf16[2,176,256]{2,1,0:T(8,128)(2,1)S(1)}, bf16[2,176,256]{2,1,0:T(8,128)(2,1)S(1)}, u32[]{:S(2)}, u32[]{:S(2)}) collective-permute-start(bf16[2,176,256]{2,1,0:T(8,128)(2,1)S(1)} %get-tuple-element.23), channel_id=1, source_target_pairs={{0,1},{1,2},{2,3},{4,5},{5,6},{6,7},{8,9},{9,10},{10,11},{12,13},{... | collective-permute-start | bytes 540680 | tf_op jit(solution)/shard_map/ppermute | solution.py:201
  12.0 11.7 %collective-permute-start.7 = (bf16[2,176,256]{2,1,0:T(8,128)(2,1)S(1)}, bf16[2,176,256]{2,1,0:T(8,128)(2,1)S(1)}, u32[]{:S(2)}, u32[]{:S(2)}) collective-permute-start(bf16[2,176,256]{2,1,0:T(8,128)(2,1)S(1)} %collective-permute-done.5.refs_10_.own_high), channel_id=1, source_target_pairs={{0,4},{1,5},{2,6},{3,7},{8,12},{9,13},{10,14},{11,15},{16,20},{17,... | collective-permute-start | bytes 540680 | tf_op jit(solution)/shard_map/ppermute | solution.py:204
  13.4 10.3 %collective-permute-start.6 = (bf16[2,176,256]{2,1,0:T(8,128)(2,1)S(1)}, bf16[2,176,256]{2,1,0:T(8,128)(2,1)S(1)}, u32[]{:S(2)}, u32[]{:S(2)}) collective-permute-start(bf16[2,176,256]{2,1,0:T(8,128)(2,1)S(1)} %collective-permute-done.4.refs_9_.own_low), channel_id=1, source_target_pairs={{0,4},{1,5},{2,6},{3,7},{8,12},{9,13},{10,14},{11,15},{16,20},{17,... | collective-permute-start | bytes 540680 | tf_op jit(solution)/shard_map/ppermute | solution.py:203
  15.8 30.8 %copy-start.6 = (f32[256]{0:T(256)S(1)}, f32[256]{0:T(256)}, u32[]{:S(2)}) copy-start(f32[256]{0:T(256)} %param.10) | copy-start | bytes 3076
  15.9 7.8 %collective-permute-start.3 = (f32[16,256]{1,0:T(8,128)S(1)}, f32[16,256]{1,0:T(8,128)S(1)}, u32[]{:S(2)}, u32[]{:S(2)}) collective-permute-start(f32[16,256]{1,0:T(8,128)S(1)} %stats.1.refs_1_), channel_id=1, source_target_pairs={{0,3},{1,2},{2,1},{3,0},{4,7},{5,6},{6,5},{7,4},{8,11},{9,10},{10,... | collective-permute-start | bytes 49160 | tf_op jit(solution)/shard_map/ppermute | solution.py:216
  21.0 3.7 %collective-permute-start.2 = (f32[16,256]{1,0:T(8,128)S(1)}, f32[16,256]{1,0:T(8,128)S(1)}, u32[]{:S(2)}, u32[]{:S(2)}) collective-permute-start(f32[16,256]{1,0:T(8,128)S(1)} %stats.1.refs_1_), channel_id=1, source_target_pairs={{0,2},{1,3},{2,0},{3,1},{4,6},{5,7},{6,4},{7,5},{8,10},{9,11},{10,... | collective-permute-start | bytes 49160 | tf_op jit(solution)/shard_map/ppermute | solution.py:216
  21.0 3.7 %collective-permute-start.1 = (f32[16,256]{1,0:T(8,128)S(1)}, f32[16,256]{1,0:T(8,128)S(1)}, u32[]{:S(2)}, u32[]{:S(2)}) collective-permute-start(f32[16,256]{1,0:T(8,128)S(1)} %stats.1.refs_1_), channel_id=1, source_target_pairs={{0,1},{1,0},{2,3},{3,2},{4,5},{5,4},{6,7},{7,6},{8,9},{9,8},{10,11... | collective-permute-start | bytes 49160 | tf_op jit(solution)/shard_map/ppermute | solution.py:216
  27.1 5.7 %collective-permute-start.9 = (bf16[144,256]{1,0:T(8,128)(2,1)S(1)}, bf16[144,256]{1,0:T(8,128)(2,1)S(1)}, u32[]{:S(2)}, u32[]{:S(2)}) collective-permute-start(bf16[144,256]{1,0:T(8,128)(2,1)S(1)} %get-tuple-element.15), channel_id=1, source_target_pairs={{0,1},{1,0},{2,3},{3,2},{8,9},{9,8},{10,11},{11,10},{16,17},{17,16... | collective-permute-start | bytes 221192 | tf_op jit(solution)/shard_map/ppermute | solution.py:270
  27.8 8.0 %collective-permute-start.10 = (bf16[144,256]{1,0:T(8,128)(2,1)S(1)}, bf16[144,256]{1,0:T(8,128)(2,1)S(1)}, u32[]{:S(2)}, u32[]{:S(2)}) collective-permute-start(bf16[144,256]{1,0:T(8,128)(2,1)S(1)} %get-tuple-element.16), channel_id=1, source_target_pairs={{0,2},{1,3},{2,0},{3,1},{8,10},{9,11},{10,8},{11,9},{16,18},{17,19... | collective-permute-start | bytes 221192 | tf_op jit(solution)/shard_map/ppermute | solution.py:270
  29.9 6.8 %collective-permute-start.11 = (bf16[144,256]{1,0:T(8,128)(2,1)S(1)}, bf16[144,256]{1,0:T(8,128)(2,1)S(1)}, u32[]{:S(2)}, u32[]{:S(2)}) collective-permute-start(bf16[144,256]{1,0:T(8,128)(2,1)S(1)} %get-tuple-element.17), channel_id=1, source_target_pairs={{0,3},{1,2},{2,1},{3,0},{8,11},{9,10},{10,9},{11,8},{16,19},{17,18... | collective-permute-start | bytes 221192 | tf_op jit(solution)/shard_map/ppermute | solution.py:270
  30.6 6.0 %collective-permute-start.12 = (bf16[144,256]{1,0:T(8,128)(2,1)S(1)}, bf16[144,256]{1,0:T(8,128)(2,1)S(1)}, u32[]{:S(2)}, u32[]{:S(2)}) collective-permute-start(bf16[144,256]{1,0:T(8,128)(2,1)S(1)} %get-tuple-element.18), channel_id=1, source_target_pairs={{0,8},{1,9},{2,10},{3,11},{8,0},{9,1},{10,2},{11,3},{16,24},{17,25... | collective-permute-start | bytes 221192 | tf_op jit(solution)/shard_map/ppermute | solution.py:270
  32.2 5.3 %collective-permute-start.13 = (bf16[144,256]{1,0:T(8,128)(2,1)S(1)}, bf16[144,256]{1,0:T(8,128)(2,1)S(1)}, u32[]{:S(2)}, u32[]{:S(2)}) collective-permute-start(bf16[144,256]{1,0:T(8,128)(2,1)S(1)} %get-tuple-element.19), channel_id=1, source_target_pairs={{0,9},{1,8},{2,11},{3,10},{8,1},{9,0},{10,3},{11,2},{16,25},{17,24... | collective-permute-start | bytes 221192 | tf_op jit(solution)/shard_map/ppermute | solution.py:270
  32.8 6.1 %collective-permute-start.14 = (bf16[144,256]{1,0:T(8,128)(2,1)S(1)}, bf16[144,256]{1,0:T(8,128)(2,1)S(1)}, u32[]{:S(2)}, u32[]{:S(2)}) collective-permute-start(bf16[144,256]{1,0:T(8,128)(2,1)S(1)} %get-tuple-element.20), channel_id=1, source_target_pairs={{0,10},{1,11},{2,8},{3,9},{8,2},{9,3},{10,0},{11,1},{16,26},{17,27... | collective-permute-start | bytes 221192 | tf_op jit(solution)/shard_map/ppermute | solution.py:270
  35.8 6.2 %collective-permute-start.15 = (bf16[144,256]{1,0:T(8,128)(2,1)S(1)}, bf16[144,256]{1,0:T(8,128)(2,1)S(1)}, u32[]{:S(2)}, u32[]{:S(2)}) collective-permute-start(bf16[144,256]{1,0:T(8,128)(2,1)S(1)} %get-tuple-element.21), channel_id=1, source_target_pairs={{0,11},{1,10},{2,9},{3,8},{8,3},{9,2},{10,1},{11,0},{16,27},{17,26... | collective-permute-start | bytes 221192 | tf_op jit(solution)/shard_map/ppermute | solution.py:270
  42.1 10.4 %collective-permute-start.18 = (bf16[144,256]{1,0:T(8,128)(2,1)S(1)}, bf16[144,256]{1,0:T(8,128)(2,1)S(1)}, u32[]{:S(2)}, u32[]{:S(2)}) collective-permute-start(bf16[144,256]{1,0:T(8,128)(2,1)S(1)} %add_convert_fusion), channel_id=1, source_target_pairs={{0,24},{8,16},{16,8},{24,0},{1,25},{9,17},{17,9},{25,1},{2,26},{10... | collective-permute-start | bytes 221192 | tf_op jit(solution)/shard_map/ppermute | solution.py:281
  45.1 7.5 %collective-permute-start.17 = (bf16[144,256]{1,0:T(8,128)(2,1)S(1)}, bf16[144,256]{1,0:T(8,128)(2,1)S(1)}, u32[]{:S(2)}, u32[]{:S(2)}) collective-permute-start(bf16[144,256]{1,0:T(8,128)(2,1)S(1)} %add_convert_fusion), channel_id=1, source_target_pairs={{0,8},{8,0},{16,24},{24,16},{1,9},{9,1},{17,25},{25,17},{2,10},{10... | collective-permute-start | bytes 221192 | tf_op jit(solution)/shard_map/ppermute | solution.py:281
  45.9 6.7 %collective-permute-start.16 = (bf16[144,256]{1,0:T(8,128)(2,1)S(1)}, bf16[144,256]{1,0:T(8,128)(2,1)S(1)}, u32[]{:S(2)}, u32[]{:S(2)}) collective-permute-start(bf16[144,256]{1,0:T(8,128)(2,1)S(1)} %add_convert_fusion), channel_id=1, source_target_pairs={{0,16},{8,24},{16,0},{24,8},{1,17},{9,25},{17,1},{25,9},{2,18},{10... | collective-permute-start | bytes 221192 | tf_op jit(solution)/shard_map/ppermute | solution.py:281
  46.5 2.0 %copy-start.5 = (bf16[3,3,3,256,256]{4,3,2,1,0:T(8,128)(2,1)S(1)}, bf16[3,3,3,256,256]{4,3,2,1,0:T(8,128)(2,1)}, u32[]{:S(2)}) copy-start(bf16[3,3,3,256,256]{4,3,2,1,0:T(8,128)(2,1)} %weight_ref.1) | copy-start | bytes 10616836
  (2 other events, 2.0 us)

commit v2 on v1

v2 whole, which is shorter than its diff:
```python
import functools

import jax
import jax.numpy as jnp
from jax import lax
from jax.experimental import pallas as pl
from jax.experimental.pallas import tpu as pltpu
from jax.sharding import PartitionSpec as P

GROUPS = 32
BF16 = jnp.bfloat16
F32 = jnp.float32
VMEM_LIMIT = 24 * 1024 * 1024


def call(kernel, outs, ins, scratch=(), flops=0, nbytes=0, trans=0, name=None, outside=(), limit=VMEM_LIMIT):
    specs = [
        pl.BlockSpec(memory_space=pltpu.HBM if k in outside else pltpu.SMEM if a.dtype == jnp.int32 else pltpu.VMEM)
        for k, a in enumerate(ins)
    ]
    return pl.pallas_call(
        kernel,
        out_shape=outs,
        in_specs=specs,
        out_specs=jax.tree.map(lambda _: pl.BlockSpec(memory_space=pltpu.VMEM), outs),
        scratch_shapes=list(scratch),
        compiler_params=pltpu.CompilerParams(vmem_limit_bytes=limit),
        cost_estimate=pl.CostEstimate(flops=flops, bytes_accessed=nbytes, transcendentals=trans),
        name=name,
    )(*ins)


def channel_sums(ref):
    frames, height, width, chans = ref.shape
    total = jnp.zeros((8, chans), F32)
    squares = jnp.zeros((8, chans), F32)
    for f in range(frames):
        for h in range(height):
            x = ref[f, h].astype(F32).reshape(width // 8, 8, chans)
            total = total + jnp.sum(x, axis=0)
            squares = squares + jnp.sum(x * x, axis=0)
    return jnp.concatenate([total, squares], axis=0)


def own_kernel(own_ref, copy_ref, sums_ref):
    copy_ref[...] = own_ref[...]
    sums_ref[...] = channel_sums(own_ref)


def prep_kernel(where_ref, own_sums_ref, own_ref, other_ref, sums_ref, early_ref, late_ref):
    frames, height, width, chans = own_ref.shape
    is_late = where_ref[0] == 1
    row = where_ref[3]
    sums = own_sums_ref[...] + channel_sums(other_ref)
    sums_ref[...] = sums
    for f in range(frames):
        mine = own_ref[f, row]
        other = other_ref[f, row]
        early_ref[f * width : (f + 1) * width, :] = jnp.where(is_late, other, mine)
        late_ref[f * width : (f + 1) * width, :] = jnp.where(is_late, mine, other)
    for k in range(3):
        term = sums.astype(BF16)
        early_ref[frames * width + 16 * k : frames * width + 16 * (k + 1), :] = term
        sums = sums - term.astype(F32)


def shift_rows(x, by):
    zero = jnp.zeros((1, x.shape[1]), x.dtype)
    if by == 1:
        return jnp.concatenate([x[1:], zero], axis=0)
    if by == -1:
        return jnp.concatenate([zero, x[:-1]], axis=0)
    return x


def cot_kernel(where_ref, own_ref, other_ref, out_ref):
    _, height, width, chans = own_ref.shape
    is_late = where_ref[0] == 1
    for h in range(height):
        a0 = own_ref[0, h].astype(F32)
        a1 = own_ref[1, h].astype(F32)
        b0 = other_ref[0, h].astype(F32)
        b1 = other_ref[1, h].astype(F32)
        first = a0 + b0 + jnp.where(is_late, b1, a1)
        last = jnp.where(is_late, a1, b1)
        high = first.astype(BF16).astype(F32)
        low = first - high
        for term, value in enumerate((high, low, last)):
            for kw in range(3):
                out_ref[kw, term, h] = shift_rows(value, 1 - kw).astype(BF16)


def group_sum(x, per_group):
    chans = x.shape[1]
    lane = lax.broadcasted_iota(jnp.int32, x.shape, 1)
    step = 1
    while step < per_group:
        up = pltpu.roll(x, step, 1)
        down = pltpu.roll(x, chans - step, 1)
        x = x + jnp.where((lane & step) != 0, up, down)
        step *= 2
    return x


def activate(x, scale, shift):
    v = x.astype(F32) * scale + shift
    return v * (0.5 + 0.5 * jnp.tanh(0.5 * v))


def grad_kernel(count, decode, n_stats, n_pieces, rows_out, *refs):
    where_ref = refs[0]
    stats = refs[1 : 1 + n_stats]
    params_ref, own_ref, other_ref, near_ref, far_ref, cots_ref = refs[1 + n_stats : 7 + n_stats]
    act_ref, norm_ref = refs[7 + n_stats : 9 + n_stats]
    pieces = refs[9 + n_stats : 9 + n_stats + n_pieces]
    wg_ref = refs[9 + n_stats + n_pieces]
    late = where_ref[0]
    is_late = late == 1
    low_is_near = where_ref[4] == 1
    frames, height, width, chans = own_ref.shape
    sums = stats[0][...]
    for ref in stats[1:]:
        sums = sums + ref[...]
    if decode:
        for ref in (near_ref, far_ref):
            base = frames * width
            terms = [ref[base + 16 * k : base + 16 * (k + 1), :].astype(F32) for k in range(3)]
            sums = sums + (terms[0] + (terms[1] + terms[2]))
    total = jnp.sum(sums[0:8], axis=0, keepdims=True)
    squares = jnp.sum(sums[8:16], axis=0, keepdims=True)
    both = group_sum(jnp.concatenate([total, squares] + [total] * 6, axis=0), chans // GROUPS) / count
    mean = both[0:1]
    var = both[1:2] - mean * mean
    scale = lax.rsqrt(var + 1e-06) * params_ref[0:1, :]
    shift = params_ref[1:2, :] - mean * scale
    norm_ref[0:1, :] = scale
    norm_ref[1:2, :] = shift
    norm_ref[2:8, :] = jnp.zeros((6, chans), F32)
    keep_low = (where_ref[1] != 0).astype(F32)
    keep_high = (where_ref[2] != 0).astype(F32)
    for f in range(frames):
        near = near_ref[f * width : (f + 1) * width, :]
        far = far_ref[f * width : (f + 1) * width, :]
        low = jnp.where(low_is_near, near, far)
        act_ref[f, 0] = (activate(low, scale, shift) * keep_low).astype(BF16)
        for h in range(height):
            x = jnp.where(is_late, other_ref[f, h], own_ref[f, h])
            act_ref[f, h + 1] = activate(x, scale, shift).astype(BF16)
        high = jnp.where(low_is_near, far, near)
        act_ref[f, height + 1] = (activate(high, scale, shift) * keep_high).astype(BF16)

    contract = (((0,), (0,)), ((), ()))
    terms = 3 * height * width

    def stack(kh):
        a0 = act_ref[0, pl.ds(kh, height)].reshape(height * width, chans)
        a1 = act_ref[1, pl.ds(kh, height)].reshape(height * width, chans)
        return jnp.concatenate([a0, a0, a1], axis=0)

    def cots(kw):
        return cots_ref[kw].reshape(terms, chans)

    half = chans // 2
    outer = stack(2 * late)
    base = pl.multiple_of(late * (chans + half), half)
    for kw in range(3):
        wg_ref[pl.ds(base + kw * chans, chans), :] = lax.dot_general(
            outer, cots(kw), contract, preferred_element_type=F32
        )
    middle = stack(1)
    base = pl.multiple_of(3 * chans - late * (5 * half), half)
    wg_ref[pl.ds(base, chans), :] = lax.dot_general(middle, cots(2 * late), contract, preferred_element_type=F32)
    lanes = jnp.where(is_late, middle[:, half:], middle[:, :half])
    base = pl.multiple_of((1 - late) * (4 * chans), half)
    wg_ref[pl.ds(base, half), :] = lax.dot_general(lanes, cots(1), contract, preferred_element_type=F32)
    for k, ref in enumerate(pieces):
        start = pl.multiple_of(where_ref[5 + k], 16)
        ref[...] = wg_ref[pl.ds(start, rows_out), :].astype(ref.dtype)


def conv_kernel(where_ref, norm_ref, act_ref, own_ref, near_ref, far_ref, weight_hbm, params_ref, out_ref, planes, acc, weight_ref, sems):
    copies = [pltpu.make_async_copy(weight_hbm.at[:, :, kw], weight_ref.at[:, :, kw], sems.at[kw]) for kw in range(3)]
    for c in copies:
        c.start()
    late = where_ref[0]
    low_is_near = where_ref[4] == 1
    frames, height, width, chans = own_ref.shape
    planes[0] = act_ref[0]
    planes[1] = act_ref[late]

    @pl.when(late == 0)
    def _():
        planes[2] = act_ref[0]
        planes[3] = act_ref[1]

    @pl.when(late == 1)
    def _():
        scale = norm_ref[0:1, :]
        shift = norm_ref[1:2, :]
        keep_low = (where_ref[1] != 0).astype(F32)
        keep_high = (where_ref[2] != 0).astype(F32)
        for f in range(frames):
            near = near_ref[f * width : (f + 1) * width, :]
            far = far_ref[f * width : (f + 1) * width, :]
            low = jnp.where(low_is_near, near, far)
            high = jnp.where(low_is_near, far, near)
            planes[frames + f, 0] = (activate(low, scale, shift) * keep_low).astype(BF16)
            for h in range(height):
                planes[frames + f, h + 1] = activate(own_ref[f, h], scale, shift).astype(BF16)
            planes[frames + f, height + 1] = (activate(high, scale, shift) * keep_high).astype(BF16)

    for kw in range(3):
        copies[kw].wait()
        for f in range(frames):
            total = None
            for kt in range(3):
                for kh in range(3):
                    lhs = planes[f + kt, kh : kh + height].reshape(height * width, chans)
                    part = jnp.dot(lhs, weight_ref[kt, kh, kw], preferred_element_type=F32)
                    total = part if total is None else total + part
            total = total.reshape(height, width, chans)
            for h in range(height):
                if kw == 0:
                    acc[f, h] = shift_rows(total[h], -1)
                elif kw == 1:
                    acc[f, h] = acc[f, h] + total[h]
                else:
                    value = own_ref[f, h].astype(F32) + params_ref[2:3, :] + acc[f, h] + shift_rows(total[h], 1)
                    out_ref[f, h] = value.astype(BF16)


def body(dp, rows, latent, gamma, beta, weight, bias, cotangent):
    nclip, frames, height, width, chans = latent.shape
    lat = latent[0]
    cot = cotangent[0]
    swap = [(0, 1), (1, 0)]
    clip = lax.axis_index("dp")
    late = lax.axis_index("tm")
    band = lax.axis_index("rows")
    count = frames * height * width * (chans // GROUPS) * 2 * rows
    size = frames * height * width * chans
    small = rows == 4 and dp == 4

    odd = band % 2
    beyond = [(r - 1) % rows if r % 2 == 0 else (r + 1) % rows for r in range(rows)]
    joint = [(r, r ^ 1) for r in range(rows)] + [(rows + r, rows + beyond[r]) for r in range(rows)]
    low_is_near = (odd ^ late) if rows > 1 else late
    edge_row = jnp.where(low_is_near == 1, 0, height - 1)
    head = [late, (band != 0), (band != rows - 1), edge_row, low_is_near]

    other = lax.ppermute(lat, "tm", swap)
    other_cot = lax.ppermute(cot, "tm", swap)
    lat, own_sums = call(
        own_kernel,
        [jax.ShapeDtypeStruct(lat.shape, lat.dtype), jax.ShapeDtypeStruct((16, chans), F32)],
        (lat,),
        flops=3 * size,
        nbytes=4 * size,
        name="own",
    )
    half = 9 * chans // 2
    if small:
        piece = half // 8
        order = [(0, 0), (0, 2), (1, 3), (1, 2), (1, 0), (1, 1), (0, 3), (0, 1)]
        starts = [(band ^ dr) * (2 * piece) + ((clip ^ dz) & 1) * piece for dz, dr in order]
        kinds = [F32] + [BF16] * 7
    else:
        piece = half
        starts = [jnp.int32(0)]
        kinds = [F32]
    where = jnp.stack([jnp.asarray(v).astype(jnp.int32) for v in head + starts])
    sums, early_rims, late_rims = call(
        prep_kernel,
        [
            jax.ShapeDtypeStruct((16, chans), F32),
            jax.ShapeDtypeStruct((frames * width + 48, chans), BF16),
            jax.ShapeDtypeStruct((frames * width, chans), BF16),
        ],
        (where, own_sums, lat, other),
        flops=3 * size,
        nbytes=6 * size,
        name="prep",
    )
    near = lax.ppermute(early_rims, ("tm", "rows"), joint)
    if small:
        stats = [sums, lax.ppermute(sums, "rows", [(r, r ^ 2) for r in range(rows)])]
    else:
        stats = [lax.psum(sums, "rows")]
    params = jnp.stack([gamma, beta, bias] + [jnp.zeros_like(bias)] * 5)
    cots = call(
        cot_kernel,
        jax.ShapeDtypeStruct((3, 3, height, width, chans), BF16),
        (where, cot, other_cot),
        flops=10 * size,
        nbytes=14 * size,
        name="cots",
    )
    near_late = lax.ppermute(late_rims, ("tm", "rows"), joint)
    near, cots, params, stats[-1] = lax.optimization_barrier((near, cots, params, stats[-1]))
    far = lax.ppermute(near, "tm", swap)
    far_late = lax.ppermute(near_late, "tm", swap)
    act, norm, *parts = call(
        functools.partial(grad_kernel, count, small, len(stats), len(kinds), piece),
        [
            jax.ShapeDtypeStruct((frames, height + 2, width, chans), BF16),
            jax.ShapeDtypeStruct((8, chans), F32),
        ]
        + [jax.ShapeDtypeStruct((piece, chans), k) for k in kinds],
        (where, *stats, params, lat, other, near, far, cots),
        scratch=[pltpu.VMEM((half, chans), F32)],
        flops=2 * half * 3 * height * width * chans,
        nbytes=20 * size,
        trans=2 * size,
        name="grad",
    )
    def convolve():
        return call(
            conv_kernel,
            jax.ShapeDtypeStruct((frames, height, width, chans), BF16),
            (where, norm, act, lat, near_late, far_late, weight, params),
            scratch=[
                pltpu.VMEM((4, height + 2, width, chans), BF16),
                pltpu.VMEM((frames, height, width, chans), F32),
                pltpu.VMEM(weight.shape, weight.dtype),
                pltpu.SemaphoreType.DMA((3,)),
            ],
            flops=2 * 27 * size * chans,
            nbytes=4 * size + 2 * weight.size,
            trans=2 * size,
            name="conv",
            outside=(6,),
            limit=51 * 1024 * 1024,
        )

    if small:
        got = [
            lax.ppermute(
                p,
                ("dp", "rows"),
                [(z * 4 + r, (z ^ dz) * 4 + (r ^ dr)) for z in range(4) for r in range(4)],
            )
            for p, (dz, dr) in zip(parts[1:], order[1:])
        ]
        total = parts[0]
        for g in got:
            total = total + g.astype(F32)
        total, far_late = lax.optimization_barrier((total.astype(BF16), far_late))
        by = [total] + [lax.ppermute(total, "dp", [(z, z ^ k) for z in range(4)]) for k in (1, 2, 3)]
        output = convolve()
        *by, output = lax.optimization_barrier((*by, output))
        by = [b.astype(F32) for b in by]
        mine = by[0] + by[2]
        theirs = by[1] + by[3]
        even = clip % 2 == 0
        grad = jnp.concatenate([jnp.where(even, mine, theirs), jnp.where(even, theirs, mine)], axis=0)
    else:
        output = convolve()
        grad = lax.psum(lax.psum_scatter(parts[0], "rows", scatter_dimension=0, tiled=True), "dp")
    return output[None], grad


def solution(mesh):
    placed = (
        P("dp", "tm", "rows", None, None),
        P(),
        P(),
        P(),
        P(),
        P("dp", "tm", "rows", None, None),
    )
    return jax.shard_map(
        functools.partial(body, mesh.shape["dp"], mesh.shape["rows"]),
        mesh=mesh,
        in_specs=placed,
        out_specs=(P("dp", "tm", "rows", None, None), P(("tm", "rows"), None)),
        check_vma=False,
    )
```

time: 53.6 us -> 42 us (0.78)
  starting transfers between devices: 29.9 us -> 21.4 us
  waiting for transfers between devices: 9.22 us -> 6.46 us
  local copies, waits for them, and re-layouts: 5.17 us -> 2.78 us
  Pallas kernels: 7.35 us -> 9.5 us
    ppermute x7 -> x5, starting transfers between devices: 15.3 us -> 6.93 us  [the longest x1 2.92 us: body(): near = lax.ppermute(early_rims, ('tm', 'rows'), joint)]
    unnamed x15 -> x4, local copies, waits for them, and re-layouts: 5.04 us -> 1.96 us
    ppermute x7 -> x5, waiting for transfers between devices: 3.88 us -> 1.19 us  [the longest x1 1.18 us: body(): near = lax.ppermute(early_rims, ('tm', 'rows'), joint)]
    pallas_call x4 -> x5, Pallas kernels: 7.35 us -> 9.5 us  [call(): pl.pallas_call(kernel, out_shape=outs, in_specs=specs, out_specs=jax.tree...]
    another operation x1 -> x4, local copies, waits for them, and re-layouts: 0.09 us -> 0.82 us  [the longest x3 0.73 us: body(): params = jnp.stack([gamma, beta, bias] + [jnp.zeros_like(bias)] * 5)]
  transfers between devices with their start and end apart: 19 -> 17, of which waited for: 5 -> 6; matrix products, arithmetic and copies ran while one was open for 0% -> 2% of each run, Pallas kernels for 9% -> 23%
where the time goes in v2:
time: 42 us; the launch traced here: 41.7 us
  starting transfers between devices  21.4 us (51%)
  Pallas kernels  9.5 us (23%)
  waiting for transfers between devices  6.46 us (15%)
  local copies, waits for them, and re-layouts  2.78 us (7%)
  other arithmetic  0.87 us (2%)
  between operations  0.75 us (2%)
    pallas_call x5, Pallas kernels, call(): pl.pallas_call(kernel, out_shape=outs, in_specs=specs, out_specs=jax.tree...  9.5 us
    ppermute x7, starting transfers between devices, body(): lax.ppermute(p, ('dp', 'rows'), [(z * 4 + r, (z ^ dz) * 4 + (r ^ dr)) for...  9.4 us
    ppermute x7, waiting for transfers between devices, body(): lax.ppermute(p, ('dp', 'rows'), [(z * 4 + r, (z ^ dz) * 4 + (r ^ dr)) for...  4.97 us
    ppermute x3, starting transfers between devices, body(): lax.ppermute(total, 'dp', [(z, z ^ k) for z in range(4)])  4.45 us
    ppermute x1, starting transfers between devices, body(): near = lax.ppermute(early_rims, ('tm', 'rows'), joint)  2.92 us
    ppermute x1, starting transfers between devices, body(): near_late = lax.ppermute(late_rims, ('tm', 'rows'), joint)  2.19 us
    unnamed x4, local copies, waits for them, and re-layouts  1.96 us
    ppermute x1, starting transfers between devices, body(): lax.ppermute(sums, 'rows', [(r, r ^ 2) for r in range(rows)])  1.52 us
  transfers between devices with their start and end apart: 17, of which 6 were waited for; matrix products, arithmetic and copies ran while one was open for 2% of the time, Pallas kernels for 23%

profile of v2, /device:TPU:0, one launch (start us, length us, event | category | flops | bytes accessed | tf_op | source)
XLA Modules:
  0.0 41.7 jit_solution(17111422754621745347)
XLA Ops:
  1.3 1.0 %copy-done.1 = bf16[1,2,2,176,256]{4,3,2,1,0:T(8,128)(2,1)S(1)} copy-done((bf16[1,2,2,176,256]{4,3,2,1,0:T(8,128)(2,1)S(1)}, bf16[1,2,2,176,256]{4,3,2,1,0:T(8,128)(2,1)}, u32[]{:S(2)}) %copy-start.1) | copy-done | bytes 360472
  2.7 0.6 %prep.1 = (f32[16,256]{1,0:T(8,128)S(1)}, bf16[400,256]{1,0:T(8,128)(2,1)S(1)}, bf16[352,256]{1,0:T(8,128)(2,1)S(1)}) custom-call(s32[13]{0:T(128)S(1)} %stack.78.where_ref.refs_0_, f32[16,256]{1,0:T(8,128)S(1)} %get-tuple-element.28.own_sums_ref, bf16[2,2,176,256]{3,2,1,0:T(8,128)(2,1)S(1)} %get-tuple-element.29.own_ref.refs_4_, ...), custom_call_target="tpu_custom_call" | custom-call | flops 540672 | bytes 1081344 | tf_op jit(solution)/shard_map/prep/pallas_call | solution.py:21
  3.3 2.9 %collective-permute-start.1 = (bf16[400,256]{1,0:T(8,128)(2,1)S(1)}, bf16[400,256]{1,0:T(8,128)(2,1)S(1)}, u32[]{:S(2)}, u32[]{:S(2)}) collective-permute-start(bf16[400,256]{1,0:T(8,128)(2,1)S(1)} %get-tuple-element.31), channel_id=1, source_target_pairs={{0,1},{1,0},{2,3},{3,2},{4,7},{5,6},{6,5},{7,4},{8,9},{9,8},{10,11... | collective-permute-start | bytes 614408 | tf_op jit(solution)/shard_map/ppermute | solution.py:284
  6.2 1.5 %collective-permute-start.3 = (f32[16,256]{1,0:T(8,128)S(1)}, f32[16,256]{1,0:T(8,128)S(1)}, u32[]{:S(2)}, u32[]{:S(2)}) collective-permute-start(f32[16,256]{1,0:T(8,128)S(1)} %get-tuple-element.30.refs_1_), channel_id=1, source_target_pairs={{0,2},{1,3},{2,0},{3,1},{4,6},{5,7},{6,4},{7,5},{8,10},{9,11},{10,... | collective-permute-start | bytes 49160 | tf_op jit(solution)/shard_map/ppermute | solution.py:286
  7.7 0.7 %stack.83.refs_3_.params_ref = f32[8,256]{1,0:T(8,128)S(1)} concatenate(f32[1,256]{1,0:T(1,128)} %bitcast.23, f32[1,256]{1,0:T(1,128)} %bitcast.24, f32[1,256]{1,0:T(1,128)} %bitcast.25, f32[1,256]{1,0:T(1,128)S(1)} %stack_broadcast_in_dim.3, f32[4,256]{1,0:T(4,128)S(1)} %stack.82), dimensions={0} | concatenate | bytes 16384 | tf_op jit(solution)/shard_map/stack | solution.py:289
  8.5 1.0 %copy-done = bf16[1,2,2,176,256]{4,3,2,1,0:T(8,128)(2,1)S(1)} copy-done((bf16[1,2,2,176,256]{4,3,2,1,0:T(8,128)(2,1)S(1)}, bf16[1,2,2,176,256]{4,3,2,1,0:T(8,128)(2,1)}, u32[]{:S(2)}) %copy-start) | copy-done | bytes 360472
  9.5 0.9 %cots.1.refs_8_ = bf16[3,3,2,176,256]{4,3,2,1,0:T(8,128)(2,1)S(1)} custom-call(s32[13]{0:T(128)S(1)} %stack.78.where_ref.refs_0_, bf16[2,2,176,256]{3,2,1,0:T(8,128)(2,1)S(1)} %bitcast.20, bf16[2,2,176,256]{3,2,1,0:T(8,128)(2,1)S(1)} %collective-permute-done.2.other_ref), custom_call_target="tpu_custom_call" | custom-call | flops 1802240 | bytes 2523136 | tf_op jit(solution)/shard_map/cots/pallas_call | solution.py:21
  10.4 1.2 %collective-permute-done.1.refs_6_ = bf16[400,256]{1,0:T(8,128)(2,1)S(1)} collective-permute-done((bf16[400,256]{1,0:T(8,128)(2,1)S(1)}, bf16[400,256]{1,0:T(8,128)(2,1)S(1)}, u32[]{:S(2)}, u32[]{:S(2)}) %collective-permute-start.1) | collective-permute-done | bytes 204832 | tf_op jit(solution)/shard_map/ppermute | solution.py:284
  11.9 2.2 %collective-permute-start.12 = (bf16[352,256]{1,0:T(8,128)(2,1)S(1)}, bf16[352,256]{1,0:T(8,128)(2,1)S(1)}, u32[]{:S(2)}, u32[]{:S(2)}) collective-permute-start(bf16[352,256]{1,0:T(8,128)(2,1)S(1)} %get-tuple-element.44), channel_id=1, source_target_pairs={{0,1},{1,0},{2,3},{3,2},{4,7},{5,6},{6,5},{7,4},{8,9},{9,8},{10,11... | collective-permute-start | bytes 540680 | tf_op jit(solution)/shard_map/ppermute | solution.py:298
  14.1 2.3 %grad.1 = (bf16[2,4,176,256]{3,2,1,0:T(8,128)(2,1)S(1)}, f32[8,256]{1,0:T(8,128)S(1)}, f32[144,256]{1,0:T(8,128)S(1)}, bf16[144,256]{1,0:T(8,128)(2,1)S(1)}, bf1...) custom-call(s32[13]{0:T(128)S(1)} %stack.78.where_ref.refs_0_, ...), custom_call_target="tpu_custom_call" | custom-call | flops 622854144 | bytes 3604480 | tf_op jit(solution)/shard_map/grad/pallas_call | solution.py:21
  16.4 2.0 %collective-permute-start.10 = (bf16[144,256]{1,0:T(8,128)(2,1)S(1)}, bf16[144,256]{1,0:T(8,128)(2,1)S(1)}, u32[]{:S(2)}, u32[]{:S(2)}) collective-permute-start(bf16[144,256]{1,0:T(8,128)(2,1)S(1)} %get-tuple-element.42), channel_id=1, source_target_pairs={{0,3},{1,2},{2,1},{3,0},{8,11},{9,10},{10,9},{11,8},{16,19},{17,18... | collective-permute-start | bytes 221192 | tf_op jit(solution)/shard_map/ppermute | solution.py:337
  18.4 0.9 %collective-permute-start.11 = (bf16[144,256]{1,0:T(8,128)(2,1)S(1)}, bf16[144,256]{1,0:T(8,128)(2,1)S(1)}, u32[]{:S(2)}, u32[]{:S(2)}) collective-permute-start(bf16[144,256]{1,0:T(8,128)(2,1)S(1)} %get-tuple-element.43), channel_id=1, source_target_pairs={{0,1},{1,0},{2,3},{3,2},{8,9},{9,8},{10,11},{11,10},{16,17},{17,16... | collective-permute-start | bytes 221192 | tf_op jit(solution)/shard_map/ppermute | solution.py:337
  19.3 0.6 %collective-permute-start.5 = (bf16[144,256]{1,0:T(8,128)(2,1)S(1)}, bf16[144,256]{1,0:T(8,128)(2,1)S(1)}, u32[]{:S(2)}, u32[]{:S(2)}) collective-permute-start(bf16[144,256]{1,0:T(8,128)(2,1)S(1)} %get-tuple-element.37), channel_id=1, source_target_pairs={{0,2},{1,3},{2,0},{3,1},{8,10},{9,11},{10,8},{11,9},{16,18},{17,19... | collective-permute-start | bytes 221192 | tf_op jit(solution)/shard_map/ppermute | solution.py:337
  19.9 2.9 %collective-permute-start.6 = (bf16[144,256]{1,0:T(8,128)(2,1)S(1)}, bf16[144,256]{1,0:T(8,128)(2,1)S(1)}, u32[]{:S(2)}, u32[]{:S(2)}) collective-permute-start(bf16[144,256]{1,0:T(8,128)(2,1)S(1)} %get-tuple-element.38), channel_id=1, source_target_pairs={{0,11},{1,10},{2,9},{3,8},{8,3},{9,2},{10,1},{11,0},{16,27},{17,26... | collective-permute-start | bytes 221192 | tf_op jit(solution)/shard_map/ppermute | solution.py:337
  22.9 0.9 %collective-permute-start.7 = (bf16[144,256]{1,0:T(8,128)(2,1)S(1)}, bf16[144,256]{1,0:T(8,128)(2,1)S(1)}, u32[]{:S(2)}, u32[]{:S(2)}) collective-permute-start(bf16[144,256]{1,0:T(8,128)(2,1)S(1)} %get-tuple-element.39), channel_id=1, source_target_pairs={{0,10},{1,11},{2,8},{3,9},{8,2},{9,3},{10,0},{11,1},{16,26},{17,27... | collective-permute-start | bytes 221192 | tf_op jit(solution)/shard_map/ppermute | solution.py:337
  23.8 1.6 %collective-permute-start.8 = (bf16[144,256]{1,0:T(8,128)(2,1)S(1)}, bf16[144,256]{1,0:T(8,128)(2,1)S(1)}, u32[]{:S(2)}, u32[]{:S(2)}) collective-permute-start(bf16[144,256]{1,0:T(8,128)(2,1)S(1)} %get-tuple-element.40), channel_id=1, source_target_pairs={{0,8},{1,9},{2,10},{3,11},{8,0},{9,1},{10,2},{11,3},{16,24},{17,25... | collective-permute-start | bytes 221192 | tf_op jit(solution)/shard_map/ppermute | solution.py:337
  25.8 0.6 %collective-permute-done.6 = bf16[144,256]{1,0:T(8,128)(2,1)S(1)} collective-permute-done((bf16[144,256]{1,0:T(8,128)(2,1)S(1)}, bf16[144,256]{1,0:T(8,128)(2,1)S(1)}, u32[]{:S(2)}, u32[]{:S(2)}) %collective-permute-start.6) | collective-permute-done | bytes 73760 | tf_op jit(solution)/shard_map/ppermute | solution.py:337
  26.4 2.6 %collective-permute-done.7 = bf16[144,256]{1,0:T(8,128)(2,1)S(1)} collective-permute-done((bf16[144,256]{1,0:T(8,128)(2,1)S(1)}, bf16[144,256]{1,0:T(8,128)(2,1)S(1)}, u32[]{:S(2)}, u32[]{:S(2)}) %collective-permute-start.7) | collective-permute-done | bytes 73760 | tf_op jit(solution)/shard_map/ppermute | solution.py:337
  29.6 1.2 %collective-permute-done.9 = bf16[144,256]{1,0:T(8,128)(2,1)S(1)} collective-permute-done((bf16[144,256]{1,0:T(8,128)(2,1)S(1)}, bf16[144,256]{1,0:T(8,128)(2,1)S(1)}, u32[]{:S(2)}, u32[]{:S(2)}) %collective-permute-start.9) | collective-permute-done | bytes 73760 | tf_op jit(solution)/shard_map/ppermute | solution.py:337
  30.9 0.9 %collective-permute-start.14 = (bf16[144,256]{1,0:T(8,128)(2,1)S(1)}, bf16[144,256]{1,0:T(8,128)(2,1)S(1)}, u32[]{:S(2)}, u32[]{:S(2)}) collective-permute-start(bf16[144,256]{1,0:T(8,128)(2,1)S(1)} %add_convert_fusion), channel_id=1, source_target_pairs={{0,8},{8,0},{16,24},{24,16},{1,9},{9,1},{17,25},{25,17},{2,10},{10... | collective-permute-start | bytes 221192 | tf_op jit(solution)/shard_map/ppermute | solution.py:348
  31.8 2.6 %collective-permute-start.15 = (bf16[144,256]{1,0:T(8,128)(2,1)S(1)}, bf16[144,256]{1,0:T(8,128)(2,1)S(1)}, u32[]{:S(2)}, u32[]{:S(2)}) collective-permute-start(bf16[144,256]{1,0:T(8,128)(2,1)S(1)} %add_convert_fusion), channel_id=1, source_target_pairs={{0,16},{8,24},{16,0},{24,8},{1,17},{9,25},{17,1},{25,9},{2,18},{10... | collective-permute-start | bytes 221192 | tf_op jit(solution)/shard_map/ppermute | solution.py:348
  34.4 1.0 %collective-permute-start.16 = (bf16[144,256]{1,0:T(8,128)(2,1)S(1)}, bf16[144,256]{1,0:T(8,128)(2,1)S(1)}, u32[]{:S(2)}, u32[]{:S(2)}) collective-permute-start(bf16[144,256]{1,0:T(8,128)(2,1)S(1)} %add_convert_fusion), channel_id=1, source_target_pairs={{0,24},{8,16},{16,8},{24,0},{1,25},{9,17},{17,9},{25,1},{2,26},{10... | collective-permute-start | bytes 221192 | tf_op jit(solution)/shard_map/ppermute | solution.py:348
  35.3 5.6 %conv.1 = bf16[2,2,176,256]{3,2,1,0:T(8,128)(2,1)} custom-call(s32[13]{0:T(128)S(1)} %stack.78.where_ref.refs_0_, f32[8,256]{1,0:T(8,128)S(1)} %get-tuple-element.46.norm_ref, bf16[2,4,176,256]{3,2,1,0:T(8,128)(2,1)S(1)} %get-tuple-element.47.act_ref, bf16[2,2,176,256]{3,2,1,0:T(8,128)(2,1)S(1)} %get-tuple-element.29.own_ref.refs_4_, ...), custom_call_target="tpu_custom_call" | custom-call | flops 2491416576 | bytes 4259840 | tf_op jit(solution)/shard_map/conv/pallas_call | solution.py:21
  41.0 0.7 %pad_maximum_fusion = f32[288,256]{1,0:T(8,128)} fusion(f32[144,256]{1,0:T(8,128)S(1)} %get-tuple-element.55, f32[144,256]{1,0:T(8,128)S(1)} %get-tuple-element.54), kind=kLoop, calls=%fused_computation | loop fusion | flops 73728 | bytes 589824 | tf_op jit(solution)/shard_map/concatenate | solution.py:355
  (26 shorter events, 2.6 us)
Async XLA Ops:
  0.6 2.0 %collective-permute-start = (bf16[2,2,176,256]{3,2,1,0:T(8,128)(2,1)}, bf16[2,2,176,256]{3,2,1,0:T(8,128)(2,1)S(1)}, u32[]{:S(2)}, u32[]{:S(2)}) collective-permute-start(bf16[2,2,176,256]{3,2,1,0:T(8,128)(2,1)} %bitcast.21), channel_id=1, source_target_pairs={{0,4},{4,0},{1,5},{5,1},{2,6},{6,2},{3,7},{7,3},{8,12},{12,8},{9,1... | collective-permute-start | bytes 1081352 | tf_op jit(solution)/shard_map/ppermute | solution.py:251
  1.1 7.3 %collective-permute-start.2 = (bf16[2,2,176,256]{3,2,1,0:T(8,128)(2,1)}, bf16[2,2,176,256]{3,2,1,0:T(8,128)(2,1)S(1)}, u32[]{:S(2)}, u32[]{:S(2)}) collective-permute-start(bf16[2,2,176,256]{3,2,1,0:T(8,128)(2,1)} %bitcast.19), channel_id=1, source_target_pairs={{0,4},{4,0},{1,5},{5,1},{2,6},{6,2},{3,7},{7,3},{8,12},{12,8},{9,1... | collective-permute-start | bytes 1081352 | tf_op jit(solution)/shard_map/ppermute | solution.py:252
  1.3 1.0 %copy-start.1 = (bf16[1,2,2,176,256]{4,3,2,1,0:T(8,128)(2,1)S(1)}, bf16[1,2,2,176,256]{4,3,2,1,0:T(8,128)(2,1)}, u32[]{:S(2)}) copy-start(bf16[1,2,2,176,256]{4,3,2,1,0:T(8,128)(2,1)} %param.6) | copy-start | bytes 1081348
  3.3 8.3 %collective-permute-start.1 = (bf16[400,256]{1,0:T(8,128)(2,1)S(1)}, bf16[400,256]{1,0:T(8,128)(2,1)S(1)}, u32[]{:S(2)}, u32[]{:S(2)}) collective-permute-start(bf16[400,256]{1,0:T(8,128)(2,1)S(1)} %get-tuple-element.31), channel_id=1, source_target_pairs={{0,1},{1,0},{2,3},{3,2},{4,7},{5,6},{6,5},{7,4},{8,9},{9,8},{10,11... | collective-permute-start | bytes 614408 | tf_op jit(solution)/shard_map/ppermute | solution.py:284
  6.2 4.2 %collective-permute-start.3 = (f32[16,256]{1,0:T(8,128)S(1)}, f32[16,256]{1,0:T(8,128)S(1)}, u32[]{:S(2)}, u32[]{:S(2)}) collective-permute-start(f32[16,256]{1,0:T(8,128)S(1)} %get-tuple-element.30.refs_1_), channel_id=1, source_target_pairs={{0,2},{1,3},{2,0},{3,1},{4,6},{5,7},{6,4},{7,5},{8,10},{9,11},{10,... | collective-permute-start | bytes 49160 | tf_op jit(solution)/shard_map/ppermute | solution.py:286
  8.5 1.0 %copy-start = (bf16[1,2,2,176,256]{4,3,2,1,0:T(8,128)(2,1)S(1)}, bf16[1,2,2,176,256]{4,3,2,1,0:T(8,128)(2,1)}, u32[]{:S(2)}) copy-start(bf16[1,2,2,176,256]{4,3,2,1,0:T(8,128)(2,1)} %param.11) | copy-start | bytes 1081348
  11.6 2.5 %collective-permute-start.4 = (bf16[400,256]{1,0:T(8,128)(2,1)S(1)}, bf16[400,256]{1,0:T(8,128)(2,1)S(1)}, u32[]{:S(2)}, u32[]{:S(2)}) collective-permute-start(bf16[400,256]{1,0:T(8,128)(2,1)S(1)} %collective-permute-done.1.refs_6_), channel_id=1, source_target_pairs={{0,4},{4,0},{1,5},{5,1},{2,6},{6,2},{3,7},{7,3},{8,12},{12,8},{9,1... | collective-permute-start | bytes 614408 | tf_op jit(solution)/shard_map/ppermute | solution.py:300
  11.9 11.0 %collective-permute-start.12 = (bf16[352,256]{1,0:T(8,128)(2,1)S(1)}, bf16[352,256]{1,0:T(8,128)(2,1)S(1)}, u32[]{:S(2)}, u32[]{:S(2)}) collective-permute-start(bf16[352,256]{1,0:T(8,128)(2,1)S(1)} %get-tuple-element.44), channel_id=1, source_target_pairs={{0,1},{1,0},{2,3},{3,2},{4,7},{5,6},{6,5},{7,4},{8,9},{9,8},{10,11... | collective-permute-start | bytes 540680 | tf_op jit(solution)/shard_map/ppermute | solution.py:298
  16.4 7.4 %collective-permute-start.10 = (bf16[144,256]{1,0:T(8,128)(2,1)S(1)}, bf16[144,256]{1,0:T(8,128)(2,1)S(1)}, u32[]{:S(2)}, u32[]{:S(2)}) collective-permute-start(bf16[144,256]{1,0:T(8,128)(2,1)S(1)} %get-tuple-element.42), channel_id=1, source_target_pairs={{0,3},{1,2},{2,1},{3,0},{8,11},{9,10},{10,9},{11,8},{16,19},{17,18... | collective-permute-start | bytes 221192 | tf_op jit(solution)/shard_map/ppermute | solution.py:337
  18.4 7.0 %collective-permute-start.11 = (bf16[144,256]{1,0:T(8,128)(2,1)S(1)}, bf16[144,256]{1,0:T(8,128)(2,1)S(1)}, u32[]{:S(2)}, u32[]{:S(2)}) collective-permute-start(bf16[144,256]{1,0:T(8,128)(2,1)S(1)} %get-tuple-element.43), channel_id=1, source_target_pairs={{0,1},{1,0},{2,3},{3,2},{8,9},{9,8},{10,11},{11,10},{16,17},{17,16... | collective-permute-start | bytes 221192 | tf_op jit(solution)/shard_map/ppermute | solution.py:337
  19.3 6.5 %collective-permute-start.5 = (bf16[144,256]{1,0:T(8,128)(2,1)S(1)}, bf16[144,256]{1,0:T(8,128)(2,1)S(1)}, u32[]{:S(2)}, u32[]{:S(2)}) collective-permute-start(bf16[144,256]{1,0:T(8,128)(2,1)S(1)} %get-tuple-element.37), channel_id=1, source_target_pairs={{0,2},{1,3},{2,0},{3,1},{8,10},{9,11},{10,8},{11,9},{16,18},{17,19... | collective-permute-start | bytes 221192 | tf_op jit(solution)/shard_map/ppermute | solution.py:337
  19.9 6.5 %collective-permute-start.6 = (bf16[144,256]{1,0:T(8,128)(2,1)S(1)}, bf16[144,256]{1,0:T(8,128)(2,1)S(1)}, u32[]{:S(2)}, u32[]{:S(2)}) collective-permute-start(bf16[144,256]{1,0:T(8,128)(2,1)S(1)} %get-tuple-element.38), channel_id=1, source_target_pairs={{0,11},{1,10},{2,9},{3,8},{8,3},{9,2},{10,1},{11,0},{16,27},{17,26... | collective-permute-start | bytes 221192 | tf_op jit(solution)/shard_map/ppermute | solution.py:337
  22.9 6.1 %collective-permute-start.7 = (bf16[144,256]{1,0:T(8,128)(2,1)S(1)}, bf16[144,256]{1,0:T(8,128)(2,1)S(1)}, u32[]{:S(2)}, u32[]{:S(2)}) collective-permute-start(bf16[144,256]{1,0:T(8,128)(2,1)S(1)} %get-tuple-element.39), channel_id=1, source_target_pairs={{0,10},{1,11},{2,8},{3,9},{8,2},{9,3},{10,0},{11,1},{16,26},{17,27... | collective-permute-start | bytes 221192 | tf_op jit(solution)/shard_map/ppermute | solution.py:337
  23.8 5.9 %collective-permute-start.8 = (bf16[144,256]{1,0:T(8,128)(2,1)S(1)}, bf16[144,256]{1,0:T(8,128)(2,1)S(1)}, u32[]{:S(2)}, u32[]{:S(2)}) collective-permute-start(bf16[144,256]{1,0:T(8,128)(2,1)S(1)} %get-tuple-element.40), channel_id=1, source_target_pairs={{0,8},{1,9},{2,10},{3,11},{8,0},{9,1},{10,2},{11,3},{16,24},{17,25... | collective-permute-start | bytes 221192 | tf_op jit(solution)/shard_map/ppermute | solution.py:337
  25.3 5.4 %collective-permute-start.9 = (bf16[144,256]{1,0:T(8,128)(2,1)S(1)}, bf16[144,256]{1,0:T(8,128)(2,1)S(1)}, u32[]{:S(2)}, u32[]{:S(2)}) collective-permute-start(bf16[144,256]{1,0:T(8,128)(2,1)S(1)} %get-tuple-element.41), channel_id=1, source_target_pairs={{0,9},{1,8},{2,11},{3,10},{8,1},{9,0},{10,3},{11,2},{16,25},{17,24... | collective-permute-start | bytes 221192 | tf_op jit(solution)/shard_map/ppermute | solution.py:337
  25.8 5.1 %collective-permute-start.13 = (bf16[352,256]{1,0:T(8,128)(2,1)S(1)}, bf16[352,256]{1,0:T(8,128)(2,1)S(1)}, u32[]{:S(2)}, u32[]{:S(2)}) collective-permute-start(bf16[352,256]{1,0:T(8,128)(2,1)S(1)} %collective-permute-done.12.near_ref), channel_id=1, source_target_pairs={{0,4},{4,0},{1,5},{5,1},{2,6},{6,2},{3,7},{7,3},{8,12},{12,8},{9,1... | collective-permute-start | bytes 540680 | tf_op jit(solution)/shard_map/ppermute | solution.py:301
  30.9 10.1 %collective-permute-start.14 = (bf16[144,256]{1,0:T(8,128)(2,1)S(1)}, bf16[144,256]{1,0:T(8,128)(2,1)S(1)}, u32[]{:S(2)}, u32[]{:S(2)}) collective-permute-start(bf16[144,256]{1,0:T(8,128)(2,1)S(1)} %add_convert_fusion), channel_id=1, source_target_pairs={{0,8},{8,0},{16,24},{24,16},{1,9},{9,1},{17,25},{25,17},{2,10},{10... | collective-permute-start | bytes 221192 | tf_op jit(solution)/shard_map/ppermute | solution.py:348
  31.8 9.2 %collective-permute-start.15 = (bf16[144,256]{1,0:T(8,128)(2,1)S(1)}, bf16[144,256]{1,0:T(8,128)(2,1)S(1)}, u32[]{:S(2)}, u32[]{:S(2)}) collective-permute-start(bf16[144,256]{1,0:T(8,128)(2,1)S(1)} %add_convert_fusion), channel_id=1, source_target_pairs={{0,16},{8,24},{16,0},{24,8},{1,17},{9,25},{17,1},{25,9},{2,18},{10... | collective-permute-start | bytes 221192 | tf_op jit(solution)/shard_map/ppermute | solution.py:348
  34.4 6.6 %collective-permute-start.16 = (bf16[144,256]{1,0:T(8,128)(2,1)S(1)}, bf16[144,256]{1,0:T(8,128)(2,1)S(1)}, u32[]{:S(2)}, u32[]{:S(2)}) collective-permute-start(bf16[144,256]{1,0:T(8,128)(2,1)S(1)} %add_convert_fusion), channel_id=1, source_target_pairs={{0,24},{8,16},{16,8},{24,0},{1,25},{9,17},{17,9},{25,1},{2,26},{10... | collective-permute-start | bytes 221192 | tf_op jit(solution)/shard_map/ppermute | solution.py:348

commit v3 on v2

--- a/solution.py
+++ b/solution.py
@@ -110,20 +110,18 @@
 def grad_kernel(count, decode, n_stats, n_pieces, rows_out, *refs):
     where_ref = refs[0]
     stats = refs[1 : 1 + n_stats]
-    params_ref, own_ref, other_ref, near_ref, far_ref, cots_ref = refs[1 + n_stats : 7 + n_stats]
+    params_ref, own_ref, other_ref, near_ref, far_sums_ref, cots_ref = refs[1 + n_stats : 7 + n_stats]
     act_ref, norm_ref = refs[7 + n_stats : 9 + n_stats]
     pieces = refs[9 + n_stats : 9 + n_stats + n_pieces]
     wg_ref = refs[9 + n_stats + n_pieces]
     late = where_ref[0]
     is_late = late == 1
-    low_is_near = where_ref[4] == 1
     frames, height, width, chans = own_ref.shape
     sums = stats[0][...]
     for ref in stats[1:]:
         sums = sums + ref[...]
     if decode:
-        for ref in (near_ref, far_ref):
-            base = frames * width
+        for ref, base in ((near_ref, frames * width), (far_sums_ref, 0)):
             terms = [ref[base + 16 * k : base + 16 * (k + 1), :].astype(F32) for k in range(3)]
             sums = sums + (terms[0] + (terms[1] + terms[2]))
     total = jnp.sum(sums[0:8], axis=0, keepdims=True)
@@ -136,18 +134,14 @@
     norm_ref[0:1, :] = scale
     norm_ref[1:2, :] = shift
     norm_ref[2:8, :] = jnp.zeros((6, chans), F32)
-    keep_low = (where_ref[1] != 0).astype(F32)
-    keep_high = (where_ref[2] != 0).astype(F32)
+    keep = (where_ref[1] != 0).astype(F32)
     for f in range(frames):
         near = near_ref[f * width : (f + 1) * width, :]
-        far = far_ref[f * width : (f + 1) * width, :]
-        low = jnp.where(low_is_near, near, far)
-        act_ref[f, 0] = (activate(low, scale, shift) * keep_low).astype(BF16)
+        act_ref[f, late * (height + 1)] = (activate(near, scale, shift) * keep).astype(BF16)
+        act_ref[f, (1 - late) * (height + 1)] = jnp.zeros((width, chans), BF16)
         for h in range(height):
             x = jnp.where(is_late, other_ref[f, h], own_ref[f, h])
             act_ref[f, h + 1] = activate(x, scale, shift).astype(BF16)
-        high = jnp.where(low_is_near, far, near)
-        act_ref[f, height + 1] = (activate(high, scale, shift) * keep_high).astype(BF16)
 
     contract = (((0,), (0,)), ((), ()))
     terms = 3 * height * width
@@ -174,59 +168,64 @@
     base = pl.multiple_of((1 - late) * (4 * chans), half)
     wg_ref[pl.ds(base, half), :] = lax.dot_general(lanes, cots(1), contract, preferred_element_type=F32)
     for k, ref in enumerate(pieces):
-        start = pl.multiple_of(where_ref[5 + k], 16)
+        start = pl.multiple_of(where_ref[4 + k], 16)
         ref[...] = wg_ref[pl.ds(start, rows_out), :].astype(ref.dtype)
 
 
-def conv_kernel(where_ref, norm_ref, act_ref, own_ref, near_ref, far_ref, weight_hbm, params_ref, out_ref, planes, acc, weight_ref, sems):
-    copies = [pltpu.make_async_copy(weight_hbm.at[:, :, kw], weight_ref.at[:, :, kw], sems.at[kw]) for kw in range(3)]
+def conv_kernel(
+    where_ref, norm_ref, act_ref, own_ref, far_ref, near_late, far_late, weight_hbm, params_ref, out_ref, planes, acc, weight_ref, sems
+):
+    taps = [(kt, kh) for kt in range(3) for kh in range(3)]
+    copies = [
+        pltpu.make_async_copy(weight_hbm.at[kt, kh], weight_ref.at[kt, kh], sems.at[k]) for k, (kt, kh) in enumerate(taps)
+    ]
     for c in copies:
         c.start()
     late = where_ref[0]
-    low_is_near = where_ref[4] == 1
     frames, height, width, chans = own_ref.shape
-    planes[0] = act_ref[0]
-    planes[1] = act_ref[late]
+    scale = norm_ref[0:1, :]
+    shift = norm_ref[1:2, :]
+    keep_near = (where_ref[1] != 0).astype(F32)
+    keep_far = (where_ref[2] != 0).astype(F32)
+
+    def rim(ref, f, keep):
+        return (activate(ref[f * width : (f + 1) * width, :], scale, shift) * keep).astype(BF16)
 
     @pl.when(late == 0)
     def _():
-        planes[2] = act_ref[0]
-        planes[3] = act_ref[1]
+        for f in range(frames):
+            planes[2 + f] = act_ref[f]
+            planes[2 + f, height + 1] = rim(far_ref, f, keep_far)
+        for k in range(2):
+            planes[k] = planes[2]
 
     @pl.when(late == 1)
     def _():
-        scale = norm_ref[0:1, :]
-        shift = norm_ref[1:2, :]
-        keep_low = (where_ref[1] != 0).astype(F32)
-        keep_high = (where_ref[2] != 0).astype(F32)
         for f in range(frames):
-            near = near_ref[f * width : (f + 1) * width, :]
-            far = far_ref[f * width : (f + 1) * width, :]
-            low = jnp.where(low_is_near, near, far)
-            high = jnp.where(low_is_near, far, near)
-            planes[frames + f, 0] = (activate(low, scale, shift) * keep_low).astype(BF16)
+            planes[f] = act_ref[f]
+            planes[f, 0] = rim(far_ref, f, keep_far)
+            planes[2 + f, 0] = rim(far_late, f, keep_far)
             for h in range(height):
-                planes[frames + f, h + 1] = activate(own_ref[f, h], scale, shift).astype(BF16)
-            planes[frames + f, height + 1] = (activate(high, scale, shift) * keep_high).astype(BF16)
-
-    for kw in range(3):
-        copies[kw].wait()
+                planes[2 + f, h + 1] = activate(own_ref[f, h], scale, shift).astype(BF16)
+            planes[2 + f, height + 1] = rim(near_late, f, keep_near)
+
+    for kt in range(3):
+        for c in copies[3 * kt : 3 * kt + 3]:
+            c.wait()
         for f in range(frames):
-            total = None
-            for kt in range(3):
+            for kw in range(3):
+                total = None
                 for kh in range(3):
                     lhs = planes[f + kt, kh : kh + height].reshape(height * width, chans)
                     part = jnp.dot(lhs, weight_ref[kt, kh, kw], preferred_element_type=F32)
                     total = part if total is None else total + part
-            total = total.reshape(height, width, chans)
-            for h in range(height):
-                if kw == 0:
-                    acc[f, h] = shift_rows(total[h], -1)
-                elif kw == 1:
-                    acc[f, h] = acc[f, h] + total[h]
-                else:
-                    value = own_ref[f, h].astype(F32) + params_ref[2:3, :] + acc[f, h] + shift_rows(total[h], 1)
-                    out_ref[f, h] = value.astype(BF16)
+                total = total.reshape(height, width, chans)
+                acc[f, kw] = total if kt == 0 else acc[f, kw] + total
+    for f in range(frames):
+        for h in range(height):
+            value = own_ref[f, h].astype(F32) + params_ref[2:3, :]
+            value = value + acc[f, 1, h] + shift_rows(acc[f, 0, h], -1) + shift_rows(acc[f, 2, h], 1)
+            out_ref[f, h] = value.astype(BF16)
 
 
 def body(dp, rows, latent, gamma, beta, weight, bias, cotangent):
@@ -241,12 +240,14 @@
     size = frames * height * width * chans
     small = rows == 4 and dp == 4
 
-    odd = band % 2
-    beyond = [(r - 1) % rows if r % 2 == 0 else (r + 1) % rows for r in range(rows)]
-    joint = [(r, r ^ 1) for r in range(rows)] + [(rows + r, rows + beyond[r]) for r in range(rows)]
-    low_is_near = (odd ^ late) if rows > 1 else late
-    edge_row = jnp.where(low_is_near == 1, 0, height - 1)
-    head = [late, (band != 0), (band != rows - 1), edge_row, low_is_near]
+    joint = [(r, (r + 1) % rows) for r in range(rows)] + [(rows + r, rows + (r - 1) % rows) for r in range(rows)]
+    keep_low, keep_high = (band != 0), (band != rows - 1)
+    head = [
+        late,
+        jnp.where(late == 0, keep_low, keep_high),
+        jnp.where(late == 0, keep_high, keep_low),
+        jnp.where(late == 0, height - 1, 0),
+    ]
 
     other = lax.ppermute(lat, "tm", swap)
     other_cot = lax.ppermute(cot, "tm", swap)
@@ -283,7 +284,10 @@
     )
     near = lax.ppermute(early_rims, ("tm", "rows"), joint)
     if small:
-        stats = [sums, lax.ppermute(sums, "rows", [(r, r ^ 2) for r in range(rows)])]
+        stats = [
+            sums,
+            lax.ppermute(sums, "rows", [(r, (r + 2) % rows) for r in range(rows)]),
+        ]
     else:
         stats = [lax.psum(sums, "rows")]
     params = jnp.stack([gamma, beta, bias] + [jnp.zeros_like(bias)] * 5)
@@ -295,10 +299,10 @@
         nbytes=14 * size,
         name="cots",
     )
+    cots, params, late_rims, stats[-1] = lax.optimization_barrier((cots, params, late_rims, stats[-1]))
     near_late = lax.ppermute(late_rims, ("tm", "rows"), joint)
-    near, cots, params, stats[-1] = lax.optimization_barrier((near, cots, params, stats[-1]))
-    far = lax.ppermute(near, "tm", swap)
-    far_late = lax.ppermute(near_late, "tm", swap)
+    near, stats[-1], cots = lax.optimization_barrier((near, stats[-1], cots))
+    far_sums = lax.ppermute(near[frames * width :], "tm", swap)
     act, norm, *parts = call(
         functools.partial(grad_kernel, count, small, len(stats), len(kinds), piece),
         [
@@ -306,29 +310,29 @@
             jax.ShapeDtypeStruct((8, chans), F32),
         ]
         + [jax.ShapeDtypeStruct((piece, chans), k) for k in kinds],
-        (where, *stats, params, lat, other, near, far, cots),
+        (where, *stats, params, lat, other, near, far_sums, cots),
         scratch=[pltpu.VMEM((half, chans), F32)],
         flops=2 * half * 3 * height * width * chans,
         nbytes=20 * size,
         trans=2 * size,
         name="grad",
     )
-    def convolve():
+    def convolve(far, near_late, far_late):
         return call(
             conv_kernel,
             jax.ShapeDtypeStruct((frames, height, width, chans), BF16),
-            (where, norm, act, lat, near_late, far_late, weight, params),
+            (where, norm, act, lat, far, near_late, far_late, weight, params),
             scratch=[
                 pltpu.VMEM((4, height + 2, width, chans), BF16),
-                pltpu.VMEM((frames, height, width, chans), F32),
+                pltpu.VMEM((frames, 3, height, width, chans), F32),
                 pltpu.VMEM(weight.shape, weight.dtype),
-                pltpu.SemaphoreType.DMA((3,)),
+                pltpu.SemaphoreType.DMA((9,)),
             ],
             flops=2 * 27 * size * chans,
             nbytes=4 * size + 2 * weight.size,
             trans=2 * size,
             name="conv",
-            outside=(6,),
+            outside=(7,),
             limit=51 * 1024 * 1024,
         )
 
@@ -341,12 +345,14 @@
             )
             for p, (dz, dr) in zip(parts[1:], order[1:])
         ]
-        total = parts[0]
+        near, near_late, total = lax.optimization_barrier((near, near_late, parts[0]))
+        far = lax.ppermute(near, "tm", swap)
+        far_late = lax.ppermute(near_late, "tm", swap)
         for g in got:
             total = total + g.astype(F32)
-        total, far_late = lax.optimization_barrier((total.astype(BF16), far_late))
+        total, far, far_late = lax.optimization_barrier((total.astype(BF16), far, far_late))
         by = [total] + [lax.ppermute(total, "dp", [(z, z ^ k) for z in range(4)]) for k in (1, 2, 3)]
-        output = convolve()
+        output = convolve(far, near_late, far_late)
         *by, output = lax.optimization_barrier((*by, output))
         by = [b.astype(F32) for b in by]
         mine = by[0] + by[2]
@@ -354,7 +360,8 @@
         even = clip % 2 == 0
         grad = jnp.concatenate([jnp.where(even, mine, theirs), jnp.where(even, theirs, mine)], axis=0)
     else:
-        output = convolve()
+        far = lax.ppermute(near, "tm", swap)
+        output = convolve(far, near_late, lax.ppermute(near_late, "tm", swap))
         grad = lax.psum(lax.psum_scatter(parts[0], "rows", scatter_dimension=0, tiled=True), "dp")
     return output[None], grad
 

time: 42 us -> 40.9 us (0.974)
  starting transfers between devices: 21.4 us -> 20.1 us
  waiting for transfers between devices: 6.46 us -> 6.92 us
    ppermute x1 -> x2, waiting for transfers between devices: 0.01 us -> 1.2 us  [the longest x1 1.19 us: body(): far_sums = lax.ppermute(near[frames * width:], 'tm', swap)]
    ppermute x1, starting transfers between devices: 2.19 us -> 1.24 us  [body(): near_late = lax.ppermute(late_rims, ('tm', 'rows'), joint)]
    ppermute x7, waiting for transfers between devices: 4.97 us -> 4.24 us  [body(): lax.ppermute(p, ('dp', 'rows'), [(z * 4 + r, (z ^ dz) * 4 + (r ^ dr)) for...]
    ppermute x1 -> x2, starting transfers between devices: 1.52 us -> 1.52 us  [the longest x1 1.52 us: body(): lax.ppermute(sums, 'rows', [(r, (r + 2) % rows) for r in range(rows)])]
  transfers between devices with their start and end apart: 17 -> 18, of which waited for: 6 -> 8; matrix products, arithmetic and copies ran while one was open for 2% -> 2% of each run, Pallas kernels for 23% -> 23%
where the time goes in v3:
time: 40.9 us; the launch traced here: 40.7 us
  starting transfers between devices  20.1 us (49%)
  Pallas kernels  9.2 us (22%)
  waiting for transfers between devices  6.92 us (17%)
  local copies, waits for them, and re-layouts  2.78 us (7%)
  other arithmetic  0.87 us (2%)
  between operations  0.76 us (2%)
    ppermute x7, starting transfers between devices, body(): lax.ppermute(p, ('dp', 'rows'), [(z * 4 + r, (z ^ dz) * 4 + (r ^ dr)) for...  9.4 us
    pallas_call x5, Pallas kernels, call(): pl.pallas_call(kernel, out_shape=outs, in_specs=specs, out_specs=jax.tree...  9.2 us
    ppermute x3, starting transfers between devices, body(): lax.ppermute(total, 'dp', [(z, z ^ k) for z in range(4)])  4.45 us
    ppermute x7, waiting for transfers between devices, body(): lax.ppermute(p, ('dp', 'rows'), [(z * 4 + r, (z ^ dz) * 4 + (r ^ dr)) for...  4.24 us
    ppermute x1, starting transfers between devices, body(): near = lax.ppermute(early_rims, ('tm', 'rows'), joint)  2.91 us
    unnamed x4, local copies, waits for them, and re-layouts  1.96 us
    ppermute x1, starting transfers between devices, body(): lax.ppermute(sums, 'rows', [(r, (r + 2) % rows) for r in range(rows)])  1.52 us
    ppermute x1, starting transfers between devices, body(): near_late = lax.ppermute(late_rims, ('tm', 'rows'), joint)  1.24 us
  transfers between devices with their start and end apart: 18, of which 8 were waited for; matrix products, arithmetic and copies ran while one was open for 2% of the time, Pallas kernels for 23%

profile of v3, /device:TPU:0, one launch (start us, length us, event | category | flops | bytes accessed | tf_op | source)
XLA Modules:
  0.0 40.7 jit_solution(18117201390470337389)
XLA Ops:
  1.3 1.0 %copy-done.1 = bf16[1,2,2,176,256]{4,3,2,1,0:T(8,128)(2,1)S(1)} copy-done((bf16[1,2,2,176,256]{4,3,2,1,0:T(8,128)(2,1)S(1)}, bf16[1,2,2,176,256]{4,3,2,1,0:T(8,128)(2,1)}, u32[]{:S(2)}) %copy-start.1) | copy-done | bytes 360472
  2.7 0.6 %prep.1 = (f32[16,256]{1,0:T(8,128)S(1)}, bf16[400,256]{1,0:T(8,128)(2,1)S(1)}, bf16[352,256]{1,0:T(8,128)(2,1)S(1)}) custom-call(s32[12]{0:T(128)S(1)} %stack.74.where_ref.refs_0_, f32[16,256]{1,0:T(8,128)S(1)} %get-tuple-element.35.own_sums_ref, bf16[2,2,176,256]{3,2,1,0:T(8,128)(2,1)S(1)} %get-tuple-element.36.own_ref.refs_4_, ...), custom_call_target="tpu_custom_call" | custom-call | flops 540672 | bytes 1081344 | tf_op jit(solution)/shard_map/prep/pallas_call | solution.py:21
  3.3 2.9 %collective-permute-start.1 = (bf16[400,256]{1,0:T(8,128)(2,1)S(1)}, bf16[400,256]{1,0:T(8,128)(2,1)S(1)}, u32[]{:S(2)}, u32[]{:S(2)}) collective-permute-start(bf16[400,256]{1,0:T(8,128)(2,1)S(1)} %get-tuple-element.37), channel_id=1, source_target_pairs={{0,1},{1,2},{2,3},{3,0},{4,7},{5,4},{6,5},{7,6},{8,9},{9,10},{10,1... | collective-permute-start | bytes 614408 | tf_op jit(solution)/shard_map/ppermute | solution.py:285
  6.2 1.5 %collective-permute-start.3 = (f32[16,256]{1,0:T(8,128)S(1)}, f32[16,256]{1,0:T(8,128)S(1)}, u32[]{:S(2)}, u32[]{:S(2)}) collective-permute-start(f32[16,256]{1,0:T(8,128)S(1)} %get-tuple-element.39.refs_1_), channel_id=1, source_target_pairs={{0,2},{1,3},{2,0},{3,1},{4,6},{5,7},{6,4},{7,5},{8,10},{9,11},{10,... | collective-permute-start | bytes 49160 | tf_op jit(solution)/shard_map/ppermute | solution.py:289
  7.7 0.7 %stack.79.refs_3_.params_ref = f32[8,256]{1,0:T(8,128)S(1)} concatenate(f32[1,256]{1,0:T(1,128)} %bitcast.22, f32[1,256]{1,0:T(1,128)} %bitcast.23, f32[1,256]{1,0:T(1,128)} %bitcast.24, f32[1,256]{1,0:T(1,128)S(1)} %stack_broadcast_in_dim.3, f32[4,256]{1,0:T(4,128)S(1)} %stack.78), dimensions={0} | concatenate | bytes 16384 | tf_op jit(solution)/shard_map/stack | solution.py:293
  8.5 1.0 %copy-done = bf16[1,2,2,176,256]{4,3,2,1,0:T(8,128)(2,1)S(1)} copy-done((bf16[1,2,2,176,256]{4,3,2,1,0:T(8,128)(2,1)S(1)}, bf16[1,2,2,176,256]{4,3,2,1,0:T(8,128)(2,1)}, u32[]{:S(2)}) %copy-start) | copy-done | bytes 360472
  9.5 0.9 %cots.1.refs_8_ = bf16[3,3,2,176,256]{4,3,2,1,0:T(8,128)(2,1)S(1)} custom-call(s32[12]{0:T(128)S(1)} %stack.74.where_ref.refs_0_, bf16[2,2,176,256]{3,2,1,0:T(8,128)(2,1)S(1)} %bitcast.19, bf16[2,2,176,256]{3,2,1,0:T(8,128)(2,1)S(1)} %collective-permute-done.2.other_ref), custom_call_target="tpu_custom_call" | custom-call | flops 1802240 | bytes 2523136 | tf_op jit(solution)/shard_map/cots/pallas_call | solution.py:21
  10.4 1.2 %collective-permute-start.4 = (bf16[352,256]{1,0:T(8,128)(2,1)S(1)}, bf16[352,256]{1,0:T(8,128)(2,1)S(1)}, u32[]{:S(2)}, u32[]{:S(2)}) collective-permute-start(bf16[352,256]{1,0:T(8,128)(2,1)S(1)} %get-tuple-element.43), channel_id=1, source_target_pairs={{0,1},{1,2},{2,3},{3,0},{4,7},{5,4},{6,5},{7,6},{8,9},{9,10},{10,1... | collective-permute-start | bytes 540680 | tf_op jit(solution)/shard_map/ppermute | solution.py:303
  11.6 1.2 %collective-permute-done.1.refs_6_ = bf16[400,256]{1,0:T(8,128)(2,1)S(1)} collective-permute-done((bf16[400,256]{1,0:T(8,128)(2,1)S(1)}, bf16[400,256]{1,0:T(8,128)(2,1)S(1)}, u32[]{:S(2)}, u32[]{:S(2)}) %collective-permute-start.1) | collective-permute-done | bytes 204832 | tf_op jit(solution)/shard_map/ppermute | solution.py:285
  12.8 1.2 %collective-permute-done.5.refs_7_ = bf16[48,256]{1,0:T(8,128)(2,1)S(1)} collective-permute-done((bf16[48,256]{1,0:T(8,128)(2,1)S(1)}, bf16[48,256]{1,0:T(8,128)(2,1)S(1)}, u32[]{:S(2)}, u32[]{:S(2)}) %collective-permute-start.5) | collective-permute-done | bytes 24608 | tf_op jit(solution)/shard_map/ppermute | solution.py:305
  14.0 2.2 %grad.1 = (bf16[2,4,176,256]{3,2,1,0:T(8,128)(2,1)S(1)}, f32[8,256]{1,0:T(8,128)S(1)}, f32[144,256]{1,0:T(8,128)S(1)}, bf16[144,256]{1,0:T(8,128)(2,1)S(1)}, bf1...) custom-call(s32[12]{0:T(128)S(1)} %stack.74.where_ref.refs_0_, ...), custom_call_target="tpu_custom_call" | custom-call | flops 622854144 | bytes 3604480 | tf_op jit(solution)/shard_map/grad/pallas_call | solution.py:21
  16.2 0.6 %collective-permute-start.6 = (bf16[144,256]{1,0:T(8,128)(2,1)S(1)}, bf16[144,256]{1,0:T(8,128)(2,1)S(1)}, u32[]{:S(2)}, u32[]{:S(2)}) collective-permute-start(bf16[144,256]{1,0:T(8,128)(2,1)S(1)} %get-tuple-element.49), channel_id=1, source_target_pairs={{0,2},{1,3},{2,0},{3,1},{8,10},{9,11},{10,8},{11,9},{16,18},{17,19... | collective-permute-start | bytes 221192 | tf_op jit(solution)/shard_map/ppermute | solution.py:341
  16.7 3.2 %collective-permute-start.7 = (bf16[144,256]{1,0:T(8,128)(2,1)S(1)}, bf16[144,256]{1,0:T(8,128)(2,1)S(1)}, u32[]{:S(2)}, u32[]{:S(2)}) collective-permute-start(bf16[144,256]{1,0:T(8,128)(2,1)S(1)} %get-tuple-element.50), channel_id=1, source_target_pairs={{0,11},{1,10},{2,9},{3,8},{8,3},{9,2},{10,1},{11,0},{16,27},{17,26... | collective-permute-start | bytes 221192 | tf_op jit(solution)/shard_map/ppermute | solution.py:341
  20.0 0.9 %collective-permute-start.8 = (bf16[144,256]{1,0:T(8,128)(2,1)S(1)}, bf16[144,256]{1,0:T(8,128)(2,1)S(1)}, u32[]{:S(2)}, u32[]{:S(2)}) collective-permute-start(bf16[144,256]{1,0:T(8,128)(2,1)S(1)} %get-tuple-element.51), channel_id=1, source_target_pairs={{0,10},{1,11},{2,8},{3,9},{8,2},{9,3},{10,0},{11,1},{16,26},{17,27... | collective-permute-start | bytes 221192 | tf_op jit(solution)/shard_map/ppermute | solution.py:341
  20.9 1.6 %collective-permute-start.9 = (bf16[144,256]{1,0:T(8,128)(2,1)S(1)}, bf16[144,256]{1,0:T(8,128)(2,1)S(1)}, u32[]{:S(2)}, u32[]{:S(2)}) collective-permute-start(bf16[144,256]{1,0:T(8,128)(2,1)S(1)} %get-tuple-element.52), channel_id=1, source_target_pairs={{0,8},{1,9},{2,10},{3,11},{8,0},{9,1},{10,2},{11,3},{16,24},{17,25... | collective-permute-start | bytes 221192 | tf_op jit(solution)/shard_map/ppermute | solution.py:341
  22.6 2.9 %collective-permute-start.11 = (bf16[144,256]{1,0:T(8,128)(2,1)S(1)}, bf16[144,256]{1,0:T(8,128)(2,1)S(1)}, u32[]{:S(2)}, u32[]{:S(2)}) collective-permute-start(bf16[144,256]{1,0:T(8,128)(2,1)S(1)} %get-tuple-element.54), channel_id=1, source_target_pairs={{0,3},{1,2},{2,1},{3,0},{8,11},{9,10},{10,9},{11,8},{16,19},{17,18... | collective-permute-start | bytes 221192 | tf_op jit(solution)/shard_map/ppermute | solution.py:341
  26.1 1.1 %collective-permute-done.9 = bf16[144,256]{1,0:T(8,128)(2,1)S(1)} collective-permute-done((bf16[144,256]{1,0:T(8,128)(2,1)S(1)}, bf16[144,256]{1,0:T(8,128)(2,1)S(1)}, u32[]{:S(2)}, u32[]{:S(2)}) %collective-permute-start.9) | collective-permute-done | bytes 73760 | tf_op jit(solution)/shard_map/ppermute | solution.py:341
  27.2 0.6 %collective-permute-done.10 = bf16[144,256]{1,0:T(8,128)(2,1)S(1)} collective-permute-done((bf16[144,256]{1,0:T(8,128)(2,1)S(1)}, bf16[144,256]{1,0:T(8,128)(2,1)S(1)}, u32[]{:S(2)}, u32[]{:S(2)}) %collective-permute-start.10) | collective-permute-done | bytes 73760 | tf_op jit(solution)/shard_map/ppermute | solution.py:341
  27.8 1.4 %collective-permute-done.11 = bf16[144,256]{1,0:T(8,128)(2,1)S(1)} collective-permute-done((bf16[144,256]{1,0:T(8,128)(2,1)S(1)}, bf16[144,256]{1,0:T(8,128)(2,1)S(1)}, u32[]{:S(2)}, u32[]{:S(2)}) %collective-permute-start.11) | collective-permute-done | bytes 73760 | tf_op jit(solution)/shard_map/ppermute | solution.py:341
  29.2 0.6 %collective-permute-done.12 = bf16[144,256]{1,0:T(8,128)(2,1)S(1)} collective-permute-done((bf16[144,256]{1,0:T(8,128)(2,1)S(1)}, bf16[144,256]{1,0:T(8,128)(2,1)S(1)}, u32[]{:S(2)}, u32[]{:S(2)}) %collective-permute-start.12) | collective-permute-done | bytes 73760 | tf_op jit(solution)/shard_map/ppermute | solution.py:341
  30.0 3.4 %collective-permute-start.17 = (bf16[144,256]{1,0:T(8,128)(2,1)S(1)}, bf16[144,256]{1,0:T(8,128)(2,1)S(1)}, u32[]{:S(2)}, u32[]{:S(2)}) collective-permute-start(bf16[144,256]{1,0:T(8,128)(2,1)S(1)} %add_convert_fusion), channel_id=1, source_target_pairs={{0,24},{8,16},{16,8},{24,0},{1,25},{9,17},{17,9},{25,1},{2,26},{10... | collective-permute-start | bytes 221192 | tf_op jit(solution)/shard_map/ppermute | solution.py:354
  33.3 1.1 %collective-permute-start.15 = (bf16[144,256]{1,0:T(8,128)(2,1)S(1)}, bf16[144,256]{1,0:T(8,128)(2,1)S(1)}, u32[]{:S(2)}, u32[]{:S(2)}) collective-permute-start(bf16[144,256]{1,0:T(8,128)(2,1)S(1)} %add_convert_fusion), channel_id=1, source_target_pairs={{0,8},{8,0},{16,24},{24,16},{1,9},{9,1},{17,25},{25,17},{2,10},{10... | collective-permute-start | bytes 221192 | tf_op jit(solution)/shard_map/ppermute | solution.py:354
  34.4 5.4 %conv.1 = bf16[2,2,176,256]{3,2,1,0:T(8,128)(2,1)} custom-call(s32[12]{0:T(128)S(1)} %stack.74.where_ref.refs_0_, f32[8,256]{1,0:T(8,128)S(1)} %get-tuple-element.59.norm_ref, bf16[2,4,176,256]{3,2,1,0:T(8,128)(2,1)S(1)} %get-tuple-element.60.act_ref, bf16[2,2,176,256]{3,2,1,0:T(8,128)(2,1)S(1)} %get-tuple-element.36.own_ref.refs_4_, ...), custom_call_target="tpu_custom_call" | custom-call | flops 2491416576 | bytes 4259840 | tf_op jit(solution)/shard_map/conv/pallas_call | solution.py:21
  39.9 0.7 %pad_maximum_fusion = f32[288,256]{1,0:T(8,128)} fusion(f32[144,256]{1,0:T(8,128)S(1)} %get-tuple-element.69, f32[144,256]{1,0:T(8,128)S(1)} %get-tuple-element.68), kind=kLoop, calls=%fused_computation | loop fusion | flops 73728 | bytes 589824 | tf_op jit(solution)/shard_map/concatenate | solution.py:361
  (29 shorter events, 2.0 us)
Async XLA Ops:
  0.6 2.0 %collective-permute-start = (bf16[2,2,176,256]{3,2,1,0:T(8,128)(2,1)}, bf16[2,2,176,256]{3,2,1,0:T(8,128)(2,1)S(1)}, u32[]{:S(2)}, u32[]{:S(2)}) collective-permute-start(bf16[2,2,176,256]{3,2,1,0:T(8,128)(2,1)} %bitcast.20), channel_id=1, source_target_pairs={{0,4},{4,0},{1,5},{5,1},{2,6},{6,2},{3,7},{7,3},{8,12},{12,8},{9,1... | collective-permute-start | bytes 1081352 | tf_op jit(solution)/shard_map/ppermute | solution.py:252
  1.1 7.3 %collective-permute-start.2 = (bf16[2,2,176,256]{3,2,1,0:T(8,128)(2,1)}, bf16[2,2,176,256]{3,2,1,0:T(8,128)(2,1)S(1)}, u32[]{:S(2)}, u32[]{:S(2)}) collective-permute-start(bf16[2,2,176,256]{3,2,1,0:T(8,128)(2,1)} %bitcast.18), channel_id=1, source_target_pairs={{0,4},{4,0},{1,5},{5,1},{2,6},{6,2},{3,7},{7,3},{8,12},{12,8},{9,1... | collective-permute-start | bytes 1081352 | tf_op jit(solution)/shard_map/ppermute | solution.py:253
  1.3 1.0 %copy-start.1 = (bf16[1,2,2,176,256]{4,3,2,1,0:T(8,128)(2,1)S(1)}, bf16[1,2,2,176,256]{4,3,2,1,0:T(8,128)(2,1)}, u32[]{:S(2)}) copy-start(bf16[1,2,2,176,256]{4,3,2,1,0:T(8,128)(2,1)} %param.6) | copy-start | bytes 1081348
  3.3 9.5 %collective-permute-start.1 = (bf16[400,256]{1,0:T(8,128)(2,1)S(1)}, bf16[400,256]{1,0:T(8,128)(2,1)S(1)}, u32[]{:S(2)}, u32[]{:S(2)}) collective-permute-start(bf16[400,256]{1,0:T(8,128)(2,1)S(1)} %get-tuple-element.37), channel_id=1, source_target_pairs={{0,1},{1,2},{2,3},{3,0},{4,7},{5,4},{6,5},{7,6},{8,9},{9,10},{10,1... | collective-permute-start | bytes 614408 | tf_op jit(solution)/shard_map/ppermute | solution.py:285
  6.2 4.2 %collective-permute-start.3 = (f32[16,256]{1,0:T(8,128)S(1)}, f32[16,256]{1,0:T(8,128)S(1)}, u32[]{:S(2)}, u32[]{:S(2)}) collective-permute-start(f32[16,256]{1,0:T(8,128)S(1)} %get-tuple-element.39.refs_1_), channel_id=1, source_target_pairs={{0,2},{1,3},{2,0},{3,1},{4,6},{5,7},{6,4},{7,5},{8,10},{9,11},{10,... | collective-permute-start | bytes 49160 | tf_op jit(solution)/shard_map/ppermute | solution.py:289
  8.5 1.0 %copy-start = (bf16[1,2,2,176,256]{4,3,2,1,0:T(8,128)(2,1)S(1)}, bf16[1,2,2,176,256]{4,3,2,1,0:T(8,128)(2,1)}, u32[]{:S(2)}) copy-start(bf16[1,2,2,176,256]{4,3,2,1,0:T(8,128)(2,1)} %param.11) | copy-start | bytes 1081348
  10.4 12.1 %collective-permute-start.4 = (bf16[352,256]{1,0:T(8,128)(2,1)S(1)}, bf16[352,256]{1,0:T(8,128)(2,1)S(1)}, u32[]{:S(2)}, u32[]{:S(2)}) collective-permute-start(bf16[352,256]{1,0:T(8,128)(2,1)S(1)} %get-tuple-element.43), channel_id=1, source_target_pairs={{0,1},{1,2},{2,3},{3,0},{4,7},{5,4},{6,5},{7,6},{8,9},{9,10},{10,1... | collective-permute-start | bytes 540680 | tf_op jit(solution)/shard_map/ppermute | solution.py:303
  12.8 1.2 %collective-permute-start.5 = (bf16[48,256]{1,0:T(8,128)(2,1)S(1)}, bf16[48,256]{1,0:T(8,128)(2,1)S(1)}, u32[]{:S(2)}, u32[]{:S(2)}) collective-permute-start(bf16[48,256]{1,0:T(8,128)(2,1)S(1)} %slice.3), channel_id=1, source_target_pairs={{0,4},{4,0},{1,5},{5,1},{2,6},{6,2},{3,7},{7,3},{8,12},{12,8},{9,1... | collective-permute-start | bytes 73736 | tf_op jit(solution)/shard_map/ppermute | solution.py:305
  16.2 6.4 %collective-permute-start.6 = (bf16[144,256]{1,0:T(8,128)(2,1)S(1)}, bf16[144,256]{1,0:T(8,128)(2,1)S(1)}, u32[]{:S(2)}, u32[]{:S(2)}) collective-permute-start(bf16[144,256]{1,0:T(8,128)(2,1)S(1)} %get-tuple-element.49), channel_id=1, source_target_pairs={{0,2},{1,3},{2,0},{3,1},{8,10},{9,11},{10,8},{11,9},{16,18},{17,19... | collective-permute-start | bytes 221192 | tf_op jit(solution)/shard_map/ppermute | solution.py:341
  16.7 8.7 %collective-permute-start.7 = (bf16[144,256]{1,0:T(8,128)(2,1)S(1)}, bf16[144,256]{1,0:T(8,128)(2,1)S(1)}, u32[]{:S(2)}, u32[]{:S(2)}) collective-permute-start(bf16[144,256]{1,0:T(8,128)(2,1)S(1)} %get-tuple-element.50), channel_id=1, source_target_pairs={{0,11},{1,10},{2,9},{3,8},{8,3},{9,2},{10,1},{11,0},{16,27},{17,26... | collective-permute-start | bytes 221192 | tf_op jit(solution)/shard_map/ppermute | solution.py:341
  20.0 6.1 %collective-permute-start.8 = (bf16[144,256]{1,0:T(8,128)(2,1)S(1)}, bf16[144,256]{1,0:T(8,128)(2,1)S(1)}, u32[]{:S(2)}, u32[]{:S(2)}) collective-permute-start(bf16[144,256]{1,0:T(8,128)(2,1)S(1)} %get-tuple-element.51), channel_id=1, source_target_pairs={{0,10},{1,11},{2,8},{3,9},{8,2},{9,3},{10,0},{11,1},{16,26},{17,27... | collective-permute-start | bytes 221192 | tf_op jit(solution)/shard_map/ppermute | solution.py:341
  20.9 6.3 %collective-permute-start.9 = (bf16[144,256]{1,0:T(8,128)(2,1)S(1)}, bf16[144,256]{1,0:T(8,128)(2,1)S(1)}, u32[]{:S(2)}, u32[]{:S(2)}) collective-permute-start(bf16[144,256]{1,0:T(8,128)(2,1)S(1)} %get-tuple-element.52), channel_id=1, source_target_pairs={{0,8},{1,9},{2,10},{3,11},{8,0},{9,1},{10,2},{11,3},{16,24},{17,25... | collective-permute-start | bytes 221192 | tf_op jit(solution)/shard_map/ppermute | solution.py:341
  22.5 5.4 %collective-permute-start.10 = (bf16[144,256]{1,0:T(8,128)(2,1)S(1)}, bf16[144,256]{1,0:T(8,128)(2,1)S(1)}, u32[]{:S(2)}, u32[]{:S(2)}) collective-permute-start(bf16[144,256]{1,0:T(8,128)(2,1)S(1)} %get-tuple-element.53), channel_id=1, source_target_pairs={{0,9},{1,8},{2,11},{3,10},{8,1},{9,0},{10,3},{11,2},{16,25},{17,24... | collective-permute-start | bytes 221192 | tf_op jit(solution)/shard_map/ppermute | solution.py:341
  22.6 6.6 %collective-permute-start.11 = (bf16[144,256]{1,0:T(8,128)(2,1)S(1)}, bf16[144,256]{1,0:T(8,128)(2,1)S(1)}, u32[]{:S(2)}, u32[]{:S(2)}) collective-permute-start(bf16[144,256]{1,0:T(8,128)(2,1)S(1)} %get-tuple-element.54), channel_id=1, source_target_pairs={{0,3},{1,2},{2,1},{3,0},{8,11},{9,10},{10,9},{11,8},{16,19},{17,18... | collective-permute-start | bytes 221192 | tf_op jit(solution)/shard_map/ppermute | solution.py:341
  25.5 4.4 %collective-permute-start.12 = (bf16[144,256]{1,0:T(8,128)(2,1)S(1)}, bf16[144,256]{1,0:T(8,128)(2,1)S(1)}, u32[]{:S(2)}, u32[]{:S(2)}) collective-permute-start(bf16[144,256]{1,0:T(8,128)(2,1)S(1)} %get-tuple-element.55), channel_id=1, source_target_pairs={{0,1},{1,0},{2,3},{3,2},{8,9},{9,8},{10,11},{11,10},{16,17},{17,16... | collective-permute-start | bytes 221192 | tf_op jit(solution)/shard_map/ppermute | solution.py:341
  26.1 3.8 %collective-permute-start.14 = (bf16[352,256]{1,0:T(8,128)(2,1)S(1)}, bf16[352,256]{1,0:T(8,128)(2,1)S(1)}, u32[]{:S(2)}, u32[]{:S(2)}) collective-permute-start(bf16[352,256]{1,0:T(8,128)(2,1)S(1)} %collective-permute-done.4.near_late), channel_id=1, source_target_pairs={{0,4},{4,0},{1,5},{5,1},{2,6},{6,2},{3,7},{7,3},{8,12},{12,8},{9,1... | collective-permute-start | bytes 540680 | tf_op jit(solution)/shard_map/ppermute | solution.py:350
  27.2 2.7 %collective-permute-start.13 = (bf16[400,256]{1,0:T(8,128)(2,1)S(1)}, bf16[400,256]{1,0:T(8,128)(2,1)S(1)}, u32[]{:S(2)}, u32[]{:S(2)}) collective-permute-start(bf16[400,256]{1,0:T(8,128)(2,1)S(1)} %collective-permute-done.1.refs_6_), channel_id=1, source_target_pairs={{0,4},{4,0},{1,5},{5,1},{2,6},{6,2},{3,7},{7,3},{8,12},{12,8},{9,1... | collective-permute-start | bytes 614408 | tf_op jit(solution)/shard_map/ppermute | solution.py:349
  30.0 9.9 %collective-permute-start.17 = (bf16[144,256]{1,0:T(8,128)(2,1)S(1)}, bf16[144,256]{1,0:T(8,128)(2,1)S(1)}, u32[]{:S(2)}, u32[]{:S(2)}) collective-permute-start(bf16[144,256]{1,0:T(8,128)(2,1)S(1)} %add_convert_fusion), channel_id=1, source_target_pairs={{0,24},{8,16},{16,8},{24,0},{1,25},{9,17},{17,9},{25,1},{2,26},{10... | collective-permute-start | bytes 221192 | tf_op jit(solution)/shard_map/ppermute | solution.py:354
  33.3 6.5 %collective-permute-start.16 = (bf16[144,256]{1,0:T(8,128)(2,1)S(1)}, bf16[144,256]{1,0:T(8,128)(2,1)S(1)}, u32[]{:S(2)}, u32[]{:S(2)}) collective-permute-start(bf16[144,256]{1,0:T(8,128)(2,1)S(1)} %add_convert_fusion), channel_id=1, source_target_pairs={{0,16},{8,24},{16,0},{24,8},{1,17},{9,25},{17,1},{25,9},{2,18},{10... | collective-permute-start | bytes 221192 | tf_op jit(solution)/shard_map/ppermute | solution.py:354
  33.3 6.5 %collective-permute-start.15 = (bf16[144,256]{1,0:T(8,128)(2,1)S(1)}, bf16[144,256]{1,0:T(8,128)(2,1)S(1)}, u32[]{:S(2)}, u32[]{:S(2)}) collective-permute-start(bf16[144,256]{1,0:T(8,128)(2,1)S(1)} %add_convert_fusion), channel_id=1, source_target_pairs={{0,8},{8,0},{16,24},{24,16},{1,9},{9,1},{17,25},{25,17},{2,10},{10... | collective-permute-start | bytes 221192 | tf_op jit(solution)/shard_map/ppermute | solution.py:354

commit v4 on v3

--- a/solution.py
+++ b/solution.py
@@ -173,11 +173,11 @@
 
 
 def conv_kernel(
-    where_ref, norm_ref, act_ref, own_ref, far_ref, near_late, far_late, weight_hbm, params_ref, out_ref, planes, acc, weight_ref, sems
+    where_ref, norm_ref, act_ref, own_ref, far_ref, near_late, far_late, weight_hbm, params_ref, first_ref, out_ref, planes, acc, weight_ref, sems
 ):
-    taps = [(kt, kh) for kt in range(3) for kh in range(3)]
+    taps = [(0, 2)] + [(kt, kh) for kt in (1, 2) for kh in range(3)]
     copies = [
-        pltpu.make_async_copy(weight_hbm.at[kt, kh], weight_ref.at[kt, kh], sems.at[k]) for k, (kt, kh) in enumerate(taps)
+        pltpu.make_async_copy(weight_hbm.at[kt, kh], weight_ref.at[k], sems.at[k]) for k, (kt, kh) in enumerate(taps)
     ]
     for c in copies:
         c.start()
@@ -209,18 +209,22 @@
                 planes[2 + f, h + 1] = activate(own_ref[f, h], scale, shift).astype(BF16)
             planes[2 + f, height + 1] = rim(near_late, f, keep_near)
 
-    for kt in range(3):
-        for c in copies[3 * kt : 3 * kt + 3]:
-            c.wait()
+    early = first_ref.shape[1]
+    for kt, offsets in ((0, range(early)), (0, range(early, 3)), (1, range(3)), (2, range(3))):
+        first = kt == 0 and offsets[0] == 0
+        if not first:
+            for kh in offsets:
+                copies[3 * kt + kh - early].wait()
         for f in range(frames):
             for kw in range(3):
                 total = None
-                for kh in range(3):
+                for kh in offsets:
                     lhs = planes[f + kt, kh : kh + height].reshape(height * width, chans)
-                    part = jnp.dot(lhs, weight_ref[kt, kh, kw], preferred_element_type=F32)
+                    taps_ref = first_ref.at[0, kh] if first else weight_ref.at[3 * kt + kh - early]
+                    part = jnp.dot(lhs, taps_ref[kw], preferred_element_type=F32)
                     total = part if total is None else total + part
                 total = total.reshape(height, width, chans)
-                acc[f, kw] = total if kt == 0 else acc[f, kw] + total
+                acc[f, kw] = total if first else acc[f, kw] + total
     for f in range(frames):
         for h in range(height):
             value = own_ref[f, h].astype(F32) + params_ref[2:3, :]
@@ -317,23 +321,23 @@
         trans=2 * size,
         name="grad",
     )
-    def convolve(far, near_late, far_late):
+    def convolve(far, near_late, far_late, first):
         return call(
             conv_kernel,
             jax.ShapeDtypeStruct((frames, height, width, chans), BF16),
-            (where, norm, act, lat, far, near_late, far_late, weight, params),
+            (where, norm, act, lat, far, near_late, far_late, weight, params, first),
             scratch=[
                 pltpu.VMEM((4, height + 2, width, chans), BF16),
                 pltpu.VMEM((frames, 3, height, width, chans), F32),
-                pltpu.VMEM(weight.shape, weight.dtype),
-                pltpu.SemaphoreType.DMA((9,)),
+                pltpu.VMEM((7,) + weight.shape[2:], weight.dtype),
+                pltpu.SemaphoreType.DMA((7,)),
             ],
             flops=2 * 27 * size * chans,
             nbytes=4 * size + 2 * weight.size,
             trans=2 * size,
             name="conv",
             outside=(7,),
-            limit=51 * 1024 * 1024,
+            limit=50 * 1024 * 1024,
         )
 
     if small:
@@ -350,9 +354,12 @@
         far_late = lax.ppermute(near_late, "tm", swap)
         for g in got:
             total = total + g.astype(F32)
-        total, far, far_late = lax.optimization_barrier((total.astype(BF16), far, far_late))
-        by = [total] + [lax.ppermute(total, "dp", [(z, z ^ k) for z in range(4)]) for k in (1, 2, 3)]
-        output = convolve(far, near_late, far_late)
+        total = total.astype(BF16)
+        later, far, far_late, first = lax.optimization_barrier((total, far, far_late, weight[:1, :2]))
+        by = [total] + [
+            lax.ppermute(t, "dp", [(z, z ^ k) for z in range(4)]) for k, t in ((1, later), (2, total), (3, total))
+        ]
+        output = convolve(far, near_late, far_late, first)
         *by, output = lax.optimization_barrier((*by, output))
         by = [b.astype(F32) for b in by]
         mine = by[0] + by[2]
@@ -361,7 +368,7 @@
         grad = jnp.concatenate([jnp.where(even, mine, theirs), jnp.where(even, theirs, mine)], axis=0)
     else:
         far = lax.ppermute(near, "tm", swap)
-        output = convolve(far, near_late, lax.ppermute(near_late, "tm", swap))
+        output = convolve(far, near_late, lax.ppermute(near_late, "tm", swap), weight[:1, :2])
         grad = lax.psum(lax.psum_scatter(parts[0], "rows", scatter_dimension=0, tiled=True), "dp")
     return output[None], grad
 

time: 40.9 us -> 39.5 us (0.966)
  waiting for transfers between devices: 6.92 us -> 5.29 us
  local copies, waits for them, and re-layouts: 2.78 us -> 3.97 us
  Pallas kernels: 9.2 us -> 8.51 us
    ppermute x7, waiting for transfers between devices: 4.24 us -> 2.13 us  [body(): lax.ppermute(p, ('dp', 'rows'), [(z * 4 + r, (z ^ dz) * 4 + (r ^ dr)) for...]
    slice x0 -> x1, local copies, waits for them, and re-layouts: none -> 1.18 us  [body(): weight[:1, :2]]
    ppermute x3, starting transfers between devices: 4.45 us -> 3.56 us  [body(): lax.ppermute(t, 'dp', [(z, z ^ k) for z in range(4)])]
    pallas_call x5, Pallas kernels: 9.2 us -> 8.51 us  [call(): pl.pallas_call(kernel, out_shape=outs, in_specs=specs, out_specs=jax.tree...]
    ppermute x1, starting transfers between devices: 0.01 us -> 0.49 us  [body(): far_late = lax.ppermute(near_late, 'tm', swap)]
    ppermute x3, waiting for transfers between devices: 0.01 us -> 0.49 us  [body(): lax.ppermute(t, 'dp', [(z, z ^ k) for z in range(4)])]
  transfers between devices with their start and end apart: 18 -> 18, of which waited for: 8 -> 7; matrix products, arithmetic and copies ran while one was open for 2% -> 5% of each run, Pallas kernels for 23% -> 22%
where the time goes in v4:
time: 39.5 us; the launch traced here: 39.2 us
  starting transfers between devices  19.8 us (50%)
  Pallas kernels  8.51 us (22%)
  waiting for transfers between devices  5.29 us (13%)
  local copies, waits for them, and re-layouts  3.97 us (10%)
  other arithmetic  0.86 us (2%)
  between operations  0.76 us (2%)
    ppermute x7, starting transfers between devices, body(): lax.ppermute(p, ('dp', 'rows'), [(z * 4 + r, (z ^ dz) * 4 + (r ^ dr)) for...  9.4 us
    pallas_call x5, Pallas kernels, call(): pl.pallas_call(kernel, out_shape=outs, in_specs=specs, out_specs=jax.tree...  8.51 us
    ppermute x3, starting transfers between devices, body(): lax.ppermute(t, 'dp', [(z, z ^ k) for z in range(4)])  3.56 us
    ppermute x1, starting transfers between devices, body(): near = lax.ppermute(early_rims, ('tm', 'rows'), joint)  2.91 us
    ppermute x7, waiting for transfers between devices, body(): lax.ppermute(p, ('dp', 'rows'), [(z * 4 + r, (z ^ dz) * 4 + (r ^ dr)) for...  2.13 us
    unnamed x4, local copies, waits for them, and re-layouts  1.96 us
    ppermute x1, starting transfers between devices, body(): lax.ppermute(sums, 'rows', [(r, (r + 2) % rows) for r in range(rows)])  1.52 us
    ppermute x1, starting transfers between devices, body(): near_late = lax.ppermute(late_rims, ('tm', 'rows'), joint)  1.24 us
  transfers between devices with their start and end apart: 18, of which 7 were waited for; matrix products, arithmetic and copies ran while one was open for 5% of the time, Pallas kernels for 22%

profile of v4, /device:TPU:0, one launch (start us, length us, event | category | flops | bytes accessed | tf_op | source)
XLA Modules:
  0.0 39.2 jit_solution(2990641451503508490)
XLA Ops:
  1.3 1.0 %copy-done.1 = bf16[1,2,2,176,256]{4,3,2,1,0:T(8,128)(2,1)S(1)} copy-done((bf16[1,2,2,176,256]{4,3,2,1,0:T(8,128)(2,1)S(1)}, bf16[1,2,2,176,256]{4,3,2,1,0:T(8,128)(2,1)}, u32[]{:S(2)}) %copy-start.1) | copy-done | bytes 360472
  2.7 0.6 %prep.1 = (f32[16,256]{1,0:T(8,128)S(1)}, bf16[400,256]{1,0:T(8,128)(2,1)S(1)}, bf16[352,256]{1,0:T(8,128)(2,1)S(1)}) custom-call(s32[12]{0:T(128)S(1)} %stack.74.where_ref.refs_0_, f32[16,256]{1,0:T(8,128)S(1)} %get-tuple-element.36.own_sums_ref, bf16[2,2,176,256]{3,2,1,0:T(8,128)(2,1)S(1)} %get-tuple-element.37.own_ref.refs_4_, ...), custom_call_target="tpu_custom_call" | custom-call | flops 540672 | bytes 1081344 | tf_op jit(solution)/shard_map/prep/pallas_call | solution.py:21
  3.3 2.9 %collective-permute-start.1 = (bf16[400,256]{1,0:T(8,128)(2,1)S(1)}, bf16[400,256]{1,0:T(8,128)(2,1)S(1)}, u32[]{:S(2)}, u32[]{:S(2)}) collective-permute-start(bf16[400,256]{1,0:T(8,128)(2,1)S(1)} %get-tuple-element.38), channel_id=1, source_target_pairs={{0,1},{1,2},{2,3},{3,0},{4,7},{5,4},{6,5},{7,6},{8,9},{9,10},{10,1... | collective-permute-start | bytes 614408 | tf_op jit(solution)/shard_map/ppermute | solution.py:289
  6.2 1.5 %collective-permute-start.3 = (f32[16,256]{1,0:T(8,128)S(1)}, f32[16,256]{1,0:T(8,128)S(1)}, u32[]{:S(2)}, u32[]{:S(2)}) collective-permute-start(f32[16,256]{1,0:T(8,128)S(1)} %get-tuple-element.40.refs_1_), channel_id=1, source_target_pairs={{0,2},{1,3},{2,0},{3,1},{4,6},{5,7},{6,4},{7,5},{8,10},{9,11},{10,... | collective-permute-start | bytes 49160 | tf_op jit(solution)/shard_map/ppermute | solution.py:293
  7.7 0.7 %stack.79.refs_3_.params_ref = f32[8,256]{1,0:T(8,128)S(1)} concatenate(f32[1,256]{1,0:T(1,128)} %bitcast.22, f32[1,256]{1,0:T(1,128)} %bitcast.23, f32[1,256]{1,0:T(1,128)} %bitcast.24, f32[1,256]{1,0:T(1,128)S(1)} %stack_broadcast_in_dim.3, f32[4,256]{1,0:T(4,128)S(1)} %stack.78), dimensions={0} | concatenate | bytes 16384 | tf_op jit(solution)/shard_map/stack | solution.py:297
  8.5 1.0 %copy-done = bf16[1,2,2,176,256]{4,3,2,1,0:T(8,128)(2,1)S(1)} copy-done((bf16[1,2,2,176,256]{4,3,2,1,0:T(8,128)(2,1)S(1)}, bf16[1,2,2,176,256]{4,3,2,1,0:T(8,128)(2,1)}, u32[]{:S(2)}) %copy-start) | copy-done | bytes 360472
  9.5 0.9 %cots.1.refs_8_ = bf16[3,3,2,176,256]{4,3,2,1,0:T(8,128)(2,1)S(1)} custom-call(s32[12]{0:T(128)S(1)} %stack.74.where_ref.refs_0_, bf16[2,2,176,256]{3,2,1,0:T(8,128)(2,1)S(1)} %bitcast.19, bf16[2,2,176,256]{3,2,1,0:T(8,128)(2,1)S(1)} %collective-permute-done.2.other_ref), custom_call_target="tpu_custom_call" | custom-call | flops 1802240 | bytes 2523136 | tf_op jit(solution)/shard_map/cots/pallas_call | solution.py:21
  10.4 1.2 %collective-permute-start.4 = (bf16[352,256]{1,0:T(8,128)(2,1)S(1)}, bf16[352,256]{1,0:T(8,128)(2,1)S(1)}, u32[]{:S(2)}, u32[]{:S(2)}) collective-permute-start(bf16[352,256]{1,0:T(8,128)(2,1)S(1)} %get-tuple-element.44), channel_id=1, source_target_pairs={{0,1},{1,2},{2,3},{3,0},{4,7},{5,4},{6,5},{7,6},{8,9},{9,10},{10,1... | collective-permute-start | bytes 540680 | tf_op jit(solution)/shard_map/ppermute | solution.py:307
  11.6 1.2 %collective-permute-done.1.refs_6_ = bf16[400,256]{1,0:T(8,128)(2,1)S(1)} collective-permute-done((bf16[400,256]{1,0:T(8,128)(2,1)S(1)}, bf16[400,256]{1,0:T(8,128)(2,1)S(1)}, u32[]{:S(2)}, u32[]{:S(2)}) %collective-permute-start.1) | collective-permute-done | bytes 204832 | tf_op jit(solution)/shard_map/ppermute | solution.py:289
  12.8 1.2 %collective-permute-done.5.refs_7_ = bf16[48,256]{1,0:T(8,128)(2,1)S(1)} collective-permute-done((bf16[48,256]{1,0:T(8,128)(2,1)S(1)}, bf16[48,256]{1,0:T(8,128)(2,1)S(1)}, u32[]{:S(2)}, u32[]{:S(2)}) %collective-permute-start.5) | collective-permute-done | bytes 24608 | tf_op jit(solution)/shard_map/ppermute | solution.py:309
  14.0 2.2 %grad.1 = (bf16[2,4,176,256]{3,2,1,0:T(8,128)(2,1)S(1)}, f32[8,256]{1,0:T(8,128)S(1)}, f32[144,256]{1,0:T(8,128)S(1)}, bf16[144,256]{1,0:T(8,128)(2,1)S(1)}, bf1...) custom-call(s32[12]{0:T(128)S(1)} %stack.74.where_ref.refs_0_, ...), custom_call_target="tpu_custom_call" | custom-call | flops 622854144 | bytes 3604480 | tf_op jit(solution)/shard_map/grad/pallas_call | solution.py:21
  16.2 2.3 %collective-permute-start.10 = (bf16[144,256]{1,0:T(8,128)(2,1)S(1)}, bf16[144,256]{1,0:T(8,128)(2,1)S(1)}, u32[]{:S(2)}, u32[]{:S(2)}) collective-permute-start(bf16[144,256]{1,0:T(8,128)(2,1)S(1)} %get-tuple-element.54), channel_id=1, source_target_pairs={{0,9},{1,8},{2,11},{3,10},{8,1},{9,0},{10,3},{11,2},{16,25},{17,24... | collective-permute-start | bytes 221192 | tf_op jit(solution)/shard_map/ppermute | solution.py:345
  18.5 0.8 %collective-permute-start.11 = (bf16[144,256]{1,0:T(8,128)(2,1)S(1)}, bf16[144,256]{1,0:T(8,128)(2,1)S(1)}, u32[]{:S(2)}, u32[]{:S(2)}) collective-permute-start(bf16[144,256]{1,0:T(8,128)(2,1)S(1)} %get-tuple-element.55), channel_id=1, source_target_pairs={{0,3},{1,2},{2,1},{3,0},{8,11},{9,10},{10,9},{11,8},{16,19},{17,18... | collective-permute-start | bytes 221192 | tf_op jit(solution)/shard_map/ppermute | solution.py:345
  19.3 1.7 %collective-permute-start.12 = (bf16[144,256]{1,0:T(8,128)(2,1)S(1)}, bf16[144,256]{1,0:T(8,128)(2,1)S(1)}, u32[]{:S(2)}, u32[]{:S(2)}) collective-permute-start(bf16[144,256]{1,0:T(8,128)(2,1)S(1)} %get-tuple-element.56), channel_id=1, source_target_pairs={{0,1},{1,0},{2,3},{3,2},{8,9},{9,8},{10,11},{11,10},{16,17},{17,16... | collective-permute-start | bytes 221192 | tf_op jit(solution)/shard_map/ppermute | solution.py:345
  21.0 1.0 %collective-permute-start.6 = (bf16[144,256]{1,0:T(8,128)(2,1)S(1)}, bf16[144,256]{1,0:T(8,128)(2,1)S(1)}, u32[]{:S(2)}, u32[]{:S(2)}) collective-permute-start(bf16[144,256]{1,0:T(8,128)(2,1)S(1)} %get-tuple-element.50), channel_id=1, source_target_pairs={{0,2},{1,3},{2,0},{3,1},{8,10},{9,11},{10,8},{11,9},{16,18},{17,19... | collective-permute-start | bytes 221192 | tf_op jit(solution)/shard_map/ppermute | solution.py:345
  22.0 0.6 %collective-permute-start.7 = (bf16[144,256]{1,0:T(8,128)(2,1)S(1)}, bf16[144,256]{1,0:T(8,128)(2,1)S(1)}, u32[]{:S(2)}, u32[]{:S(2)}) collective-permute-start(bf16[144,256]{1,0:T(8,128)(2,1)S(1)} %get-tuple-element.51), channel_id=1, source_target_pairs={{0,11},{1,10},{2,9},{3,8},{8,3},{9,2},{10,1},{11,0},{16,27},{17,26... | collective-permute-start | bytes 221192 | tf_op jit(solution)/shard_map/ppermute | solution.py:345
  22.6 2.5 %collective-permute-start.8 = (bf16[144,256]{1,0:T(8,128)(2,1)S(1)}, bf16[144,256]{1,0:T(8,128)(2,1)S(1)}, u32[]{:S(2)}, u32[]{:S(2)}) collective-permute-start(bf16[144,256]{1,0:T(8,128)(2,1)S(1)} %get-tuple-element.52), channel_id=1, source_target_pairs={{0,10},{1,11},{2,8},{3,9},{8,2},{9,3},{10,0},{11,1},{16,26},{17,27... | collective-permute-start | bytes 221192 | tf_op jit(solution)/shard_map/ppermute | solution.py:345
  25.6 1.2 %slice.7.first_ref = bf16[1,2,3,256,256]{4,3,2,1,0:T(8,128)(2,1)S(1)} slice(bf16[3,3,3,256,256]{4,3,2,1,0:T(8,128)(2,1)} %weight_hbm.1), slice={[0:1], [0:2], [0:3], [0:256], [0:256]} | slice | bytes 1572864 | tf_op jit(solution)/shard_map/slice | solution.py:358
  27.4 1.2 %collective-permute-done.7 = bf16[144,256]{1,0:T(8,128)(2,1)S(1)} collective-permute-done((bf16[144,256]{1,0:T(8,128)(2,1)S(1)}, bf16[144,256]{1,0:T(8,128)(2,1)S(1)}, u32[]{:S(2)}, u32[]{:S(2)}) %collective-permute-start.7) | collective-permute-done | bytes 73760 | tf_op jit(solution)/shard_map/ppermute | solution.py:345
  29.0 0.5 %collective-permute-done.9 = bf16[144,256]{1,0:T(8,128)(2,1)S(1)} collective-permute-done((bf16[144,256]{1,0:T(8,128)(2,1)S(1)}, bf16[144,256]{1,0:T(8,128)(2,1)S(1)}, u32[]{:S(2)}, u32[]{:S(2)}) %collective-permute-start.9) | collective-permute-done | bytes 73760 | tf_op jit(solution)/shard_map/ppermute | solution.py:345
  29.6 2.7 %collective-permute-start.16 = (bf16[144,256]{1,0:T(8,128)(2,1)S(1)}, bf16[144,256]{1,0:T(8,128)(2,1)S(1)}, u32[]{:S(2)}, u32[]{:S(2)}) collective-permute-start(bf16[144,256]{1,0:T(8,128)(2,1)S(1)} %add_convert_fusion), channel_id=1, source_target_pairs={{0,16},{8,24},{16,0},{24,8},{1,17},{9,25},{17,1},{25,9},{2,18},{10... | collective-permute-start | bytes 221192 | tf_op jit(solution)/shard_map/ppermute | solution.py:360
  32.2 0.6 %collective-permute-start.17 = (bf16[144,256]{1,0:T(8,128)(2,1)S(1)}, bf16[144,256]{1,0:T(8,128)(2,1)S(1)}, u32[]{:S(2)}, u32[]{:S(2)}) collective-permute-start(bf16[144,256]{1,0:T(8,128)(2,1)S(1)} %add_convert_fusion), channel_id=1, source_target_pairs={{0,24},{8,16},{16,8},{24,0},{1,25},{9,17},{17,9},{25,1},{2,26},{10... | collective-permute-start | bytes 221192 | tf_op jit(solution)/shard_map/ppermute | solution.py:360
  33.1 4.7 %conv.1 = bf16[2,2,176,256]{3,2,1,0:T(8,128)(2,1)} custom-call(s32[12]{0:T(128)S(1)} %stack.74.where_ref.refs_0_, f32[8,256]{1,0:T(8,128)S(1)} %get-tuple-element.60.norm_ref, bf16[2,4,176,256]{3,2,1,0:T(8,128)(2,1)S(1)} %get-tuple-element.61.act_ref, bf16[2,2,176,256]{3,2,1,0:T(8,128)(2,1)S(1)} %get-tuple-element.37.own_ref.refs_4_, ...), custom_call_target="tpu_custom_call" | custom-call | flops 2491416576 | bytes 4259840 | tf_op jit(solution)/shard_map/conv/pallas_call | solution.py:21
  38.4 0.7 %pad_maximum_fusion = f32[288,256]{1,0:T(8,128)} fusion(f32[144,256]{1,0:T(8,128)S(1)} %get-tuple-element.71, f32[144,256]{1,0:T(8,128)S(1)} %get-tuple-element.70), kind=kLoop, calls=%fused_computation | loop fusion | flops 73728 | bytes 589824 | tf_op jit(solution)/shard_map/concatenate | solution.py:368
  (30 shorter events, 3.4 us)
Async XLA Ops:
  0.6 2.0 %collective-permute-start = (bf16[2,2,176,256]{3,2,1,0:T(8,128)(2,1)}, bf16[2,2,176,256]{3,2,1,0:T(8,128)(2,1)S(1)}, u32[]{:S(2)}, u32[]{:S(2)}) collective-permute-start(bf16[2,2,176,256]{3,2,1,0:T(8,128)(2,1)} %bitcast.20), channel_id=1, source_target_pairs={{0,4},{4,0},{1,5},{5,1},{2,6},{6,2},{3,7},{7,3},{8,12},{12,8},{9,1... | collective-permute-start | bytes 1081352 | tf_op jit(solution)/shard_map/ppermute | solution.py:256
  1.1 7.3 %collective-permute-start.2 = (bf16[2,2,176,256]{3,2,1,0:T(8,128)(2,1)}, bf16[2,2,176,256]{3,2,1,0:T(8,128)(2,1)S(1)}, u32[]{:S(2)}, u32[]{:S(2)}) collective-permute-start(bf16[2,2,176,256]{3,2,1,0:T(8,128)(2,1)} %bitcast.18), channel_id=1, source_target_pairs={{0,4},{4,0},{1,5},{5,1},{2,6},{6,2},{3,7},{7,3},{8,12},{12,8},{9,1... | collective-permute-start | bytes 1081352 | tf_op jit(solution)/shard_map/ppermute | solution.py:257
  1.3 1.0 %copy-start.1 = (bf16[1,2,2,176,256]{4,3,2,1,0:T(8,128)(2,1)S(1)}, bf16[1,2,2,176,256]{4,3,2,1,0:T(8,128)(2,1)}, u32[]{:S(2)}) copy-start(bf16[1,2,2,176,256]{4,3,2,1,0:T(8,128)(2,1)} %param.6) | copy-start | bytes 1081348
  3.3 9.5 %collective-permute-start.1 = (bf16[400,256]{1,0:T(8,128)(2,1)S(1)}, bf16[400,256]{1,0:T(8,128)(2,1)S(1)}, u32[]{:S(2)}, u32[]{:S(2)}) collective-permute-start(bf16[400,256]{1,0:T(8,128)(2,1)S(1)} %get-tuple-element.38), channel_id=1, source_target_pairs={{0,1},{1,2},{2,3},{3,0},{4,7},{5,4},{6,5},{7,6},{8,9},{9,10},{10,1... | collective-permute-start | bytes 614408 | tf_op jit(solution)/shard_map/ppermute | solution.py:289
  6.2 4.2 %collective-permute-start.3 = (f32[16,256]{1,0:T(8,128)S(1)}, f32[16,256]{1,0:T(8,128)S(1)}, u32[]{:S(2)}, u32[]{:S(2)}) collective-permute-start(f32[16,256]{1,0:T(8,128)S(1)} %get-tuple-element.40.refs_1_), channel_id=1, source_target_pairs={{0,2},{1,3},{2,0},{3,1},{4,6},{5,7},{6,4},{7,5},{8,10},{9,11},{10,... | collective-permute-start | bytes 49160 | tf_op jit(solution)/shard_map/ppermute | solution.py:293
  8.5 1.0 %copy-start = (bf16[1,2,2,176,256]{4,3,2,1,0:T(8,128)(2,1)S(1)}, bf16[1,2,2,176,256]{4,3,2,1,0:T(8,128)(2,1)}, u32[]{:S(2)}) copy-start(bf16[1,2,2,176,256]{4,3,2,1,0:T(8,128)(2,1)} %param.11) | copy-start | bytes 1081348
  10.4 11.6 %collective-permute-start.4 = (bf16[352,256]{1,0:T(8,128)(2,1)S(1)}, bf16[352,256]{1,0:T(8,128)(2,1)S(1)}, u32[]{:S(2)}, u32[]{:S(2)}) collective-permute-start(bf16[352,256]{1,0:T(8,128)(2,1)S(1)} %get-tuple-element.44), channel_id=1, source_target_pairs={{0,1},{1,2},{2,3},{3,0},{4,7},{5,4},{6,5},{7,6},{8,9},{9,10},{10,1... | collective-permute-start | bytes 540680 | tf_op jit(solution)/shard_map/ppermute | solution.py:307
  12.8 1.2 %collective-permute-start.5 = (bf16[48,256]{1,0:T(8,128)(2,1)S(1)}, bf16[48,256]{1,0:T(8,128)(2,1)S(1)}, u32[]{:S(2)}, u32[]{:S(2)}) collective-permute-start(bf16[48,256]{1,0:T(8,128)(2,1)S(1)} %slice.6), channel_id=1, source_target_pairs={{0,4},{4,0},{1,5},{5,1},{2,6},{6,2},{3,7},{7,3},{8,12},{12,8},{9,1... | collective-permute-start | bytes 73736 | tf_op jit(solution)/shard_map/ppermute | solution.py:309
  16.2 6.4 %collective-permute-start.10 = (bf16[144,256]{1,0:T(8,128)(2,1)S(1)}, bf16[144,256]{1,0:T(8,128)(2,1)S(1)}, u32[]{:S(2)}, u32[]{:S(2)}) collective-permute-start(bf16[144,256]{1,0:T(8,128)(2,1)S(1)} %get-tuple-element.54), channel_id=1, source_target_pairs={{0,9},{1,8},{2,11},{3,10},{8,1},{9,0},{10,3},{11,2},{16,25},{17,24... | collective-permute-start | bytes 221192 | tf_op jit(solution)/shard_map/ppermute | solution.py:345
  18.5 6.6 %collective-permute-start.11 = (bf16[144,256]{1,0:T(8,128)(2,1)S(1)}, bf16[144,256]{1,0:T(8,128)(2,1)S(1)}, u32[]{:S(2)}, u32[]{:S(2)}) collective-permute-start(bf16[144,256]{1,0:T(8,128)(2,1)S(1)} %get-tuple-element.55), channel_id=1, source_target_pairs={{0,3},{1,2},{2,1},{3,0},{8,11},{9,10},{10,9},{11,8},{16,19},{17,18... | collective-permute-start | bytes 221192 | tf_op jit(solution)/shard_map/ppermute | solution.py:345
  19.3 7.5 %collective-permute-start.12 = (bf16[144,256]{1,0:T(8,128)(2,1)S(1)}, bf16[144,256]{1,0:T(8,128)(2,1)S(1)}, u32[]{:S(2)}, u32[]{:S(2)}) collective-permute-start(bf16[144,256]{1,0:T(8,128)(2,1)S(1)} %get-tuple-element.56), channel_id=1, source_target_pairs={{0,1},{1,0},{2,3},{3,2},{8,9},{9,8},{10,11},{11,10},{16,17},{17,16... | collective-permute-start | bytes 221192 | tf_op jit(solution)/shard_map/ppermute | solution.py:345
  21.0 5.9 %collective-permute-start.6 = (bf16[144,256]{1,0:T(8,128)(2,1)S(1)}, bf16[144,256]{1,0:T(8,128)(2,1)S(1)}, u32[]{:S(2)}, u32[]{:S(2)}) collective-permute-start(bf16[144,256]{1,0:T(8,128)(2,1)S(1)} %get-tuple-element.50), channel_id=1, source_target_pairs={{0,2},{1,3},{2,0},{3,1},{8,10},{9,11},{10,8},{11,9},{16,18},{17,19... | collective-permute-start | bytes 221192 | tf_op jit(solution)/shard_map/ppermute | solution.py:345
  22.0 6.6 %collective-permute-start.7 = (bf16[144,256]{1,0:T(8,128)(2,1)S(1)}, bf16[144,256]{1,0:T(8,128)(2,1)S(1)}, u32[]{:S(2)}, u32[]{:S(2)}) collective-permute-start(bf16[144,256]{1,0:T(8,128)(2,1)S(1)} %get-tuple-element.51), channel_id=1, source_target_pairs={{0,11},{1,10},{2,9},{3,8},{8,3},{9,2},{10,1},{11,0},{16,27},{17,26... | collective-permute-start | bytes 221192 | tf_op jit(solution)/shard_map/ppermute | solution.py:345
  22.6 6.4 %collective-permute-start.8 = (bf16[144,256]{1,0:T(8,128)(2,1)S(1)}, bf16[144,256]{1,0:T(8,128)(2,1)S(1)}, u32[]{:S(2)}, u32[]{:S(2)}) collective-permute-start(bf16[144,256]{1,0:T(8,128)(2,1)S(1)} %get-tuple-element.52), channel_id=1, source_target_pairs={{0,10},{1,11},{2,8},{3,9},{8,2},{9,3},{10,0},{11,1},{16,26},{17,27... | collective-permute-start | bytes 221192 | tf_op jit(solution)/shard_map/ppermute | solution.py:345
  25.1 4.4 %collective-permute-start.9 = (bf16[144,256]{1,0:T(8,128)(2,1)S(1)}, bf16[144,256]{1,0:T(8,128)(2,1)S(1)}, u32[]{:S(2)}, u32[]{:S(2)}) collective-permute-start(bf16[144,256]{1,0:T(8,128)(2,1)S(1)} %get-tuple-element.53), channel_id=1, source_target_pairs={{0,8},{1,9},{2,10},{3,11},{8,0},{9,1},{10,2},{11,3},{16,24},{17,25... | collective-permute-start | bytes 221192 | tf_op jit(solution)/shard_map/ppermute | solution.py:345
  26.8 6.0 %collective-permute-start.13 = (bf16[400,256]{1,0:T(8,128)(2,1)S(1)}, bf16[400,256]{1,0:T(8,128)(2,1)S(1)}, u32[]{:S(2)}, u32[]{:S(2)}) collective-permute-start(bf16[400,256]{1,0:T(8,128)(2,1)S(1)} %collective-permute-done.1.refs_6_), channel_id=1, source_target_pairs={{0,4},{4,0},{1,5},{5,1},{2,6},{6,2},{3,7},{7,3},{8,12},{12,8},{9,1... | collective-permute-start | bytes 614408 | tf_op jit(solution)/shard_map/ppermute | solution.py:353
  26.9 5.9 %collective-permute-start.14 = (bf16[352,256]{1,0:T(8,128)(2,1)S(1)}, bf16[352,256]{1,0:T(8,128)(2,1)S(1)}, u32[]{:S(2)}, u32[]{:S(2)}) collective-permute-start(bf16[352,256]{1,0:T(8,128)(2,1)S(1)} %collective-permute-done.4.near_late), channel_id=1, source_target_pairs={{0,4},{4,0},{1,5},{5,1},{2,6},{6,2},{3,7},{7,3},{8,12},{12,8},{9,1... | collective-permute-start | bytes 540680 | tf_op jit(solution)/shard_map/ppermute | solution.py:354
  29.6 8.3 %collective-permute-start.16 = (bf16[144,256]{1,0:T(8,128)(2,1)S(1)}, bf16[144,256]{1,0:T(8,128)(2,1)S(1)}, u32[]{:S(2)}, u32[]{:S(2)}) collective-permute-start(bf16[144,256]{1,0:T(8,128)(2,1)S(1)} %add_convert_fusion), channel_id=1, source_target_pairs={{0,16},{8,24},{16,0},{24,8},{1,17},{9,25},{17,1},{25,9},{2,18},{10... | collective-permute-start | bytes 221192 | tf_op jit(solution)/shard_map/ppermute | solution.py:360
  32.2 6.2 %collective-permute-start.17 = (bf16[144,256]{1,0:T(8,128)(2,1)S(1)}, bf16[144,256]{1,0:T(8,128)(2,1)S(1)}, u32[]{:S(2)}, u32[]{:S(2)}) collective-permute-start(bf16[144,256]{1,0:T(8,128)(2,1)S(1)} %add_convert_fusion), channel_id=1, source_target_pairs={{0,24},{8,16},{16,8},{24,0},{1,25},{9,17},{17,9},{25,1},{2,26},{10... | collective-permute-start | bytes 221192 | tf_op jit(solution)/shard_map/ppermute | solution.py:360
  32.8 5.6 %collective-permute-start.15 = (bf16[144,256]{1,0:T(8,128)(2,1)S(1)}, bf16[144,256]{1,0:T(8,128)(2,1)S(1)}, u32[]{:S(2)}, u32[]{:S(2)}) collective-permute-start(bf16[144,256]{1,0:T(8,128)(2,1)S(1)} %add_convert_fusion), channel_id=1, source_target_pairs={{0,8},{8,0},{16,24},{24,16},{1,9},{9,1},{17,25},{25,17},{2,10},{10... | collective-permute-start | bytes 221192 | tf_op jit(solution)/shard_map/ppermute | solution.py:360

commit v5 on v4

--- a/solution.py
+++ b/solution.py
@@ -266,7 +266,7 @@
     half = 9 * chans // 2
     if small:
         piece = half // 8
-        order = [(0, 0), (0, 2), (1, 3), (1, 2), (1, 0), (1, 1), (0, 3), (0, 1)]
+        order = [(0, 0), (1, 3), (1, 0), (0, 1), (0, 2), (1, 2), (1, 1), (0, 3)]
         starts = [(band ^ dr) * (2 * piece) + ((clip ^ dz) & 1) * piece for dz, dr in order]
         kinds = [F32] + [BF16] * 7
     else:

time: 39.5 us -> 38.9 us (0.985)
  waiting for transfers between devices: 5.29 us -> 4.61 us
    ppermute x3, starting transfers between devices: 3.56 us -> 4.1 us  [body(): lax.ppermute(t, 'dp', [(z, z ^ k) for z in range(4)])]
  transfers between devices with their start and end apart: 18 -> 18, of which waited for: 7 -> 9; matrix products, arithmetic and copies ran while one was open for 5% -> 5% of each run, Pallas kernels for 22% -> 22%
where the time goes in v5:
time: 38.9 us; the launch traced here: 38.6 us
  starting transfers between devices  19.9 us (51%)
  Pallas kernels  8.51 us (22%)
  waiting for transfers between devices  4.61 us (12%)
  local copies, waits for them, and re-layouts  3.97 us (10%)
  other arithmetic  0.86 us (2%)
  between operations  0.74 us (2%)
    ppermute x7, starting transfers between devices, body(): lax.ppermute(p, ('dp', 'rows'), [(z * 4 + r, (z ^ dz) * 4 + (r ^ dr)) for...  9.41 us
    pallas_call x5, Pallas kernels, call(): pl.pallas_call(kernel, out_shape=outs, in_specs=specs, out_specs=jax.tree...  8.51 us
    ppermute x3, starting transfers between devices, body(): lax.ppermute(t, 'dp', [(z, z ^ k) for z in range(4)])  4.1 us
    ppermute x1, starting transfers between devices, body(): near = lax.ppermute(early_rims, ('tm', 'rows'), joint)  2.91 us
    unnamed x4, local copies, waits for them, and re-layouts  1.96 us
    ppermute x7, waiting for transfers between devices, body(): lax.ppermute(p, ('dp', 'rows'), [(z * 4 + r, (z ^ dz) * 4 + (r ^ dr)) for...  1.81 us
    ppermute x1, starting transfers between devices, body(): lax.ppermute(sums, 'rows', [(r, (r + 2) % rows) for r in range(rows)])  1.52 us
    ppermute x1, starting transfers between devices, body(): near_late = lax.ppermute(late_rims, ('tm', 'rows'), joint)  1.24 us
  transfers between devices with their start and end apart: 18, of which 9 were waited for; matrix products, arithmetic and copies ran while one was open for 5% of the time, Pallas kernels for 22%

profile of v5, /device:TPU:0, one launch (start us, length us, event | category | flops | bytes accessed | tf_op | source)
XLA Modules:
  0.0 38.6 jit_solution(12019964906812398973)
XLA Ops:
  0.6 0.5 %collective-permute-start = (bf16[2,2,176,256]{3,2,1,0:T(8,128)(2,1)}, bf16[2,2,176,256]{3,2,1,0:T(8,128)(2,1)S(1)}, u32[]{:S(2)}, u32[]{:S(2)}) collective-permute-start(bf16[2,2,176,256]{3,2,1,0:T(8,128)(2,1)} %bitcast.20), channel_id=1, source_target_pairs={{0,4},{4,0},{1,5},{5,1},{2,6},{6,2},{3,7},{7,3},{8,12},{12,8},{9,1... | collective-permute-start | bytes 1081352 | tf_op jit(solution)/shard_map/ppermute | solution.py:256
  1.3 1.0 %copy-done.1 = bf16[1,2,2,176,256]{4,3,2,1,0:T(8,128)(2,1)S(1)} copy-done((bf16[1,2,2,176,256]{4,3,2,1,0:T(8,128)(2,1)S(1)}, bf16[1,2,2,176,256]{4,3,2,1,0:T(8,128)(2,1)}, u32[]{:S(2)}) %copy-start.1) | copy-done | bytes 360472
  2.7 0.6 %prep.1 = (f32[16,256]{1,0:T(8,128)S(1)}, bf16[400,256]{1,0:T(8,128)(2,1)S(1)}, bf16[352,256]{1,0:T(8,128)(2,1)S(1)}) custom-call(s32[12]{0:T(128)S(1)} %stack.74.where_ref.refs_0_, f32[16,256]{1,0:T(8,128)S(1)} %get-tuple-element.36.own_sums_ref, bf16[2,2,176,256]{3,2,1,0:T(8,128)(2,1)S(1)} %get-tuple-element.37.own_ref.refs_4_, ...), custom_call_target="tpu_custom_call" | custom-call | flops 540672 | bytes 1081344 | tf_op jit(solution)/shard_map/prep/pallas_call | solution.py:21
  3.3 2.9 %collective-permute-start.1 = (bf16[400,256]{1,0:T(8,128)(2,1)S(1)}, bf16[400,256]{1,0:T(8,128)(2,1)S(1)}, u32[]{:S(2)}, u32[]{:S(2)}) collective-permute-start(bf16[400,256]{1,0:T(8,128)(2,1)S(1)} %get-tuple-element.38), channel_id=1, source_target_pairs={{0,1},{1,2},{2,3},{3,0},{4,7},{5,4},{6,5},{7,6},{8,9},{9,10},{10,1... | collective-permute-start | bytes 614408 | tf_op jit(solution)/shard_map/ppermute | solution.py:289
  6.2 1.5 %collective-permute-start.3 = (f32[16,256]{1,0:T(8,128)S(1)}, f32[16,256]{1,0:T(8,128)S(1)}, u32[]{:S(2)}, u32[]{:S(2)}) collective-permute-start(f32[16,256]{1,0:T(8,128)S(1)} %get-tuple-element.40.refs_1_), channel_id=1, source_target_pairs={{0,2},{1,3},{2,0},{3,1},{4,6},{5,7},{6,4},{7,5},{8,10},{9,11},{10,... | collective-permute-start | bytes 49160 | tf_op jit(solution)/shard_map/ppermute | solution.py:293
  7.7 0.7 %stack.79.refs_3_.params_ref = f32[8,256]{1,0:T(8,128)S(1)} concatenate(f32[1,256]{1,0:T(1,128)} %bitcast.22, f32[1,256]{1,0:T(1,128)} %bitcast.23, f32[1,256]{1,0:T(1,128)} %bitcast.24, f32[1,256]{1,0:T(1,128)S(1)} %stack_broadcast_in_dim.3, f32[4,256]{1,0:T(4,128)S(1)} %stack.78), dimensions={0} | concatenate | bytes 16384 | tf_op jit(solution)/shard_map/stack | solution.py:297
  8.5 1.0 %copy-done = bf16[1,2,2,176,256]{4,3,2,1,0:T(8,128)(2,1)S(1)} copy-done((bf16[1,2,2,176,256]{4,3,2,1,0:T(8,128)(2,1)S(1)}, bf16[1,2,2,176,256]{4,3,2,1,0:T(8,128)(2,1)}, u32[]{:S(2)}) %copy-start) | copy-done | bytes 360472
  9.5 0.9 %cots.1.refs_8_ = bf16[3,3,2,176,256]{4,3,2,1,0:T(8,128)(2,1)S(1)} custom-call(s32[12]{0:T(128)S(1)} %stack.74.where_ref.refs_0_, bf16[2,2,176,256]{3,2,1,0:T(8,128)(2,1)S(1)} %bitcast.19, bf16[2,2,176,256]{3,2,1,0:T(8,128)(2,1)S(1)} %collective-permute-done.2.other_ref), custom_call_target="tpu_custom_call" | custom-call | flops 1802240 | bytes 2523136 | tf_op jit(solution)/shard_map/cots/pallas_call | solution.py:21
  10.4 1.2 %collective-permute-start.4 = (bf16[352,256]{1,0:T(8,128)(2,1)S(1)}, bf16[352,256]{1,0:T(8,128)(2,1)S(1)}, u32[]{:S(2)}, u32[]{:S(2)}) collective-permute-start(bf16[352,256]{1,0:T(8,128)(2,1)S(1)} %get-tuple-element.44), channel_id=1, source_target_pairs={{0,1},{1,2},{2,3},{3,0},{4,7},{5,4},{6,5},{7,6},{8,9},{9,10},{10,1... | collective-permute-start | bytes 540680 | tf_op jit(solution)/shard_map/ppermute | solution.py:307
  11.6 1.2 %collective-permute-done.1.refs_6_ = bf16[400,256]{1,0:T(8,128)(2,1)S(1)} collective-permute-done((bf16[400,256]{1,0:T(8,128)(2,1)S(1)}, bf16[400,256]{1,0:T(8,128)(2,1)S(1)}, u32[]{:S(2)}, u32[]{:S(2)}) %collective-permute-start.1) | collective-permute-done | bytes 204832 | tf_op jit(solution)/shard_map/ppermute | solution.py:289
  12.8 1.2 %collective-permute-done.5.refs_7_ = bf16[48,256]{1,0:T(8,128)(2,1)S(1)} collective-permute-done((bf16[48,256]{1,0:T(8,128)(2,1)S(1)}, bf16[48,256]{1,0:T(8,128)(2,1)S(1)}, u32[]{:S(2)}, u32[]{:S(2)}) %collective-permute-start.5) | collective-permute-done | bytes 24608 | tf_op jit(solution)/shard_map/ppermute | solution.py:309
  14.0 2.2 %grad.1 = (bf16[2,4,176,256]{3,2,1,0:T(8,128)(2,1)S(1)}, f32[8,256]{1,0:T(8,128)S(1)}, f32[144,256]{1,0:T(8,128)S(1)}, bf16[144,256]{1,0:T(8,128)(2,1)S(1)}, bf1...) custom-call(s32[12]{0:T(128)S(1)} %stack.74.where_ref.refs_0_, ...), custom_call_target="tpu_custom_call" | custom-call | flops 622854144 | bytes 3604480 | tf_op jit(solution)/shard_map/grad/pallas_call | solution.py:21
  16.2 1.7 %collective-permute-start.10 = (bf16[144,256]{1,0:T(8,128)(2,1)S(1)}, bf16[144,256]{1,0:T(8,128)(2,1)S(1)}, u32[]{:S(2)}, u32[]{:S(2)}) collective-permute-start(bf16[144,256]{1,0:T(8,128)(2,1)S(1)} %get-tuple-element.54), channel_id=1, source_target_pairs={{0,10},{1,11},{2,8},{3,9},{8,2},{9,3},{10,0},{11,1},{16,26},{17,27... | collective-permute-start | bytes 221192 | tf_op jit(solution)/shard_map/ppermute | solution.py:345
  17.9 1.6 %collective-permute-start.11 = (bf16[144,256]{1,0:T(8,128)(2,1)S(1)}, bf16[144,256]{1,0:T(8,128)(2,1)S(1)}, u32[]{:S(2)}, u32[]{:S(2)}) collective-permute-start(bf16[144,256]{1,0:T(8,128)(2,1)S(1)} %get-tuple-element.55), channel_id=1, source_target_pairs={{0,9},{1,8},{2,11},{3,10},{8,1},{9,0},{10,3},{11,2},{16,25},{17,24... | collective-permute-start | bytes 221192 | tf_op jit(solution)/shard_map/ppermute | solution.py:345
  19.4 1.2 %collective-permute-start.12 = (bf16[144,256]{1,0:T(8,128)(2,1)S(1)}, bf16[144,256]{1,0:T(8,128)(2,1)S(1)}, u32[]{:S(2)}, u32[]{:S(2)}) collective-permute-start(bf16[144,256]{1,0:T(8,128)(2,1)S(1)} %get-tuple-element.56), channel_id=1, source_target_pairs={{0,3},{1,2},{2,1},{3,0},{8,11},{9,10},{10,9},{11,8},{16,19},{17,18... | collective-permute-start | bytes 221192 | tf_op jit(solution)/shard_map/ppermute | solution.py:345
  20.6 2.8 %collective-permute-start.6 = (bf16[144,256]{1,0:T(8,128)(2,1)S(1)}, bf16[144,256]{1,0:T(8,128)(2,1)S(1)}, u32[]{:S(2)}, u32[]{:S(2)}) collective-permute-start(bf16[144,256]{1,0:T(8,128)(2,1)S(1)} %get-tuple-element.50), channel_id=1, source_target_pairs={{0,11},{1,10},{2,9},{3,8},{8,3},{9,2},{10,1},{11,0},{16,27},{17,26... | collective-permute-start | bytes 221192 | tf_op jit(solution)/shard_map/ppermute | solution.py:345
  24.1 1.5 %collective-permute-start.9 = (bf16[144,256]{1,0:T(8,128)(2,1)S(1)}, bf16[144,256]{1,0:T(8,128)(2,1)S(1)}, u32[]{:S(2)}, u32[]{:S(2)}) collective-permute-start(bf16[144,256]{1,0:T(8,128)(2,1)S(1)} %get-tuple-element.53), channel_id=1, source_target_pairs={{0,2},{1,3},{2,0},{3,1},{8,10},{9,11},{10,8},{11,9},{16,18},{17,19... | collective-permute-start | bytes 221192 | tf_op jit(solution)/shard_map/ppermute | solution.py:345
  25.6 1.2 %slice.7.first_ref = bf16[1,2,3,256,256]{4,3,2,1,0:T(8,128)(2,1)S(1)} slice(bf16[3,3,3,256,256]{4,3,2,1,0:T(8,128)(2,1)} %weight_hbm.1), slice={[0:1], [0:2], [0:3], [0:256], [0:256]} | slice | bytes 1572864 | tf_op jit(solution)/shard_map/slice | solution.py:358
  27.7 0.5 %collective-permute-done.8 = bf16[144,256]{1,0:T(8,128)(2,1)S(1)} collective-permute-done((bf16[144,256]{1,0:T(8,128)(2,1)S(1)}, bf16[144,256]{1,0:T(8,128)(2,1)S(1)}, u32[]{:S(2)}, u32[]{:S(2)}) %collective-permute-start.8) | collective-permute-done | bytes 73760 | tf_op jit(solution)/shard_map/ppermute | solution.py:345
  28.3 0.5 %collective-permute-done.9 = bf16[144,256]{1,0:T(8,128)(2,1)S(1)} collective-permute-done((bf16[144,256]{1,0:T(8,128)(2,1)S(1)}, bf16[144,256]{1,0:T(8,128)(2,1)S(1)}, u32[]{:S(2)}, u32[]{:S(2)}) %collective-permute-start.9) | collective-permute-done | bytes 73760 | tf_op jit(solution)/shard_map/ppermute | solution.py:345
  28.8 2.5 %collective-permute-start.16 = (bf16[144,256]{1,0:T(8,128)(2,1)S(1)}, bf16[144,256]{1,0:T(8,128)(2,1)S(1)}, u32[]{:S(2)}, u32[]{:S(2)}) collective-permute-start(bf16[144,256]{1,0:T(8,128)(2,1)S(1)} %add_convert_fusion), channel_id=1, source_target_pairs={{0,16},{8,24},{16,0},{24,8},{1,17},{9,25},{17,1},{25,9},{2,18},{10... | collective-permute-start | bytes 221192 | tf_op jit(solution)/shard_map/ppermute | solution.py:360
  31.3 1.3 %collective-permute-start.17 = (bf16[144,256]{1,0:T(8,128)(2,1)S(1)}, bf16[144,256]{1,0:T(8,128)(2,1)S(1)}, u32[]{:S(2)}, u32[]{:S(2)}) collective-permute-start(bf16[144,256]{1,0:T(8,128)(2,1)S(1)} %add_convert_fusion), channel_id=1, source_target_pairs={{0,24},{8,16},{16,8},{24,0},{1,25},{9,17},{17,9},{25,1},{2,26},{10... | collective-permute-start | bytes 221192 | tf_op jit(solution)/shard_map/ppermute | solution.py:360
  32.9 4.7 %conv.1 = bf16[2,2,176,256]{3,2,1,0:T(8,128)(2,1)} custom-call(s32[12]{0:T(128)S(1)} %stack.74.where_ref.refs_0_, f32[8,256]{1,0:T(8,128)S(1)} %get-tuple-element.60.norm_ref, bf16[2,4,176,256]{3,2,1,0:T(8,128)(2,1)S(1)} %get-tuple-element.61.act_ref, bf16[2,2,176,256]{3,2,1,0:T(8,128)(2,1)S(1)} %get-tuple-element.37.own_ref.refs_4_, ...), custom_call_target="tpu_custom_call" | custom-call | flops 2491416576 | bytes 4259840 | tf_op jit(solution)/shard_map/conv/pallas_call | solution.py:21
  37.9 0.7 %pad_maximum_fusion = f32[288,256]{1,0:T(8,128)} fusion(f32[144,256]{1,0:T(8,128)S(1)} %get-tuple-element.71, f32[144,256]{1,0:T(8,128)S(1)} %get-tuple-element.70), kind=kLoop, calls=%fused_computation | loop fusion | flops 73728 | bytes 589824 | tf_op jit(solution)/shard_map/concatenate | solution.py:368
  (30 shorter events, 2.8 us)
Async XLA Ops:
  0.6 2.0 %collective-permute-start = (bf16[2,2,176,256]{3,2,1,0:T(8,128)(2,1)}, bf16[2,2,176,256]{3,2,1,0:T(8,128)(2,1)S(1)}, u32[]{:S(2)}, u32[]{:S(2)}) collective-permute-start(bf16[2,2,176,256]{3,2,1,0:T(8,128)(2,1)} %bitcast.20), channel_id=1, source_target_pairs={{0,4},{4,0},{1,5},{5,1},{2,6},{6,2},{3,7},{7,3},{8,12},{12,8},{9,1... | collective-permute-start | bytes 1081352 | tf_op jit(solution)/shard_map/ppermute | solution.py:256
  1.1 7.3 %collective-permute-start.2 = (bf16[2,2,176,256]{3,2,1,0:T(8,128)(2,1)}, bf16[2,2,176,256]{3,2,1,0:T(8,128)(2,1)S(1)}, u32[]{:S(2)}, u32[]{:S(2)}) collective-permute-start(bf16[2,2,176,256]{3,2,1,0:T(8,128)(2,1)} %bitcast.18), channel_id=1, source_target_pairs={{0,4},{4,0},{1,5},{5,1},{2,6},{6,2},{3,7},{7,3},{8,12},{12,8},{9,1... | collective-permute-start | bytes 1081352 | tf_op jit(solution)/shard_map/ppermute | solution.py:257
  1.3 1.0 %copy-start.1 = (bf16[1,2,2,176,256]{4,3,2,1,0:T(8,128)(2,1)S(1)}, bf16[1,2,2,176,256]{4,3,2,1,0:T(8,128)(2,1)}, u32[]{:S(2)}) copy-start(bf16[1,2,2,176,256]{4,3,2,1,0:T(8,128)(2,1)} %param.6) | copy-start | bytes 1081348
  3.3 9.5 %collective-permute-start.1 = (bf16[400,256]{1,0:T(8,128)(2,1)S(1)}, bf16[400,256]{1,0:T(8,128)(2,1)S(1)}, u32[]{:S(2)}, u32[]{:S(2)}) collective-permute-start(bf16[400,256]{1,0:T(8,128)(2,1)S(1)} %get-tuple-element.38), channel_id=1, source_target_pairs={{0,1},{1,2},{2,3},{3,0},{4,7},{5,4},{6,5},{7,6},{8,9},{9,10},{10,1... | collective-permute-start | bytes 614408 | tf_op jit(solution)/shard_map/ppermute | solution.py:289
  6.2 4.2 %collective-permute-start.3 = (f32[16,256]{1,0:T(8,128)S(1)}, f32[16,256]{1,0:T(8,128)S(1)}, u32[]{:S(2)}, u32[]{:S(2)}) collective-permute-start(f32[16,256]{1,0:T(8,128)S(1)} %get-tuple-element.40.refs_1_), channel_id=1, source_target_pairs={{0,2},{1,3},{2,0},{3,1},{4,6},{5,7},{6,4},{7,5},{8,10},{9,11},{10,... | collective-permute-start | bytes 49160 | tf_op jit(solution)/shard_map/ppermute | solution.py:293
  8.5 1.0 %copy-start = (bf16[1,2,2,176,256]{4,3,2,1,0:T(8,128)(2,1)S(1)}, bf16[1,2,2,176,256]{4,3,2,1,0:T(8,128)(2,1)}, u32[]{:S(2)}) copy-start(bf16[1,2,2,176,256]{4,3,2,1,0:T(8,128)(2,1)} %param.11) | copy-start | bytes 1081348
  10.4 13.0 %collective-permute-start.4 = (bf16[352,256]{1,0:T(8,128)(2,1)S(1)}, bf16[352,256]{1,0:T(8,128)(2,1)S(1)}, u32[]{:S(2)}, u32[]{:S(2)}) collective-permute-start(bf16[352,256]{1,0:T(8,128)(2,1)S(1)} %get-tuple-element.44), channel_id=1, source_target_pairs={{0,1},{1,2},{2,3},{3,0},{4,7},{5,4},{6,5},{7,6},{8,9},{9,10},{10,1... | collective-permute-start | bytes 540680 | tf_op jit(solution)/shard_map/ppermute | solution.py:307
  12.8 1.2 %collective-permute-start.5 = (bf16[48,256]{1,0:T(8,128)(2,1)S(1)}, bf16[48,256]{1,0:T(8,128)(2,1)S(1)}, u32[]{:S(2)}, u32[]{:S(2)}) collective-permute-start(bf16[48,256]{1,0:T(8,128)(2,1)S(1)} %slice.6), channel_id=1, source_target_pairs={{0,4},{4,0},{1,5},{5,1},{2,6},{6,2},{3,7},{7,3},{8,12},{12,8},{9,1... | collective-permute-start | bytes 73736 | tf_op jit(solution)/shard_map/ppermute | solution.py:309
  16.2 7.7 %collective-permute-start.10 = (bf16[144,256]{1,0:T(8,128)(2,1)S(1)}, bf16[144,256]{1,0:T(8,128)(2,1)S(1)}, u32[]{:S(2)}, u32[]{:S(2)}) collective-permute-start(bf16[144,256]{1,0:T(8,128)(2,1)S(1)} %get-tuple-element.54), channel_id=1, source_target_pairs={{0,10},{1,11},{2,8},{3,9},{8,2},{9,3},{10,0},{11,1},{16,26},{17,27... | collective-permute-start | bytes 221192 | tf_op jit(solution)/shard_map/ppermute | solution.py:345
  17.9 6.3 %collective-permute-start.11 = (bf16[144,256]{1,0:T(8,128)(2,1)S(1)}, bf16[144,256]{1,0:T(8,128)(2,1)S(1)}, u32[]{:S(2)}, u32[]{:S(2)}) collective-permute-start(bf16[144,256]{1,0:T(8,128)(2,1)S(1)} %get-tuple-element.55), channel_id=1, source_target_pairs={{0,9},{1,8},{2,11},{3,10},{8,1},{9,0},{10,3},{11,2},{16,25},{17,24... | collective-permute-start | bytes 221192 | tf_op jit(solution)/shard_map/ppermute | solution.py:345
  19.4 7.5 %collective-permute-start.12 = (bf16[144,256]{1,0:T(8,128)(2,1)S(1)}, bf16[144,256]{1,0:T(8,128)(2,1)S(1)}, u32[]{:S(2)}, u32[]{:S(2)}) collective-permute-start(bf16[144,256]{1,0:T(8,128)(2,1)S(1)} %get-tuple-element.56), channel_id=1, source_target_pairs={{0,3},{1,2},{2,1},{3,0},{8,11},{9,10},{10,9},{11,8},{16,19},{17,18... | collective-permute-start | bytes 221192 | tf_op jit(solution)/shard_map/ppermute | solution.py:345
  20.6 6.7 %collective-permute-start.6 = (bf16[144,256]{1,0:T(8,128)(2,1)S(1)}, bf16[144,256]{1,0:T(8,128)(2,1)S(1)}, u32[]{:S(2)}, u32[]{:S(2)}) collective-permute-start(bf16[144,256]{1,0:T(8,128)(2,1)S(1)} %get-tuple-element.50), channel_id=1, source_target_pairs={{0,11},{1,10},{2,9},{3,8},{8,3},{9,2},{10,1},{11,0},{16,27},{17,26... | collective-permute-start | bytes 221192 | tf_op jit(solution)/shard_map/ppermute | solution.py:345
  23.4 4.4 %collective-permute-start.7 = (bf16[144,256]{1,0:T(8,128)(2,1)S(1)}, bf16[144,256]{1,0:T(8,128)(2,1)S(1)}, u32[]{:S(2)}, u32[]{:S(2)}) collective-permute-start(bf16[144,256]{1,0:T(8,128)(2,1)S(1)} %get-tuple-element.51), channel_id=1, source_target_pairs={{0,8},{1,9},{2,10},{3,11},{8,0},{9,1},{10,2},{11,3},{16,24},{17,25... | collective-permute-start | bytes 221192 | tf_op jit(solution)/shard_map/ppermute | solution.py:345
  23.8 4.4 %collective-permute-start.8 = (bf16[144,256]{1,0:T(8,128)(2,1)S(1)}, bf16[144,256]{1,0:T(8,128)(2,1)S(1)}, u32[]{:S(2)}, u32[]{:S(2)}) collective-permute-start(bf16[144,256]{1,0:T(8,128)(2,1)S(1)} %get-tuple-element.52), channel_id=1, source_target_pairs={{0,1},{1,0},{2,3},{3,2},{8,9},{9,8},{10,11},{11,10},{16,17},{17,16... | collective-permute-start | bytes 221192 | tf_op jit(solution)/shard_map/ppermute | solution.py:345
  24.1 4.6 %collective-permute-start.9 = (bf16[144,256]{1,0:T(8,128)(2,1)S(1)}, bf16[144,256]{1,0:T(8,128)(2,1)S(1)}, u32[]{:S(2)}, u32[]{:S(2)}) collective-permute-start(bf16[144,256]{1,0:T(8,128)(2,1)S(1)} %get-tuple-element.53), channel_id=1, source_target_pairs={{0,2},{1,3},{2,0},{3,1},{8,10},{9,11},{10,8},{11,9},{16,18},{17,19... | collective-permute-start | bytes 221192 | tf_op jit(solution)/shard_map/ppermute | solution.py:345
  27.0 5.6 %collective-permute-start.13 = (bf16[400,256]{1,0:T(8,128)(2,1)S(1)}, bf16[400,256]{1,0:T(8,128)(2,1)S(1)}, u32[]{:S(2)}, u32[]{:S(2)}) collective-permute-start(bf16[400,256]{1,0:T(8,128)(2,1)S(1)} %collective-permute-done.1.refs_6_), channel_id=1, source_target_pairs={{0,4},{4,0},{1,5},{5,1},{2,6},{6,2},{3,7},{7,3},{8,12},{12,8},{9,1... | collective-permute-start | bytes 614408 | tf_op jit(solution)/shard_map/ppermute | solution.py:353
  27.4 5.3 %collective-permute-start.14 = (bf16[352,256]{1,0:T(8,128)(2,1)S(1)}, bf16[352,256]{1,0:T(8,128)(2,1)S(1)}, u32[]{:S(2)}, u32[]{:S(2)}) collective-permute-start(bf16[352,256]{1,0:T(8,128)(2,1)S(1)} %collective-permute-done.4.near_late), channel_id=1, source_target_pairs={{0,4},{4,0},{1,5},{5,1},{2,6},{6,2},{3,7},{7,3},{8,12},{12,8},{9,1... | collective-permute-start | bytes 540680 | tf_op jit(solution)/shard_map/ppermute | solution.py:354
  28.8 8.9 %collective-permute-start.16 = (bf16[144,256]{1,0:T(8,128)(2,1)S(1)}, bf16[144,256]{1,0:T(8,128)(2,1)S(1)}, u32[]{:S(2)}, u32[]{:S(2)}) collective-permute-start(bf16[144,256]{1,0:T(8,128)(2,1)S(1)} %add_convert_fusion), channel_id=1, source_target_pairs={{0,16},{8,24},{16,0},{24,8},{1,17},{9,25},{17,1},{25,9},{2,18},{10... | collective-permute-start | bytes 221192 | tf_op jit(solution)/shard_map/ppermute | solution.py:360
  31.3 6.4 %collective-permute-start.17 = (bf16[144,256]{1,0:T(8,128)(2,1)S(1)}, bf16[144,256]{1,0:T(8,128)(2,1)S(1)}, u32[]{:S(2)}, u32[]{:S(2)}) collective-permute-start(bf16[144,256]{1,0:T(8,128)(2,1)S(1)} %add_convert_fusion), channel_id=1, source_target_pairs={{0,24},{8,16},{16,8},{24,0},{1,25},{9,17},{17,9},{25,1},{2,26},{10... | collective-permute-start | bytes 221192 | tf_op jit(solution)/shard_map/ppermute | solution.py:360
  32.6 5.2 %collective-permute-start.15 = (bf16[144,256]{1,0:T(8,128)(2,1)S(1)}, bf16[144,256]{1,0:T(8,128)(2,1)S(1)}, u32[]{:S(2)}, u32[]{:S(2)}) collective-permute-start(bf16[144,256]{1,0:T(8,128)(2,1)S(1)} %add_convert_fusion), channel_id=1, source_target_pairs={{0,8},{8,0},{16,24},{24,16},{1,9},{9,1},{17,25},{25,17},{2,10},{10... | collective-permute-start | bytes 221192 | tf_op jit(solution)/shard_map/ppermute | solution.py:360

commit v6 on v5

--- a/solution.py
+++ b/solution.py
@@ -103,8 +103,8 @@
 
 
 def activate(x, scale, shift):
-    v = x.astype(F32) * scale + shift
-    return v * (0.5 + 0.5 * jnp.tanh(0.5 * v))
+    half = x.astype(F32) * scale + shift
+    return half + half * jnp.tanh(half)
 
 
 def grad_kernel(count, decode, n_stats, n_pieces, rows_out, *refs):
@@ -129,8 +129,8 @@
     both = group_sum(jnp.concatenate([total, squares] + [total] * 6, axis=0), chans // GROUPS) / count
     mean = both[0:1]
     var = both[1:2] - mean * mean
-    scale = lax.rsqrt(var + 1e-06) * params_ref[0:1, :]
-    shift = params_ref[1:2, :] - mean * scale
+    scale = lax.rsqrt(var + 1e-06) * params_ref[0:1, :] * 0.5
+    shift = params_ref[1:2, :] * 0.5 - mean * scale
     norm_ref[0:1, :] = scale
     norm_ref[1:2, :] = shift
     norm_ref[2:8, :] = jnp.zeros((6, chans), F32)

time: 38.9 us -> 38.8 us (level)
  starting transfers between devices: 19.9 us -> 20.3 us
  transfers between devices with their start and end apart: 18 -> 18, of which waited for: 9 -> 7; matrix products, arithmetic and copies ran while one was open for 5% -> 5% of each run, Pallas kernels for 22% -> 22%
where the time goes in v6:
time: 38.8 us; the launch traced here: 38.5 us
  starting transfers between devices  20.3 us (52%)
  Pallas kernels  8.43 us (22%)
  waiting for transfers between devices  4.23 us (11%)
  local copies, waits for them, and re-layouts  3.97 us (10%)
  other arithmetic  0.86 us (2%)
  between operations  0.74 us (2%)
    ppermute x7, starting transfers between devices, body(): lax.ppermute(p, ('dp', 'rows'), [(z * 4 + r, (z ^ dz) * 4 + (r ^ dr)) for...  9.41 us
    pallas_call x5, Pallas kernels, call(): pl.pallas_call(kernel, out_shape=outs, in_specs=specs, out_specs=jax.tree...  8.43 us
    ppermute x3, starting transfers between devices, body(): lax.ppermute(t, 'dp', [(z, z ^ k) for z in range(4)])  4.1 us
    ppermute x1, starting transfers between devices, body(): near = lax.ppermute(early_rims, ('tm', 'rows'), joint)  2.91 us
    unnamed x4, local copies, waits for them, and re-layouts  1.96 us
    ppermute x1, starting transfers between devices, body(): lax.ppermute(sums, 'rows', [(r, (r + 2) % rows) for r in range(rows)])  1.52 us
    ppermute x7, waiting for transfers between devices, body(): lax.ppermute(p, ('dp', 'rows'), [(z * 4 + r, (z ^ dz) * 4 + (r ^ dr)) for...  1.43 us
    ppermute x1, starting transfers between devices, body(): near_late = lax.ppermute(late_rims, ('tm', 'rows'), joint)  1.24 us
  transfers between devices with their start and end apart: 18, of which 7 were waited for; matrix products, arithmetic and copies ran while one was open for 5% of the time, Pallas kernels for 22%

profile of v6, /device:TPU:0, one launch (start us, length us, event | category | flops | bytes accessed | tf_op | source)
XLA Modules:
  0.0 38.5 jit_solution(4711142152146952313)
XLA Ops:
  0.6 0.5 %collective-permute-start = (bf16[2,2,176,256]{3,2,1,0:T(8,128)(2,1)}, bf16[2,2,176,256]{3,2,1,0:T(8,128)(2,1)S(1)}, u32[]{:S(2)}, u32[]{:S(2)}) collective-permute-start(bf16[2,2,176,256]{3,2,1,0:T(8,128)(2,1)} %bitcast.20), channel_id=1, source_target_pairs={{0,4},{4,0},{1,5},{5,1},{2,6},{6,2},{3,7},{7,3},{8,12},{12,8},{9,1... | collective-permute-start | bytes 1081352 | tf_op jit(solution)/shard_map/ppermute | solution.py:256
  1.3 1.0 %copy-done.1 = bf16[1,2,2,176,256]{4,3,2,1,0:T(8,128)(2,1)S(1)} copy-done((bf16[1,2,2,176,256]{4,3,2,1,0:T(8,128)(2,1)S(1)}, bf16[1,2,2,176,256]{4,3,2,1,0:T(8,128)(2,1)}, u32[]{:S(2)}) %copy-start.1) | copy-done | bytes 360472
  2.7 0.6 %prep.1 = (f32[16,256]{1,0:T(8,128)S(1)}, bf16[400,256]{1,0:T(8,128)(2,1)S(1)}, bf16[352,256]{1,0:T(8,128)(2,1)S(1)}) custom-call(s32[12]{0:T(128)S(1)} %stack.74.where_ref.refs_0_, f32[16,256]{1,0:T(8,128)S(1)} %get-tuple-element.36.own_sums_ref, bf16[2,2,176,256]{3,2,1,0:T(8,128)(2,1)S(1)} %get-tuple-element.37.own_ref.refs_4_, ...), custom_call_target="tpu_custom_call" | custom-call | flops 540672 | bytes 1081344 | tf_op jit(solution)/shard_map/prep/pallas_call | solution.py:21
  3.3 2.9 %collective-permute-start.1 = (bf16[400,256]{1,0:T(8,128)(2,1)S(1)}, bf16[400,256]{1,0:T(8,128)(2,1)S(1)}, u32[]{:S(2)}, u32[]{:S(2)}) collective-permute-start(bf16[400,256]{1,0:T(8,128)(2,1)S(1)} %get-tuple-element.38), channel_id=1, source_target_pairs={{0,1},{1,2},{2,3},{3,0},{4,7},{5,4},{6,5},{7,6},{8,9},{9,10},{10,1... | collective-permute-start | bytes 614408 | tf_op jit(solution)/shard_map/ppermute | solution.py:289
  6.2 1.5 %collective-permute-start.3 = (f32[16,256]{1,0:T(8,128)S(1)}, f32[16,256]{1,0:T(8,128)S(1)}, u32[]{:S(2)}, u32[]{:S(2)}) collective-permute-start(f32[16,256]{1,0:T(8,128)S(1)} %get-tuple-element.40.refs_1_), channel_id=1, source_target_pairs={{0,2},{1,3},{2,0},{3,1},{4,6},{5,7},{6,4},{7,5},{8,10},{9,11},{10,... | collective-permute-start | bytes 49160 | tf_op jit(solution)/shard_map/ppermute | solution.py:293
  7.7 0.7 %stack.79.refs_3_.params_ref = f32[8,256]{1,0:T(8,128)S(1)} concatenate(f32[1,256]{1,0:T(1,128)} %bitcast.22, f32[1,256]{1,0:T(1,128)} %bitcast.23, f32[1,256]{1,0:T(1,128)} %bitcast.24, f32[1,256]{1,0:T(1,128)S(1)} %stack_broadcast_in_dim.3, f32[4,256]{1,0:T(4,128)S(1)} %stack.78), dimensions={0} | concatenate | bytes 16384 | tf_op jit(solution)/shard_map/stack | solution.py:297
  8.5 1.0 %copy-done = bf16[1,2,2,176,256]{4,3,2,1,0:T(8,128)(2,1)S(1)} copy-done((bf16[1,2,2,176,256]{4,3,2,1,0:T(8,128)(2,1)S(1)}, bf16[1,2,2,176,256]{4,3,2,1,0:T(8,128)(2,1)}, u32[]{:S(2)}) %copy-start) | copy-done | bytes 360472
  9.5 0.9 %cots.1.refs_8_ = bf16[3,3,2,176,256]{4,3,2,1,0:T(8,128)(2,1)S(1)} custom-call(s32[12]{0:T(128)S(1)} %stack.74.where_ref.refs_0_, bf16[2,2,176,256]{3,2,1,0:T(8,128)(2,1)S(1)} %bitcast.19, bf16[2,2,176,256]{3,2,1,0:T(8,128)(2,1)S(1)} %collective-permute-done.2.other_ref), custom_call_target="tpu_custom_call" | custom-call | flops 1802240 | bytes 2523136 | tf_op jit(solution)/shard_map/cots/pallas_call | solution.py:21
  10.4 1.2 %collective-permute-start.4 = (bf16[352,256]{1,0:T(8,128)(2,1)S(1)}, bf16[352,256]{1,0:T(8,128)(2,1)S(1)}, u32[]{:S(2)}, u32[]{:S(2)}) collective-permute-start(bf16[352,256]{1,0:T(8,128)(2,1)S(1)} %get-tuple-element.44), channel_id=1, source_target_pairs={{0,1},{1,2},{2,3},{3,0},{4,7},{5,4},{6,5},{7,6},{8,9},{9,10},{10,1... | collective-permute-start | bytes 540680 | tf_op jit(solution)/shard_map/ppermute | solution.py:307
  11.6 1.2 %collective-permute-done.1.refs_6_ = bf16[400,256]{1,0:T(8,128)(2,1)S(1)} collective-permute-done((bf16[400,256]{1,0:T(8,128)(2,1)S(1)}, bf16[400,256]{1,0:T(8,128)(2,1)S(1)}, u32[]{:S(2)}, u32[]{:S(2)}) %collective-permute-start.1) | collective-permute-done | bytes 204832 | tf_op jit(solution)/shard_map/ppermute | solution.py:289
  12.8 1.2 %collective-permute-done.5.refs_7_ = bf16[48,256]{1,0:T(8,128)(2,1)S(1)} collective-permute-done((bf16[48,256]{1,0:T(8,128)(2,1)S(1)}, bf16[48,256]{1,0:T(8,128)(2,1)S(1)}, u32[]{:S(2)}, u32[]{:S(2)}) %collective-permute-start.5) | collective-permute-done | bytes 24608 | tf_op jit(solution)/shard_map/ppermute | solution.py:309
  14.0 2.1 %grad.1 = (bf16[2,4,176,256]{3,2,1,0:T(8,128)(2,1)S(1)}, f32[8,256]{1,0:T(8,128)S(1)}, f32[144,256]{1,0:T(8,128)S(1)}, bf16[144,256]{1,0:T(8,128)(2,1)S(1)}, bf1...) custom-call(s32[12]{0:T(128)S(1)} %stack.74.where_ref.refs_0_, ...), custom_call_target="tpu_custom_call" | custom-call | flops 622854144 | bytes 3604480 | tf_op jit(solution)/shard_map/grad/pallas_call | solution.py:21
  16.1 1.7 %collective-permute-start.10 = (bf16[144,256]{1,0:T(8,128)(2,1)S(1)}, bf16[144,256]{1,0:T(8,128)(2,1)S(1)}, u32[]{:S(2)}, u32[]{:S(2)}) collective-permute-start(bf16[144,256]{1,0:T(8,128)(2,1)S(1)} %get-tuple-element.54), channel_id=1, source_target_pairs={{0,10},{1,11},{2,8},{3,9},{8,2},{9,3},{10,0},{11,1},{16,26},{17,27... | collective-permute-start | bytes 221192 | tf_op jit(solution)/shard_map/ppermute | solution.py:345
  17.8 1.6 %collective-permute-start.11 = (bf16[144,256]{1,0:T(8,128)(2,1)S(1)}, bf16[144,256]{1,0:T(8,128)(2,1)S(1)}, u32[]{:S(2)}, u32[]{:S(2)}) collective-permute-start(bf16[144,256]{1,0:T(8,128)(2,1)S(1)} %get-tuple-element.55), channel_id=1, source_target_pairs={{0,9},{1,8},{2,11},{3,10},{8,1},{9,0},{10,3},{11,2},{16,25},{17,24... | collective-permute-start | bytes 221192 | tf_op jit(solution)/shard_map/ppermute | solution.py:345
  19.4 1.2 %collective-permute-start.12 = (bf16[144,256]{1,0:T(8,128)(2,1)S(1)}, bf16[144,256]{1,0:T(8,128)(2,1)S(1)}, u32[]{:S(2)}, u32[]{:S(2)}) collective-permute-start(bf16[144,256]{1,0:T(8,128)(2,1)S(1)} %get-tuple-element.56), channel_id=1, source_target_pairs={{0,3},{1,2},{2,1},{3,0},{8,11},{9,10},{10,9},{11,8},{16,19},{17,18... | collective-permute-start | bytes 221192 | tf_op jit(solution)/shard_map/ppermute | solution.py:345
  20.5 2.8 %collective-permute-start.6 = (bf16[144,256]{1,0:T(8,128)(2,1)S(1)}, bf16[144,256]{1,0:T(8,128)(2,1)S(1)}, u32[]{:S(2)}, u32[]{:S(2)}) collective-permute-start(bf16[144,256]{1,0:T(8,128)(2,1)S(1)} %get-tuple-element.50), channel_id=1, source_target_pairs={{0,11},{1,10},{2,9},{3,8},{8,3},{9,2},{10,1},{11,0},{16,27},{17,26... | collective-permute-start | bytes 221192 | tf_op jit(solution)/shard_map/ppermute | solution.py:345
  24.0 1.5 %collective-permute-start.9 = (bf16[144,256]{1,0:T(8,128)(2,1)S(1)}, bf16[144,256]{1,0:T(8,128)(2,1)S(1)}, u32[]{:S(2)}, u32[]{:S(2)}) collective-permute-start(bf16[144,256]{1,0:T(8,128)(2,1)S(1)} %get-tuple-element.53), channel_id=1, source_target_pairs={{0,2},{1,3},{2,0},{3,1},{8,10},{9,11},{10,8},{11,9},{16,18},{17,19... | collective-permute-start | bytes 221192 | tf_op jit(solution)/shard_map/ppermute | solution.py:345
  25.5 1.2 %slice.7.first_ref = bf16[1,2,3,256,256]{4,3,2,1,0:T(8,128)(2,1)S(1)} slice(bf16[3,3,3,256,256]{4,3,2,1,0:T(8,128)(2,1)} %weight_hbm.1), slice={[0:1], [0:2], [0:3], [0:256], [0:256]} | slice | bytes 1572864 | tf_op jit(solution)/shard_map/slice | solution.py:358
  26.7 0.5 %collective-permute-done.12 = bf16[144,256]{1,0:T(8,128)(2,1)S(1)} collective-permute-done((bf16[144,256]{1,0:T(8,128)(2,1)S(1)}, bf16[144,256]{1,0:T(8,128)(2,1)S(1)}, u32[]{:S(2)}, u32[]{:S(2)}) %collective-permute-start.12) | collective-permute-done | bytes 73760 | tf_op jit(solution)/shard_map/ppermute | solution.py:345
  27.3 0.5 %collective-permute-start.14 = (bf16[352,256]{1,0:T(8,128)(2,1)S(1)}, bf16[352,256]{1,0:T(8,128)(2,1)S(1)}, u32[]{:S(2)}, u32[]{:S(2)}) collective-permute-start(bf16[352,256]{1,0:T(8,128)(2,1)S(1)} %collective-permute-done.4.near_late), channel_id=1, source_target_pairs={{0,4},{4,0},{1,5},{5,1},{2,6},{6,2},{3,7},{7,3},{8,12},{12,8},{9,1... | collective-permute-start | bytes 540680 | tf_op jit(solution)/shard_map/ppermute | solution.py:354
  28.7 2.5 %collective-permute-start.16 = (bf16[144,256]{1,0:T(8,128)(2,1)S(1)}, bf16[144,256]{1,0:T(8,128)(2,1)S(1)}, u32[]{:S(2)}, u32[]{:S(2)}) collective-permute-start(bf16[144,256]{1,0:T(8,128)(2,1)S(1)} %add_convert_fusion), channel_id=1, source_target_pairs={{0,16},{8,24},{16,0},{24,8},{1,17},{9,25},{17,1},{25,9},{2,18},{10... | collective-permute-start | bytes 221192 | tf_op jit(solution)/shard_map/ppermute | solution.py:360
  31.2 1.3 %collective-permute-start.17 = (bf16[144,256]{1,0:T(8,128)(2,1)S(1)}, bf16[144,256]{1,0:T(8,128)(2,1)S(1)}, u32[]{:S(2)}, u32[]{:S(2)}) collective-permute-start(bf16[144,256]{1,0:T(8,128)(2,1)S(1)} %add_convert_fusion), channel_id=1, source_target_pairs={{0,24},{8,16},{16,8},{24,0},{1,25},{9,17},{17,9},{25,1},{2,26},{10... | collective-permute-start | bytes 221192 | tf_op jit(solution)/shard_map/ppermute | solution.py:360
  32.8 4.7 %conv.1 = bf16[2,2,176,256]{3,2,1,0:T(8,128)(2,1)} custom-call(s32[12]{0:T(128)S(1)} %stack.74.where_ref.refs_0_, f32[8,256]{1,0:T(8,128)S(1)} %get-tuple-element.60.norm_ref, bf16[2,4,176,256]{3,2,1,0:T(8,128)(2,1)S(1)} %get-tuple-element.61.act_ref, bf16[2,2,176,256]{3,2,1,0:T(8,128)(2,1)S(1)} %get-tuple-element.37.own_ref.refs_4_, ...), custom_call_target="tpu_custom_call" | custom-call | flops 2491416576 | bytes 4259840 | tf_op jit(solution)/shard_map/conv/pallas_call | solution.py:21
  37.8 0.7 %pad_maximum_fusion = f32[288,256]{1,0:T(8,128)} fusion(f32[144,256]{1,0:T(8,128)S(1)} %get-tuple-element.71, f32[144,256]{1,0:T(8,128)S(1)} %get-tuple-element.70), kind=kLoop, calls=%fused_computation | loop fusion | flops 73728 | bytes 589824 | tf_op jit(solution)/shard_map/concatenate | solution.py:368
  (30 shorter events, 2.7 us)
Async XLA Ops:
  0.6 2.0 %collective-permute-start = (bf16[2,2,176,256]{3,2,1,0:T(8,128)(2,1)}, bf16[2,2,176,256]{3,2,1,0:T(8,128)(2,1)S(1)}, u32[]{:S(2)}, u32[]{:S(2)}) collective-permute-start(bf16[2,2,176,256]{3,2,1,0:T(8,128)(2,1)} %bitcast.20), channel_id=1, source_target_pairs={{0,4},{4,0},{1,5},{5,1},{2,6},{6,2},{3,7},{7,3},{8,12},{12,8},{9,1... | collective-permute-start | bytes 1081352 | tf_op jit(solution)/shard_map/ppermute | solution.py:256
  1.1 7.3 %collective-permute-start.2 = (bf16[2,2,176,256]{3,2,1,0:T(8,128)(2,1)}, bf16[2,2,176,256]{3,2,1,0:T(8,128)(2,1)S(1)}, u32[]{:S(2)}, u32[]{:S(2)}) collective-permute-start(bf16[2,2,176,256]{3,2,1,0:T(8,128)(2,1)} %bitcast.18), channel_id=1, source_target_pairs={{0,4},{4,0},{1,5},{5,1},{2,6},{6,2},{3,7},{7,3},{8,12},{12,8},{9,1... | collective-permute-start | bytes 1081352 | tf_op jit(solution)/shard_map/ppermute | solution.py:257
  1.3 1.0 %copy-start.1 = (bf16[1,2,2,176,256]{4,3,2,1,0:T(8,128)(2,1)S(1)}, bf16[1,2,2,176,256]{4,3,2,1,0:T(8,128)(2,1)}, u32[]{:S(2)}) copy-start(bf16[1,2,2,176,256]{4,3,2,1,0:T(8,128)(2,1)} %param.6) | copy-start | bytes 1081348
  3.3 9.5 %collective-permute-start.1 = (bf16[400,256]{1,0:T(8,128)(2,1)S(1)}, bf16[400,256]{1,0:T(8,128)(2,1)S(1)}, u32[]{:S(2)}, u32[]{:S(2)}) collective-permute-start(bf16[400,256]{1,0:T(8,128)(2,1)S(1)} %get-tuple-element.38), channel_id=1, source_target_pairs={{0,1},{1,2},{2,3},{3,0},{4,7},{5,4},{6,5},{7,6},{8,9},{9,10},{10,1... | collective-permute-start | bytes 614408 | tf_op jit(solution)/shard_map/ppermute | solution.py:289
  6.2 4.2 %collective-permute-start.3 = (f32[16,256]{1,0:T(8,128)S(1)}, f32[16,256]{1,0:T(8,128)S(1)}, u32[]{:S(2)}, u32[]{:S(2)}) collective-permute-start(f32[16,256]{1,0:T(8,128)S(1)} %get-tuple-element.40.refs_1_), channel_id=1, source_target_pairs={{0,2},{1,3},{2,0},{3,1},{4,6},{5,7},{6,4},{7,5},{8,10},{9,11},{10,... | collective-permute-start | bytes 49160 | tf_op jit(solution)/shard_map/ppermute | solution.py:293
  8.5 1.0 %copy-start = (bf16[1,2,2,176,256]{4,3,2,1,0:T(8,128)(2,1)S(1)}, bf16[1,2,2,176,256]{4,3,2,1,0:T(8,128)(2,1)}, u32[]{:S(2)}) copy-start(bf16[1,2,2,176,256]{4,3,2,1,0:T(8,128)(2,1)} %param.11) | copy-start | bytes 1081348
  10.4 12.9 %collective-permute-start.4 = (bf16[352,256]{1,0:T(8,128)(2,1)S(1)}, bf16[352,256]{1,0:T(8,128)(2,1)S(1)}, u32[]{:S(2)}, u32[]{:S(2)}) collective-permute-start(bf16[352,256]{1,0:T(8,128)(2,1)S(1)} %get-tuple-element.44), channel_id=1, source_target_pairs={{0,1},{1,2},{2,3},{3,0},{4,7},{5,4},{6,5},{7,6},{8,9},{9,10},{10,1... | collective-permute-start | bytes 540680 | tf_op jit(solution)/shard_map/ppermute | solution.py:307
  12.8 1.2 %collective-permute-start.5 = (bf16[48,256]{1,0:T(8,128)(2,1)S(1)}, bf16[48,256]{1,0:T(8,128)(2,1)S(1)}, u32[]{:S(2)}, u32[]{:S(2)}) collective-permute-start(bf16[48,256]{1,0:T(8,128)(2,1)S(1)} %slice.6), channel_id=1, source_target_pairs={{0,4},{4,0},{1,5},{5,1},{2,6},{6,2},{3,7},{7,3},{8,12},{12,8},{9,1... | collective-permute-start | bytes 73736 | tf_op jit(solution)/shard_map/ppermute | solution.py:309
  16.1 7.7 %collective-permute-start.10 = (bf16[144,256]{1,0:T(8,128)(2,1)S(1)}, bf16[144,256]{1,0:T(8,128)(2,1)S(1)}, u32[]{:S(2)}, u32[]{:S(2)}) collective-permute-start(bf16[144,256]{1,0:T(8,128)(2,1)S(1)} %get-tuple-element.54), channel_id=1, source_target_pairs={{0,10},{1,11},{2,8},{3,9},{8,2},{9,3},{10,0},{11,1},{16,26},{17,27... | collective-permute-start | bytes 221192 | tf_op jit(solution)/shard_map/ppermute | solution.py:345
  17.8 6.3 %collective-permute-start.11 = (bf16[144,256]{1,0:T(8,128)(2,1)S(1)}, bf16[144,256]{1,0:T(8,128)(2,1)S(1)}, u32[]{:S(2)}, u32[]{:S(2)}) collective-permute-start(bf16[144,256]{1,0:T(8,128)(2,1)S(1)} %get-tuple-element.55), channel_id=1, source_target_pairs={{0,9},{1,8},{2,11},{3,10},{8,1},{9,0},{10,3},{11,2},{16,25},{17,24... | collective-permute-start | bytes 221192 | tf_op jit(solution)/shard_map/ppermute | solution.py:345
  19.4 7.9 %collective-permute-start.12 = (bf16[144,256]{1,0:T(8,128)(2,1)S(1)}, bf16[144,256]{1,0:T(8,128)(2,1)S(1)}, u32[]{:S(2)}, u32[]{:S(2)}) collective-permute-start(bf16[144,256]{1,0:T(8,128)(2,1)S(1)} %get-tuple-element.56), channel_id=1, source_target_pairs={{0,3},{1,2},{2,1},{3,0},{8,11},{9,10},{10,9},{11,8},{16,19},{17,18... | collective-permute-start | bytes 221192 | tf_op jit(solution)/shard_map/ppermute | solution.py:345
  20.5 6.7 %collective-permute-start.6 = (bf16[144,256]{1,0:T(8,128)(2,1)S(1)}, bf16[144,256]{1,0:T(8,128)(2,1)S(1)}, u32[]{:S(2)}, u32[]{:S(2)}) collective-permute-start(bf16[144,256]{1,0:T(8,128)(2,1)S(1)} %get-tuple-element.50), channel_id=1, source_target_pairs={{0,11},{1,10},{2,9},{3,8},{8,3},{9,2},{10,1},{11,0},{16,27},{17,26... | collective-permute-start | bytes 221192 | tf_op jit(solution)/shard_map/ppermute | solution.py:345
  23.3 4.5 %collective-permute-start.7 = (bf16[144,256]{1,0:T(8,128)(2,1)S(1)}, bf16[144,256]{1,0:T(8,128)(2,1)S(1)}, u32[]{:S(2)}, u32[]{:S(2)}) collective-permute-start(bf16[144,256]{1,0:T(8,128)(2,1)S(1)} %get-tuple-element.51), channel_id=1, source_target_pairs={{0,8},{1,9},{2,10},{3,11},{8,0},{9,1},{10,2},{11,3},{16,24},{17,25... | collective-permute-start | bytes 221192 | tf_op jit(solution)/shard_map/ppermute | solution.py:345
  23.8 4.4 %collective-permute-start.8 = (bf16[144,256]{1,0:T(8,128)(2,1)S(1)}, bf16[144,256]{1,0:T(8,128)(2,1)S(1)}, u32[]{:S(2)}, u32[]{:S(2)}) collective-permute-start(bf16[144,256]{1,0:T(8,128)(2,1)S(1)} %get-tuple-element.52), channel_id=1, source_target_pairs={{0,1},{1,0},{2,3},{3,2},{8,9},{9,8},{10,11},{11,10},{16,17},{17,16... | collective-permute-start | bytes 221192 | tf_op jit(solution)/shard_map/ppermute | solution.py:345
  24.0 4.6 %collective-permute-start.9 = (bf16[144,256]{1,0:T(8,128)(2,1)S(1)}, bf16[144,256]{1,0:T(8,128)(2,1)S(1)}, u32[]{:S(2)}, u32[]{:S(2)}) collective-permute-start(bf16[144,256]{1,0:T(8,128)(2,1)S(1)} %get-tuple-element.53), channel_id=1, source_target_pairs={{0,2},{1,3},{2,0},{3,1},{8,10},{9,11},{10,8},{11,9},{16,18},{17,19... | collective-permute-start | bytes 221192 | tf_op jit(solution)/shard_map/ppermute | solution.py:345
  27.3 5.3 %collective-permute-start.13 = (bf16[400,256]{1,0:T(8,128)(2,1)S(1)}, bf16[400,256]{1,0:T(8,128)(2,1)S(1)}, u32[]{:S(2)}, u32[]{:S(2)}) collective-permute-start(bf16[400,256]{1,0:T(8,128)(2,1)S(1)} %collective-permute-done.1.refs_6_), channel_id=1, source_target_pairs={{0,4},{4,0},{1,5},{5,1},{2,6},{6,2},{3,7},{7,3},{8,12},{12,8},{9,1... | collective-permute-start | bytes 614408 | tf_op jit(solution)/shard_map/ppermute | solution.py:353
  27.3 5.3 %collective-permute-start.14 = (bf16[352,256]{1,0:T(8,128)(2,1)S(1)}, bf16[352,256]{1,0:T(8,128)(2,1)S(1)}, u32[]{:S(2)}, u32[]{:S(2)}) collective-permute-start(bf16[352,256]{1,0:T(8,128)(2,1)S(1)} %collective-permute-done.4.near_late), channel_id=1, source_target_pairs={{0,4},{4,0},{1,5},{5,1},{2,6},{6,2},{3,7},{7,3},{8,12},{12,8},{9,1... | collective-permute-start | bytes 540680 | tf_op jit(solution)/shard_map/ppermute | solution.py:354
  28.7 8.9 %collective-permute-start.16 = (bf16[144,256]{1,0:T(8,128)(2,1)S(1)}, bf16[144,256]{1,0:T(8,128)(2,1)S(1)}, u32[]{:S(2)}, u32[]{:S(2)}) collective-permute-start(bf16[144,256]{1,0:T(8,128)(2,1)S(1)} %add_convert_fusion), channel_id=1, source_target_pairs={{0,16},{8,24},{16,0},{24,8},{1,17},{9,25},{17,1},{25,9},{2,18},{10... | collective-permute-start | bytes 221192 | tf_op jit(solution)/shard_map/ppermute | solution.py:360
  31.2 6.4 %collective-permute-start.17 = (bf16[144,256]{1,0:T(8,128)(2,1)S(1)}, bf16[144,256]{1,0:T(8,128)(2,1)S(1)}, u32[]{:S(2)}, u32[]{:S(2)}) collective-permute-start(bf16[144,256]{1,0:T(8,128)(2,1)S(1)} %add_convert_fusion), channel_id=1, source_target_pairs={{0,24},{8,16},{16,8},{24,0},{1,25},{9,17},{17,9},{25,1},{2,26},{10... | collective-permute-start | bytes 221192 | tf_op jit(solution)/shard_map/ppermute | solution.py:360
  32.5 5.2 %collective-permute-start.15 = (bf16[144,256]{1,0:T(8,128)(2,1)S(1)}, bf16[144,256]{1,0:T(8,128)(2,1)S(1)}, u32[]{:S(2)}, u32[]{:S(2)}) collective-permute-start(bf16[144,256]{1,0:T(8,128)(2,1)S(1)} %add_convert_fusion), channel_id=1, source_target_pairs={{0,8},{8,0},{16,24},{24,16},{1,9},{9,1},{17,25},{25,17},{2,10},{10... | collective-permute-start | bytes 221192 | tf_op jit(solution)/shard_map/ppermute | solution.py:360
